TPU v7x, 32 devices: a whole 2x2x4 slice. The times are simulated.
32 devices in a mesh: lon: 16 (over z, x, core), lat: 2 (over y).
Axes of the slice: x: 2, y: 2, z: 4, core: 2. Of those that a mesh axis runs over, the one named last changes fastest.
Arguments:
- states: bfloat16 [8, 256, 128, 128], P(None, 'lon', 'lat'), may hold values from -6 to 6
- targets: bfloat16 [8, 256, 128, 128], P(None, 'lon', 'lat'), may hold values from -6 to 6
- sea_temp: bfloat16 [8, 256, 128], P(None, 'lon', 'lat'), may hold values from -6 to 6
- ocean: int32 [8, 256, 128], P(None, 'lon', 'lat'), may hold values from 0 to 1
- valid: int32 [8, 256, 128], P(None, 'lon', 'lat'), may hold values from 0 to 1
- order: int32 [8], replicated, may hold values from 0 to 7, each once
- w_enc: float32 [2, 9, 128, 256], replicated, may hold values from -0.1875 to 0.1875
- w_mid: float32 [2, 256, 256], replicated, may hold values from -0.375 to 0.375
- w_dec: float32 [2, 256, 128], replicated, may hold values from -0.375 to 0.375
- biases: float32 [2, 896], replicated, may hold values from -3 to 3
- mom_enc: float32 [2, 9, 128, 256], replicated, may hold values from -0.625 to 0.625
- mom_mid: float32 [2, 256, 256], replicated, may hold values from -0.625 to 0.625
- mom_dec: float32 [2, 256, 128], replicated, may hold values from -0.625 to 0.625
- mom_bias: float32 [2, 896], replicated, may hold values from -0.625 to 0.625
- avg_enc: float32 [2, 9, 128, 256], replicated, may hold values from -0.1875 to 0.1875
- avg_mid: float32 [2, 256, 256], replicated, may hold values from -0.375 to 0.375
- avg_dec: float32 [2, 256, 128], replicated, may hold values from -0.375 to 0.375
- avg_bias: float32 [2, 896], replicated, may hold values from -3 to 3
Outputs:
- loss_sum: float32 [], replicated
- weight_sum: float32 [], replicated
- new_enc: float32 [2, 9, 128, 256], replicated
- new_mid: float32 [2, 256, 256], replicated
- new_dec: float32 [2, 256, 128], replicated
- new_bias: float32 [2, 896], replicated
- next_mom_enc: float32 [2, 9, 128, 256], replicated
- next_mom_mid: float32 [2, 256, 256], replicated
- next_mom_dec: float32 [2, 256, 128], replicated
- next_mom_bias: float32 [2, 896], replicated
- next_avg_enc: float32 [2, 9, 128, 256], replicated
- next_avg_mid: float32 [2, 256, 256], replicated
- next_avg_dec: float32 [2, 256, 128], replicated
- next_avg_bias: float32 [2, 896], replicated
- copy_enc: bfloat16 [2, 9, 128, 256], replicated
- copy_mid: bfloat16 [2, 256, 256], replicated
- copy_dec: bfloat16 [2, 256, 128], replicated
- copy_bias: bfloat16 [2, 896], replicated
Inputs may be any that keep to these rules, and one draw needn't show every extreme that they name: order names every snapshot once.
All inputs are finite; a program needn't handle non-finite values.
Results may differ from a plain program's by a relative error of at most 0.0024.
The roundings to bfloat16 on the way count: a program that leaves them out, or rounds other values in their place, can miss the bound.
Values may be sent and summed in bfloat16 or wider, within the bound.
No kernel may reach another device: no remote copies, remote signals or barrier semaphores. Data moves between devices by JAX's collectives and lax.ppermute only.
A program may use at most 448 MiB of HBM per device.

v0:
```python
import math

import jax
import jax.numpy as jnp
from jax import lax
from jax.sharding import PartitionSpec as P

MW = 86
NDEG = 86
MB = 4


HIGH = lax.Precision.HIGHEST
MOMENTUM = 0.9
AVERAGE = 0.99
RATE_BASE = 0.0006


def with_halo(block, sides, width, periodic):
    for axis, dim in sides:
        count = lax.axis_size(axis)
        forward = [(i, i + 1) for i in range(count - 1)]
        if periodic:
            forward.append((count - 1, 0))
        backward = [(target, source) for source, target in forward]
        low = lax.ppermute(
            lax.slice_in_dim(block, block.shape[dim] - width, None, axis=dim), axis, forward
        )
        high = lax.ppermute(lax.slice_in_dim(block, 0, width, axis=dim), axis, backward)
        block = jnp.concatenate([low, block, high], axis=dim)
    return block


def tables(nlon, nlat, groups):
    coeffs = jnp.arange(2 * MW)
    wave = jnp.where(coeffs < MW, coeffs, coeffs - MW + 1).astype(jnp.float32)
    places = jnp.arange(nlon).astype(jnp.float32)
    angle = 2.0 * math.pi * wave[:, None] * places[None, :] / nlon
    fourier = jnp.where((coeffs < MW)[:, None], jnp.cos(angle), jnp.sin(angle)) * math.sqrt(
        2.0 / nlon
    )
    phase = ((jnp.arange(nlat).astype(jnp.float32) + 0.5) / nlat - 0.5) * math.pi
    sine = jnp.sin(phase)
    quad = jnp.cos(phase) * math.pi / nlat
    polys = [jnp.ones_like(sine), sine]
    for degree in range(1, NDEG - 1):
        polys.append(((2 * degree + 1) * sine * polys[-1] - degree * polys[-2]) / (degree + 1))
    stacked = jnp.stack(polys[:NDEG])
    degrees = jnp.arange(NDEG).astype(jnp.float32)
    legendre = jnp.sqrt((2 * degrees + 1) / 2)[:, None] * jnp.sqrt(quad)[None, :] * stacked
    damping = 1.5 * (1.0 - 2.0 * degrees * (degrees + 1) / (NDEG * (NDEG + 1)))
    filters = damping[None, :] * (1.0 - 0.5 * wave / MW)[:, None]
    kept = 2 * MW
    slots = (kept + groups - 1) // groups * groups
    fourier = jnp.pad(fourier, ((0, slots - kept), (0, 0)))
    filters = jnp.pad(filters, ((0, slots - kept), (0, 0)))
    return (fourier, legendre, filters)


def spectral(values, tabs):
    fourier, legendre, filters = tabs
    cycles = lax.all_to_all(
        values.astype(jnp.bfloat16), "lon", split_axis=3, concat_axis=1, tiled=True
    ).astype(values.dtype)
    coeff = jnp.einsum("kx,sxjc->skjc", fourier, cycles, precision=HIGH)
    block = fourier.shape[0] // lax.axis_size("lat")
    where = lax.axis_index("lat")
    block_filter = lax.dynamic_slice_in_dim(filters, where * block, block, 0)
    columns = lax.all_to_all(
        coeff.astype(jnp.bfloat16), "lat", split_axis=1, concat_axis=2, tiled=True
    ).astype(coeff.dtype)
    spec = (
        jnp.einsum("nj,skjc->sknc", legendre, columns, precision=HIGH)
        * block_filter[None, :, :, None]
    )
    back = jnp.einsum("nj,sknc->skjc", legendre, spec, precision=HIGH)
    coeff_back = lax.all_to_all(
        back.astype(jnp.bfloat16), "lat", split_axis=2, concat_axis=1, tiled=True
    ).astype(back.dtype)
    grid = jnp.einsum("kx,skjc->sxjc", fourier, coeff_back, precision=HIGH)
    return lax.all_to_all(
        grid.astype(jnp.bfloat16), "lon", split_axis=1, concat_axis=3, tiled=True
    ).astype(grid.dtype)


def extend(field):
    wider = with_halo(field, (("lon", 1),), 1, True)
    return with_halo(wider, (("lat", 2),), 1, False)


def neighbours(padded, flipped, lon_t, lat_t):
    parts = []
    for row_off in range(3):
        for col_off in range(3):
            first = 2 - row_off if flipped else row_off
            second = 2 - col_off if flipped else col_off
            parts.append(padded[:, first : first + lon_t, second : second + lat_t])
    stacked = jnp.stack(parts, axis=3)
    return stacked.reshape(-1, 9 * padded.shape[-1])


def gelu_fn(value):
    return jax.nn.gelu(value, approximate=True)


def gelu_back(value, grad):
    return jax.vjp(gelu_fn, value)[1](grad)[0]


def layer_forward(state, sea, enc, mid, dec, vec, tabs):
    hid = mid.shape[0]
    lon_t, lat_t = (state.shape[1], state.shape[2])
    moved = state + spectral(state, tabs)
    patches = neighbours(extend(moved.astype(jnp.bfloat16)), False, lon_t, lat_t)
    pre1 = jnp.dot(patches, enc, preferred_element_type=jnp.float32)
    pre1 = pre1 + sea.reshape(-1, 1) * vec[hid : 2 * hid] + vec[:hid]
    active1 = gelu_fn(pre1).astype(jnp.bfloat16)
    pre2 = jnp.dot(active1, mid, preferred_element_type=jnp.float32) + vec[2 * hid : 3 * hid]
    active2 = gelu_fn(pre2).astype(jnp.bfloat16)
    output = jnp.dot(active2, dec, preferred_element_type=jnp.float32) + vec[3 * hid :]
    return (moved + output.reshape(state.shape), (patches, pre1, active1, pre2, active2))


def layer_backward(grad_state, sea, enc, mid, dec, saved, tabs):
    patches, pre1, active1, pre2, active2 = saved
    hid = mid.shape[0]
    shape = grad_state.shape
    chans = shape[-1]
    g_out = grad_state.reshape(-1, chans).astype(jnp.bfloat16)
    g_dec = jnp.einsum("rh,rc->hc", active2, g_out, preferred_element_type=jnp.float32)
    g_act2 = jnp.einsum("rc,hc->rh", g_out, dec, preferred_element_type=jnp.float32)
    g_pre2 = gelu_back(pre2, g_act2).astype(jnp.bfloat16)
    g_mid = jnp.einsum("rh,rg->hg", active1, g_pre2, preferred_element_type=jnp.float32)
    g_act1 = jnp.einsum("rg,hg->rh", g_pre2, mid, preferred_element_type=jnp.float32)
    g_pre1 = gelu_back(pre1, g_act1).astype(jnp.bfloat16)
    g_enc = jnp.einsum("rk,rh->kh", patches, g_pre1, preferred_element_type=jnp.float32)
    wide1 = g_pre1.astype(jnp.float32)
    g_vec = jnp.concatenate(
        [
            jnp.sum(wide1, 0),
            jnp.sum(sea.reshape(-1, 1) * wide1, 0),
            jnp.sum(g_pre2.astype(jnp.float32), 0),
            jnp.sum(g_out.astype(jnp.float32), 0),
        ]
    )
    spread = extend(g_pre1.reshape(shape[0], shape[1], shape[2], hid))
    gathered = neighbours(spread, True, shape[1], shape[2]).reshape(-1, 9, hid)
    g_input = jnp.einsum(
        "rkh,kch->rc", gathered, enc.reshape(9, chans, hid), preferred_element_type=jnp.float32
    )
    grad_moved = grad_state + g_input.reshape(shape)
    return (grad_moved + spectral(grad_moved, tabs), (g_enc, g_mid, g_dec, g_vec))


def body(
    states,
    targets,
    sea_temp,
    ocean,
    valid,
    order,
    w_enc,
    w_mid,
    w_dec,
    biases,
    mom_enc,
    mom_mid,
    mom_dec,
    mom_bias,
    avg_enc,
    avg_mid,
    avg_dec,
    avg_bias,
):
    pool, lon_t, lat_t, chans = states.shape
    layers, hid = (w_mid.shape[0], w_mid.shape[1])
    nlon = lon_t * lax.axis_size("lon")
    nlat = lat_t * lax.axis_size("lat")
    tabs = tables(nlon, nlat, lax.axis_size("lat"))
    lat_glob = (lax.axis_index("lat") * lat_t + jnp.arange(lat_t)).astype(jnp.float32)
    area = jnp.cos(((lat_glob + 0.5) / nlat - 0.5) * math.pi)
    enc_low = w_enc.astype(jnp.bfloat16).reshape(layers, 9 * chans, hid)
    mid_low = w_mid.astype(jnp.bfloat16)
    dec_low = w_dec.astype(jnp.bfloat16)
    snaps = pool // MB
    sums = [
        jnp.zeros((layers, 9 * chans, hid), jnp.float32),
        jnp.zeros_like(w_mid),
        jnp.zeros_like(w_dec),
        jnp.zeros_like(biases),
    ]
    loss = jnp.zeros((), jnp.float32)
    total = jnp.zeros((), jnp.float32)
    for batch_id in range(MB):
        picks = lax.dynamic_slice_in_dim(order, batch_id * snaps, snaps)
        state = jnp.take(states, picks, axis=0).astype(jnp.float32)
        target = jnp.take(targets, picks, axis=0).astype(jnp.float32)
        sea = jnp.take(ocean, picks, axis=0).astype(jnp.float32) * jnp.take(
            sea_temp, picks, axis=0
        ).astype(jnp.float32)
        weight = jnp.take(valid, picks, axis=0).astype(jnp.float32) * area[None, None, :]
        kept = []
        for layer_id in range(layers):
            state, saved = layer_forward(
                state,
                sea,
                enc_low[layer_id],
                mid_low[layer_id],
                dec_low[layer_id],
                biases[layer_id],
                tabs,
            )
            kept.append(saved)
        diff = state - target
        loss = loss + jnp.sum(weight[..., None] * diff * diff)
        total = total + jnp.sum(weight)
        grad_state = 2.0 * weight[..., None] * diff
        for layer_id in reversed(range(layers)):
            grad_state, found = layer_backward(
                grad_state,
                sea,
                enc_low[layer_id],
                mid_low[layer_id],
                dec_low[layer_id],
                kept[layer_id],
                tabs,
            )
            sums = [acc.at[layer_id].add(part) for acc, part in zip(sums, found)]
    g_enc, g_mid, g_dec, g_vec, loss, total = lax.psum(
        (sums[0], sums[1], sums[2], sums[3], loss, total), ("lon", "lat")
    )
    grads = (g_enc.reshape(w_enc.shape), g_mid, g_dec, g_vec)
    rate = RATE_BASE * math.sqrt(pool * nlon * nlat)
    news, moms, avgs, copies = ([], [], [], [])
    for weight_now, grad, mom, avg in zip(
        (w_enc, w_mid, w_dec, biases),
        grads,
        (mom_enc, mom_mid, mom_dec, mom_bias),
        (avg_enc, avg_mid, avg_dec, avg_bias),
    ):
        scaled = grad / total
        mom_new = MOMENTUM * mom + scaled
        fresh = weight_now - rate * (scaled + MOMENTUM * mom_new)
        news.append(fresh)
        moms.append(mom_new)
        avgs.append(AVERAGE * avg + (1.0 - AVERAGE) * fresh)
        copies.append(fresh.astype(jnp.bfloat16))
    return (
        loss,
        total,
        news[0],
        news[1],
        news[2],
        news[3],
        moms[0],
        moms[1],
        moms[2],
        moms[3],
        avgs[0],
        avgs[1],
        avgs[2],
        avgs[3],
        copies[0],
        copies[1],
        copies[2],
        copies[3],
    )


def solution(mesh):
    placed = (
        P(None, "lon", "lat", None),
        P(None, "lon", "lat", None),
        P(None, "lon", "lat"),
        P(None, "lon", "lat"),
        P(None, "lon", "lat"),
        P(),
        P(),
        P(),
        P(),
        P(),
        P(),
        P(),
        P(),
        P(),
        P(),
        P(),
        P(),
        P(),
    )
    return jax.shard_map(
        body,
        mesh=mesh,
        in_specs=placed,
        out_specs=(
            P(),
            P(),
            P(),
            P(),
            P(),
            P(),
            P(),
            P(),
            P(),
            P(),
            P(),
            P(),
            P(),
            P(),
            P(),
            P(),
            P(),
            P(),
        ),
        check_vma=False,
    )
```

profile of v0, /device:TPU:0, one launch (start us, length us, event | category | flops | bytes accessed | tf_op | source)
XLA Modules:
  0.0 1520.6 jit_solution(11252338073238415400)
XLA Ops:
  15.2 7.9 all-to-all-start.8
  47.0 6.1 all-to-all-start
  53.2 14.4 all-to-all-done
  71.8 14.4 all-to-all-done.24
  86.2 4.4 all-to-all-start.16
  163.5 6.0 all-to-all-done.2
  189.9 5.6 all-to-all-start.11
  223.4 6.3 all-to-all-start.3
  245.1 6.2 all-to-all-start.27
  252.0 4.5 collective-permute-start.9
  266.2 4.3 all-to-all-start.19
  295.6 4.5 collective-permute-start.25
  300.1 4.5 collective-permute-start.17
  308.4 5.1 collective-permute-start.2
  315.5 5.7 collective-permute-start.26
  323.2 5.9 collective-permute-start.18
  337.7 11.6 copy.619
  363.6 4.3 all-to-all-start.12
  378.5 11.6 copy.584
  407.2 11.7 copy.689
  436.7 6.0 all-to-all-start.4
  454.0 14.8 copy.654
  468.9 6.1 all-to-all-start.28
  475.1 5.1 fusion.116
  489.5 5.9 all-to-all-start.20
  572.4 5.0 all-to-all-done.6
  600.1 5.8 all-to-all-start.15
  611.0 9.3 all-to-all-done.15
  620.3 4.5 all-to-all-start.7
  667.1 6.2 all-to-all-start.31
  676.6 4.2 collective-permute-start.13
  691.4 4.2 all-to-all-start.23
  725.6 4.5 collective-permute-start.29
  730.2 4.5 collective-permute-start.21
  737.9 4.5 collective-permute-start.6
  743.9 4.5 collective-permute-start.30
  749.8 4.8 collective-permute-start.22
  763.1 11.5 copy.635
  785.3 14.9 copy.600
  824.9 4.5 collective-permute-start.33
  838.3 11.5 copy.705
  856.5 4.4 collective-permute-start.37
  870.2 11.5 copy.670
  899.6 4.2 collective-permute-start.41
  904.1 4.5 collective-permute-start.45
  912.2 4.7 collective-permute-start.35
  920.3 5.8 collective-permute-start.39
  929.6 5.7 collective-permute-start.43
  954.0 5.3 collective-permute-start.47
  996.3 7.4 fusion.359
  1003.7 6.0 all-to-all-start.36
  1024.3 4.6 all-to-all-start.40
  1031.2 5.5 fusion.357
  1043.6 6.4 all-to-all-start.44
  1107.4 4.3 all-to-all-start.37
  1159.3 7.4 all-to-all-done.38
  1177.8 4.6 all-to-all-start.46
  1189.1 5.6 all-to-all-start.35
  1227.9 6.0 all-to-all-start.39
  1249.2 5.3 all-to-all-start.43
  1276.4 6.1 all-to-all-start.47
  1353.4 6.7 fusion.77
  1363.6 41.3 %all-reduce = (f32[]{:T(128)}, f32[]{:T(128)}, f32[2,896]{1,0:T(2,128)S(1)}) all-reduce(f32[]{:T(128)S(6)} %add.1634, f32[]{:T(128)S(6)} %add.1637, f32[2,896]{1,0:T(2,128)S(1)} %scatter-add.139), channel_id=1, replica_groups=mesh['lon'=16,'lat'=2] {'lon','lat'}, use_global_device_ids=true, to_apply=%region_4.8 | all-reduce | flops 1794 | bytes 14352 | tf_op jit(solution)/shard_map/psum | solution.py:229
  1406.8 93.7 %all-reduce.4.cloned.1.call-done = (f32[2,1152,256]{2,1,0:T(8,128)}, f32[2,256,256]{2,1,0:T(8,128)}, f32[2,256,128]{2,1,0:T(8,128)}) async-done(((f32[2,1152,256]{2,1,0:T(8,128)}, f32[2,256,256]{2,1,0:T(8,128)}, f32[2,256,128]{2,1,0:T(8,128)}), (f32[2,1152,256]{2,1,0:T(8,128)}, f32[2,256,256]{2,1,0:T(8,128)}, f32[2,256,128]{2,1,0:T(8,128)})) %all-reduce.4.cloned.1.call-update) | async-done | bytes 3145744 | tf_op jit(solution)/shard_map/psum | solution.py:229
  (1463 shorter events, 950.8 us)
Async XLA Ops:
  15.2 31.8 %all-to-all-start.8 = ((bf16[16,2,8192]{2,1,0:T(2,128)(2,1)}), bf16[16,2,8192]{2,1,0:T(2,128)(2,1)}, u32[]{:S(2)}, u32[]{:S(2)}) async-start(bf16[16,2,8192]{2,1,0:T(2,128)(2,1)} %reshape.2306), calls=%async_computation.8 | async-start | bytes 1048576 | tf_op jit(solution)/shard_map/all_to_all | solution.py:62
  47.0 20.6 %all-to-all-start = ((bf16[16,2,8192]{2,1,0:T(2,128)(2,1)}), bf16[16,2,8192]{2,1,0:T(2,128)(2,1)S(1)}, u32[]{:S(2)}, u32[]{:S(2)}) async-start(bf16[16,2,8192]{2,1,0:T(2,128)(2,1)} %reshape.2294), calls=%async_computation | async-start | bytes 1048576 | tf_op jit(solution)/shard_map/all_to_all | solution.py:62
  67.6 18.6 %all-to-all-start.24 = ((bf16[16,2,8192]{2,1,0:T(2,128)(2,1)}), bf16[16,2,8192]{2,1,0:T(2,128)(2,1)S(1)}, u32[]{:S(2)}, u32[]{:S(2)}) async-start(bf16[16,2,8192]{2,1,0:T(2,128)(2,1)} %reshape.2330), calls=%async_computation.24 | async-start | bytes 1048576 | tf_op jit(solution)/shard_map/all_to_all | solution.py:62
  86.2 22.9 %all-to-all-start.16 = ((bf16[16,2,8192]{2,1,0:T(2,128)(2,1)}), bf16[16,2,8192]{2,1,0:T(2,128)(2,1)}, u32[]{:S(2)}, u32[]{:S(2)}) async-start(bf16[16,2,8192]{2,1,0:T(2,128)(2,1)} %reshape.2318), calls=%async_computation.16 | async-start | bytes 1048576 | tf_op jit(solution)/shard_map/all_to_all | solution.py:62
  189.9 33.5 %all-to-all-start.11 = ((bf16[16,2,8192]{2,1,0:T(2,128)(2,1)}), bf16[16,2,8192]{2,1,0:T(2,128)(2,1)S(1)}, u32[]{:S(2)}, u32[]{:S(2)}) async-start(bf16[16,2,8192]{2,1,0:T(2,128)(2,1)} %reshape.2310), calls=%async_computation.11 | async-start | bytes 1048576 | tf_op jit(solution)/shard_map/all_to_all | solution.py:81
  223.4 21.7 %all-to-all-start.3 = ((bf16[16,2,8192]{2,1,0:T(2,128)(2,1)}), bf16[16,2,8192]{2,1,0:T(2,128)(2,1)}, u32[]{:S(2)}, u32[]{:S(2)}) async-start(bf16[16,2,8192]{2,1,0:T(2,128)(2,1)} %reshape.2298), calls=%async_computation.3 | async-start | bytes 1048576 | tf_op jit(solution)/shard_map/all_to_all | solution.py:81
  245.1 21.1 %all-to-all-start.27 = ((bf16[16,2,8192]{2,1,0:T(2,128)(2,1)}), bf16[16,2,8192]{2,1,0:T(2,128)(2,1)}, u32[]{:S(2)}, u32[]{:S(2)}) async-start(bf16[16,2,8192]{2,1,0:T(2,128)(2,1)} %reshape.2334), calls=%async_computation.27 | async-start | bytes 1048576 | tf_op jit(solution)/shard_map/all_to_all | solution.py:81
  251.6 43.9 %collective-permute-start.8 = (bf16[2,1,64,128]{3,2,0,1:T(8,128)(2,1)S(1)}, bf16[2,1,64,128]{3,2,0,1:T(8,128)(2,1)S(1)}, u32[]{:S(2)}, u32[]{:S(2)}) collective-permute-start(bf16[2,1,64,128]{3,2,0,1:T(8,128)(2,1)S(1)} %get-tuple-element.661), channel_id=1, source_target_pairs={{0,2},{2,4},{4,6},{6,8},{8,10},{10,12},{12,14},{14,16},{16,18},{18... | collective-permute-start | bytes 98312 | tf_op jit(solution)/shard_map/ppermute | solution.py:26
  252.0 48.0 %collective-permute-start.9 = (bf16[2,1,64,128]{3,2,0,1:T(8,128)(2,1)S(1)}, bf16[2,1,64,128]{3,2,0,1:T(8,128)(2,1)S(1)}, u32[]{:S(2)}, u32[]{:S(2)}) collective-permute-start(bf16[2,1,64,128]{3,2,0,1:T(8,128)(2,1)S(1)} %get-tuple-element.662), channel_id=1, source_target_pairs={{2,0},{4,2},{6,4},{8,6},{10,8},{12,10},{14,12},{16,14},{18,16},{20... | collective-permute-start | bytes 98312 | tf_op jit(solution)/shard_map/ppermute | solution.py:29
  266.2 19.8 %all-to-all-start.19 = ((bf16[16,2,8192]{2,1,0:T(2,128)(2,1)}), bf16[16,2,8192]{2,1,0:T(2,128)(2,1)}, u32[]{:S(2)}, u32[]{:S(2)}) async-start(bf16[16,2,8192]{2,1,0:T(2,128)(2,1)} %reshape.2322), calls=%async_computation.19 | async-start | bytes 1048576 | tf_op jit(solution)/shard_map/all_to_all | solution.py:81
  271.1 29.0 %collective-permute-start = (bf16[2,1,64,128]{3,2,0,1:T(8,128)(2,1)S(1)}, bf16[2,1,64,128]{3,2,0,1:T(8,128)(2,1)S(1)}, u32[]{:S(2)}, u32[]{:S(2)}) collective-permute-start(bf16[2,1,64,128]{3,2,0,1:T(8,128)(2,1)S(1)} %get-tuple-element.665), channel_id=1, source_target_pairs={{0,2},{2,4},{4,6},{6,8},{8,10},{10,12},{12,14},{14,16},{16,18},{18... | collective-permute-start | bytes 98312 | tf_op jit(solution)/shard_map/ppermute | solution.py:26
  271.3 33.3 %collective-permute-start.1 = (bf16[2,1,64,128]{3,2,0,1:T(8,128)(2,1)}, bf16[2,1,64,128]{3,2,0,1:T(8,128)(2,1)S(1)}, u32[]{:S(2)}, u32[]{:S(2)}) collective-permute-start(bf16[2,1,64,128]{3,2,0,1:T(8,128)(2,1)} %get-tuple-element.666), channel_id=1, source_target_pairs={{2,0},{4,2},{6,4},{8,6},{10,8},{12,10},{14,12},{16,14},{18,16},{20... | collective-permute-start | bytes 98312 | tf_op jit(solution)/shard_map/ppermute | solution.py:29
  286.0 21.1 %collective-permute-start.24 = (bf16[2,1,64,128]{3,2,0,1:T(8,128)(2,1)}, bf16[2,1,64,128]{3,2,0,1:T(8,128)(2,1)S(1)}, u32[]{:S(2)}, u32[]{:S(2)}) collective-permute-start(bf16[2,1,64,128]{3,2,0,1:T(8,128)(2,1)} %get-tuple-element.653), channel_id=1, source_target_pairs={{0,2},{2,4},{4,6},{6,8},{8,10},{10,12},{12,14},{14,16},{16,18},{18... | collective-permute-start | bytes 98312 | tf_op jit(solution)/shard_map/ppermute | solution.py:26
  304.6 17.3 %collective-permute-start.10 = (bf16[2,18,1,128]{3,2,0,1:T(2,128)(2,1)S(1)}, bf16[2,18,1,128]{3,2,0,1:T(2,128)(2,1)S(1)}, u32[]{:S(2)}, u32[]{:S(2)}) collective-permute-start(bf16[2,18,1,128]{3,2,0,1:T(2,128)(2,1)S(1)} %get-tuple-element.642), channel_id=1, source_target_pairs={{0,1},{2,3},{4,5},{6,7},{8,9},{10,11},{12,13},{14,15},{16,17},{18,... | collective-permute-start | bytes 27656 | tf_op jit(solution)/shard_map/ppermute | solution.py:26
  308.4 59.5 %collective-permute-start.2 = (bf16[2,18,1,128]{3,2,0,1:T(2,128)(2,1)}, bf16[2,18,1,128]{3,2,0,1:T(2,128)(2,1)}, u32[]{:S(2)}, u32[]{:S(2)}) collective-permute-start(bf16[2,18,1,128]{3,2,0,1:T(2,128)(2,1)} %get-tuple-element.650), channel_id=1, source_target_pairs={{0,1},{2,3},{4,5},{6,7},{8,9},{10,11},{12,13},{14,15},{16,17},{18,... | collective-permute-start | bytes 27656 | tf_op jit(solution)/shard_map/ppermute | solution.py:26
  314.2 55.0 %collective-permute-start.3 = (bf16[2,18,1,128]{3,2,0,1:T(2,128)(2,1)S(1)}, bf16[2,18,1,128]{3,2,0,1:T(2,128)(2,1)}, u32[]{:S(2)}, u32[]{:S(2)}) collective-permute-start(bf16[2,18,1,128]{3,2,0,1:T(2,128)(2,1)S(1)} %get-tuple-element.649), channel_id=1, source_target_pairs={{1,0},{3,2},{5,4},{7,6},{9,8},{11,10},{13,12},{15,14},{17,16},{19,... | collective-permute-start | bytes 27656 | tf_op jit(solution)/shard_map/ppermute | solution.py:29
  315.5 82.4 %collective-permute-start.26 = (bf16[2,18,1,128]{3,2,0,1:T(2,128)(2,1)}, bf16[2,18,1,128]{3,2,0,1:T(2,128)(2,1)}, u32[]{:S(2)}, u32[]{:S(2)}) collective-permute-start(bf16[2,18,1,128]{3,2,0,1:T(2,128)(2,1)} %get-tuple-element.626), channel_id=1, source_target_pairs={{0,1},{2,3},{4,5},{6,7},{8,9},{10,11},{12,13},{14,15},{16,17},{18,... | collective-permute-start | bytes 27656 | tf_op jit(solution)/shard_map/ppermute | solution.py:26
  321.9 76.1 %collective-permute-start.27 = (bf16[2,18,1,128]{3,2,0,1:T(2,128)(2,1)}, bf16[2,18,1,128]{3,2,0,1:T(2,128)(2,1)}, u32[]{:S(2)}, u32[]{:S(2)}) collective-permute-start(bf16[2,18,1,128]{3,2,0,1:T(2,128)(2,1)} %get-tuple-element.625), channel_id=1, source_target_pairs={{1,0},{3,2},{5,4},{7,6},{9,8},{11,10},{13,12},{15,14},{17,16},{19,... | collective-permute-start | bytes 27656 | tf_op jit(solution)/shard_map/ppermute | solution.py:29
  323.2 95.8 %collective-permute-start.18 = (bf16[2,18,1,128]{3,2,0,1:T(2,128)(2,1)}, bf16[2,18,1,128]{3,2,0,1:T(2,128)(2,1)}, u32[]{:S(2)}, u32[]{:S(2)}) collective-permute-start(bf16[2,18,1,128]{3,2,0,1:T(2,128)(2,1)} %get-tuple-element.634), channel_id=1, source_target_pairs={{0,1},{2,3},{4,5},{6,7},{8,9},{10,11},{12,13},{14,15},{16,17},{18,... | collective-permute-start | bytes 27656 | tf_op jit(solution)/shard_map/ppermute | solution.py:26
  363.6 73.1 %all-to-all-start.12 = ((bf16[16,2,8192]{2,1,0:T(2,128)(2,1)}), bf16[16,2,8192]{2,1,0:T(2,128)(2,1)}, u32[]{:S(2)}, u32[]{:S(2)}) async-start(bf16[16,2,8192]{2,1,0:T(2,128)(2,1)} %reshape.2312), calls=%async_computation.12 | async-start | bytes 1048576 | tf_op jit(solution)/shard_map/all_to_all | solution.py:62
  367.9 51.1 %collective-permute-start.19 = (bf16[2,18,1,128]{3,2,0,1:T(2,128)(2,1)}, bf16[2,18,1,128]{3,2,0,1:T(2,128)(2,1)S(1)}, u32[]{:S(2)}, u32[]{:S(2)}) collective-permute-start(bf16[2,18,1,128]{3,2,0,1:T(2,128)(2,1)} %get-tuple-element.633), channel_id=1, source_target_pairs={{1,0},{3,2},{5,4},{7,6},{9,8},{11,10},{13,12},{15,14},{17,16},{19,... | collective-permute-start | bytes 27656 | tf_op jit(solution)/shard_map/ppermute | solution.py:29
  436.7 32.2 %all-to-all-start.4 = ((bf16[16,2,8192]{2,1,0:T(2,128)(2,1)}), bf16[16,2,8192]{2,1,0:T(2,128)(2,1)}, u32[]{:S(2)}, u32[]{:S(2)}) async-start(bf16[16,2,8192]{2,1,0:T(2,128)(2,1)} %reshape.2300), calls=%async_computation.4 | async-start | bytes 1048576 | tf_op jit(solution)/shard_map/all_to_all | solution.py:62
  468.9 20.6 %all-to-all-start.28 = ((bf16[16,2,8192]{2,1,0:T(2,128)(2,1)}), bf16[16,2,8192]{2,1,0:T(2,128)(2,1)S(1)}, u32[]{:S(2)}, u32[]{:S(2)}) async-start(bf16[16,2,8192]{2,1,0:T(2,128)(2,1)} %reshape.2336), calls=%async_computation.28 | async-start | bytes 1048576 | tf_op jit(solution)/shard_map/all_to_all | solution.py:62
  489.5 25.7 %all-to-all-start.20 = ((bf16[16,2,8192]{2,1,0:T(2,128)(2,1)}), bf16[16,2,8192]{2,1,0:T(2,128)(2,1)}, u32[]{:S(2)}, u32[]{:S(2)}) async-start(bf16[16,2,8192]{2,1,0:T(2,128)(2,1)} %reshape.2324), calls=%async_computation.20 | async-start | bytes 1048576 | tf_op jit(solution)/shard_map/all_to_all | solution.py:62
  600.1 20.2 %all-to-all-start.15 = ((bf16[16,2,8192]{2,1,0:T(2,128)(2,1)}), bf16[16,2,8192]{2,1,0:T(2,128)(2,1)S(1)}, u32[]{:S(2)}, u32[]{:S(2)}) async-start(bf16[16,2,8192]{2,1,0:T(2,128)(2,1)} %reshape.2316), calls=%async_computation.15 | async-start | bytes 1048576 | tf_op jit(solution)/shard_map/all_to_all | solution.py:81
  620.3 46.0 %all-to-all-start.7 = ((bf16[16,2,8192]{2,1,0:T(2,128)(2,1)}), bf16[16,2,8192]{2,1,0:T(2,128)(2,1)S(1)}, u32[]{:S(2)}, u32[]{:S(2)}) async-start(bf16[16,2,8192]{2,1,0:T(2,128)(2,1)} %reshape.2304), calls=%async_computation.7 | async-start | bytes 1048576 | tf_op jit(solution)/shard_map/all_to_all | solution.py:81
  667.1 24.3 %all-to-all-start.31 = ((bf16[16,2,8192]{2,1,0:T(2,128)(2,1)}), bf16[16,2,8192]{2,1,0:T(2,128)(2,1)}, u32[]{:S(2)}, u32[]{:S(2)}) async-start(bf16[16,2,8192]{2,1,0:T(2,128)(2,1)} %reshape.2340), calls=%async_computation.31 | async-start | bytes 1048576 | tf_op jit(solution)/shard_map/all_to_all | solution.py:81
  676.3 49.4 %collective-permute-start.12 = (bf16[2,1,64,128]{3,2,0,1:T(8,128)(2,1)S(1)}, bf16[2,1,64,128]{3,2,0,1:T(8,128)(2,1)S(1)}, u32[]{:S(2)}, u32[]{:S(2)}) collective-permute-start(bf16[2,1,64,128]{3,2,0,1:T(8,128)(2,1)S(1)} %get-tuple-element.659), channel_id=1, source_target_pairs={{0,2},{2,4},{4,6},{6,8},{8,10},{10,12},{12,14},{14,16},{16,18},{18... | collective-permute-start | bytes 98312 | tf_op jit(solution)/shard_map/ppermute | solution.py:26
  676.6 53.5 %collective-permute-start.13 = (bf16[2,1,64,128]{3,2,0,1:T(8,128)(2,1)S(1)}, bf16[2,1,64,128]{3,2,0,1:T(8,128)(2,1)S(1)}, u32[]{:S(2)}, u32[]{:S(2)}) collective-permute-start(bf16[2,1,64,128]{3,2,0,1:T(8,128)(2,1)S(1)} %get-tuple-element.660), channel_id=1, source_target_pairs={{2,0},{4,2},{6,4},{8,6},{10,8},{12,10},{14,12},{16,14},{18,16},{20... | collective-permute-start | bytes 98312 | tf_op jit(solution)/shard_map/ppermute | solution.py:29
  691.4 22.0 %all-to-all-start.23 = ((bf16[16,2,8192]{2,1,0:T(2,128)(2,1)}), bf16[16,2,8192]{2,1,0:T(2,128)(2,1)}, u32[]{:S(2)}, u32[]{:S(2)}) async-start(bf16[16,2,8192]{2,1,0:T(2,128)(2,1)} %reshape.2328), calls=%async_computation.23 | async-start | bytes 1048576 | tf_op jit(solution)/shard_map/all_to_all | solution.py:81
  695.7 34.5 %collective-permute-start.4 = (bf16[2,1,64,128]{3,2,0,1:T(8,128)(2,1)S(1)}, bf16[2,1,64,128]{3,2,0,1:T(8,128)(2,1)S(1)}, u32[]{:S(2)}, u32[]{:S(2)}) collective-permute-start(bf16[2,1,64,128]{3,2,0,1:T(8,128)(2,1)S(1)} %get-tuple-element.663), channel_id=1, source_target_pairs={{0,2},{2,4},{4,6},{6,8},{8,10},{10,12},{12,14},{14,16},{16,18},{18... | collective-permute-start | bytes 98312 | tf_op jit(solution)/shard_map/ppermute | solution.py:26
  696.0 38.7 %collective-permute-start.5 = (bf16[2,1,64,128]{3,2,0,1:T(8,128)(2,1)S(1)}, bf16[2,1,64,128]{3,2,0,1:T(8,128)(2,1)S(1)}, u32[]{:S(2)}, u32[]{:S(2)}) collective-permute-start(bf16[2,1,64,128]{3,2,0,1:T(8,128)(2,1)S(1)} %get-tuple-element.664), channel_id=1, source_target_pairs={{2,0},{4,2},{6,4},{8,6},{10,8},{12,10},{14,12},{16,14},{18,16},{20... | collective-permute-start | bytes 98312 | tf_op jit(solution)/shard_map/ppermute | solution.py:29
  713.4 23.2 %collective-permute-start.28 = (bf16[2,1,64,128]{3,2,0,1:T(8,128)(2,1)}, bf16[2,1,64,128]{3,2,0,1:T(8,128)(2,1)S(1)}, u32[]{:S(2)}, u32[]{:S(2)}) collective-permute-start(bf16[2,1,64,128]{3,2,0,1:T(8,128)(2,1)} %get-tuple-element.651), channel_id=1, source_target_pairs={{0,2},{2,4},{4,6},{6,8},{8,10},{10,12},{12,14},{14,16},{16,18},{18... | collective-permute-start | bytes 98312 | tf_op jit(solution)/shard_map/ppermute | solution.py:26
  737.9 36.7 %collective-permute-start.6 = (bf16[2,18,1,128]{3,2,0,1:T(2,128)(2,1)S(1)}, bf16[2,18,1,128]{3,2,0,1:T(2,128)(2,1)S(1)}, u32[]{:S(2)}, u32[]{:S(2)}) collective-permute-start(bf16[2,18,1,128]{3,2,0,1:T(2,128)(2,1)S(1)} %get-tuple-element.646), channel_id=1, source_target_pairs={{0,1},{2,3},{4,5},{6,7},{8,9},{10,11},{12,13},{14,15},{16,17},{18,... | collective-permute-start | bytes 27656 | tf_op jit(solution)/shard_map/ppermute | solution.py:26
  742.5 33.8 %collective-permute-start.7 = (bf16[2,18,1,128]{3,2,0,1:T(2,128)(2,1)S(1)}, bf16[2,18,1,128]{3,2,0,1:T(2,128)(2,1)S(1)}, u32[]{:S(2)}, u32[]{:S(2)}) collective-permute-start(bf16[2,18,1,128]{3,2,0,1:T(2,128)(2,1)S(1)} %get-tuple-element.645), channel_id=1, source_target_pairs={{1,0},{3,2},{5,4},{7,6},{9,8},{11,10},{13,12},{15,14},{17,16},{19,... | collective-permute-start | bytes 27656 | tf_op jit(solution)/shard_map/ppermute | solution.py:29
  743.9 81.1 %collective-permute-start.30 = (bf16[2,18,1,128]{3,2,0,1:T(2,128)(2,1)S(1)}, bf16[2,18,1,128]{3,2,0,1:T(2,128)(2,1)S(1)}, u32[]{:S(2)}, u32[]{:S(2)}) collective-permute-start(bf16[2,18,1,128]{3,2,0,1:T(2,128)(2,1)S(1)} %get-tuple-element.622), channel_id=1, source_target_pairs={{0,1},{2,3},{4,5},{6,7},{8,9},{10,11},{12,13},{14,15},{16,17},{18,... | collective-permute-start | bytes 27656 | tf_op jit(solution)/shard_map/ppermute | solution.py:26
  748.5 80.9 %collective-permute-start.31 = (bf16[2,18,1,128]{3,2,0,1:T(2,128)(2,1)S(1)}, bf16[2,18,1,128]{3,2,0,1:T(2,128)(2,1)S(1)}, u32[]{:S(2)}, u32[]{:S(2)}) collective-permute-start(bf16[2,18,1,128]{3,2,0,1:T(2,128)(2,1)S(1)} %get-tuple-element.621), channel_id=1, source_target_pairs={{1,0},{3,2},{5,4},{7,6},{9,8},{11,10},{13,12},{15,14},{17,16},{19,... | collective-permute-start | bytes 27656 | tf_op jit(solution)/shard_map/ppermute | solution.py:29
  749.8 106.7 %collective-permute-start.22 = (bf16[2,18,1,128]{3,2,0,1:T(2,128)(2,1)S(1)}, bf16[2,18,1,128]{3,2,0,1:T(2,128)(2,1)S(1)}, u32[]{:S(2)}, u32[]{:S(2)}) collective-permute-start(bf16[2,18,1,128]{3,2,0,1:T(2,128)(2,1)S(1)} %get-tuple-element.630), channel_id=1, source_target_pairs={{0,1},{2,3},{4,5},{6,7},{8,9},{10,11},{12,13},{14,15},{16,17},{18,... | collective-permute-start | bytes 27656 | tf_op jit(solution)/shard_map/ppermute | solution.py:26
  774.6 86.3 %collective-permute-start.23 = (bf16[2,18,1,128]{3,2,0,1:T(2,128)(2,1)S(1)}, bf16[2,18,1,128]{3,2,0,1:T(2,128)(2,1)}, u32[]{:S(2)}, u32[]{:S(2)}) collective-permute-start(bf16[2,18,1,128]{3,2,0,1:T(2,128)(2,1)S(1)} %get-tuple-element.629), channel_id=1, source_target_pairs={{1,0},{3,2},{5,4},{7,6},{9,8},{11,10},{13,12},{15,14},{17,16},{19,... | collective-permute-start | bytes 27656 | tf_op jit(solution)/shard_map/ppermute | solution.py:29
  821.0 78.6 %collective-permute-start.32 = (bf16[2,1,64,256]{3,2,1,0:T(8,128)(2,1)S(1)}, bf16[2,1,64,256]{3,2,1,0:T(8,128)(2,1)S(1)}, u32[]{:S(2)}, u32[]{:S(2)}) collective-permute-start(bf16[2,1,64,256]{3,2,1,0:T(8,128)(2,1)S(1)} %get-tuple-element.617), channel_id=1, source_target_pairs={{0,2},{2,4},{4,6},{6,8},{8,10},{10,12},{12,14},{14,16},{16,18},{18... | collective-permute-start | bytes 196616 | tf_op jit(solution)/shard_map/ppermute | solution.py:26
  824.9 79.0 %collective-permute-start.33 = (bf16[2,1,64,256]{3,2,1,0:T(8,128)(2,1)S(1)}, bf16[2,1,64,256]{3,2,1,0:T(8,128)(2,1)S(1)}, u32[]{:S(2)}, u32[]{:S(2)}) collective-permute-start(bf16[2,1,64,256]{3,2,1,0:T(8,128)(2,1)S(1)} %get-tuple-element.618), channel_id=1, source_target_pairs={{2,0},{4,2},{6,4},{8,6},{10,8},{12,10},{14,12},{16,14},{18,16},{20... | collective-permute-start | bytes 196616 | tf_op jit(solution)/shard_map/ppermute | solution.py:29
  829.4 74.7 %collective-permute-start.36 = (bf16[2,1,64,256]{3,2,1,0:T(8,128)(2,1)S(1)}, bf16[2,1,64,256]{3,2,1,0:T(8,128)(2,1)S(1)}, u32[]{:S(2)}, u32[]{:S(2)}) collective-permute-start(bf16[2,1,64,256]{3,2,1,0:T(8,128)(2,1)S(1)} %get-tuple-element.612), channel_id=1, source_target_pairs={{0,2},{2,4},{4,6},{6,8},{8,10},{10,12},{12,14},{14,16},{16,18},{18... | collective-permute-start | bytes 196616 | tf_op jit(solution)/shard_map/ppermute | solution.py:26
  856.5 52.1 %collective-permute-start.37 = (bf16[2,1,64,256]{3,2,1,0:T(8,128)(2,1)S(1)}, bf16[2,1,64,256]{3,2,1,0:T(8,128)(2,1)S(1)}, u32[]{:S(2)}, u32[]{:S(2)}) collective-permute-start(bf16[2,1,64,256]{3,2,1,0:T(8,128)(2,1)S(1)} %get-tuple-element.613), channel_id=1, source_target_pairs={{2,0},{4,2},{6,4},{8,6},{10,8},{12,10},{14,12},{16,14},{18,16},{20... | collective-permute-start | bytes 196616 | tf_op jit(solution)/shard_map/ppermute | solution.py:29
  895.5 16.7 %collective-permute-start.40 = (bf16[2,1,64,256]{3,2,1,0:T(8,128)(2,1)S(1)}, bf16[2,1,64,256]{3,2,1,0:T(8,128)(2,1)S(1)}, u32[]{:S(2)}, u32[]{:S(2)}) collective-permute-start(bf16[2,1,64,256]{3,2,1,0:T(8,128)(2,1)S(1)} %get-tuple-element.607), channel_id=1, source_target_pairs={{0,2},{2,4},{4,6},{6,8},{8,10},{10,12},{12,14},{14,16},{16,18},{18... | collective-permute-start | bytes 196616 | tf_op jit(solution)/shard_map/ppermute | solution.py:26
  899.6 17.2 %collective-permute-start.41 = (bf16[2,1,64,256]{3,2,1,0:T(8,128)(2,1)S(1)}, bf16[2,1,64,256]{3,2,1,0:T(8,128)(2,1)S(1)}, u32[]{:S(2)}, u32[]{:S(2)}) collective-permute-start(bf16[2,1,64,256]{3,2,1,0:T(8,128)(2,1)S(1)} %get-tuple-element.608), channel_id=1, source_target_pairs={{2,0},{4,2},{6,4},{8,6},{10,8},{12,10},{14,12},{16,14},{18,16},{20... | collective-permute-start | bytes 196616 | tf_op jit(solution)/shard_map/ppermute | solution.py:29
  903.9 16.5 %collective-permute-start.44 = (bf16[2,1,64,256]{3,2,1,0:T(8,128)(2,1)S(1)}, bf16[2,1,64,256]{3,2,1,0:T(8,128)(2,1)S(1)}, u32[]{:S(2)}, u32[]{:S(2)}) collective-permute-start(bf16[2,1,64,256]{3,2,1,0:T(8,128)(2,1)S(1)} %get-tuple-element.602), channel_id=1, source_target_pairs={{0,2},{2,4},{4,6},{6,8},{8,10},{10,12},{12,14},{14,16},{16,18},{18... | collective-permute-start | bytes 196616 | tf_op jit(solution)/shard_map/ppermute | solution.py:26
  904.1 22.0 %collective-permute-start.45 = (bf16[2,1,64,256]{3,2,1,0:T(8,128)(2,1)S(1)}, bf16[2,1,64,256]{3,2,1,0:T(8,128)(2,1)S(1)}, u32[]{:S(2)}, u32[]{:S(2)}) collective-permute-start(bf16[2,1,64,256]{3,2,1,0:T(8,128)(2,1)S(1)} %get-tuple-element.603), channel_id=1, source_target_pairs={{2,0},{4,2},{6,4},{8,6},{10,8},{12,10},{14,12},{16,14},{18,16},{20... | collective-permute-start | bytes 196616 | tf_op jit(solution)/shard_map/ppermute | solution.py:29
  908.6 21.0 %collective-permute-start.34 = (bf16[2,18,1,256]{3,2,1,0:T(2,128)(2,1)S(1)}, bf16[2,18,1,256]{3,2,1,0:T(2,128)(2,1)S(1)}, u32[]{:S(2)}, u32[]{:S(2)}) collective-permute-start(bf16[2,18,1,256]{3,2,1,0:T(2,128)(2,1)S(1)} %get-tuple-element.596), channel_id=1, source_target_pairs={{1,0},{3,2},{5,4},{7,6},{9,8},{11,10},{13,12},{15,14},{17,16},{19,... | collective-permute-start | bytes 55304 | tf_op jit(solution)/shard_map/ppermute | solution.py:29
  912.2 23.2 %collective-permute-start.35 = (bf16[2,18,1,256]{3,2,1,0:T(2,128)(2,1)S(1)}, bf16[2,18,1,256]{3,2,1,0:T(2,128)(2,1)S(1)}, u32[]{:S(2)}, u32[]{:S(2)}) collective-permute-start(bf16[2,18,1,256]{3,2,1,0:T(2,128)(2,1)S(1)} %get-tuple-element.595), channel_id=1, source_target_pairs={{0,1},{2,3},{4,5},{6,7},{8,9},{10,11},{12,13},{14,15},{16,17},{18,... | collective-permute-start | bytes 55304 | tf_op jit(solution)/shard_map/ppermute | solution.py:26
  916.9 37.1 %collective-permute-start.38 = (bf16[2,18,1,256]{3,2,1,0:T(2,128)(2,1)}, bf16[2,18,1,256]{3,2,1,0:T(2,128)(2,1)}, u32[]{:S(2)}, u32[]{:S(2)}) collective-permute-start(bf16[2,18,1,256]{3,2,1,0:T(2,128)(2,1)} %get-tuple-element.592), channel_id=1, source_target_pairs={{1,0},{3,2},{5,4},{7,6},{9,8},{11,10},{13,12},{15,14},{17,16},{19,... | collective-permute-start | bytes 55304 | tf_op jit(solution)/shard_map/ppermute | solution.py:29
  920.3 39.0 %collective-permute-start.39 = (bf16[2,18,1,256]{3,2,1,0:T(2,128)(2,1)}, bf16[2,18,1,256]{3,2,1,0:T(2,128)(2,1)}, u32[]{:S(2)}, u32[]{:S(2)}) collective-permute-start(bf16[2,18,1,256]{3,2,1,0:T(2,128)(2,1)} %get-tuple-element.591), channel_id=1, source_target_pairs={{0,1},{2,3},{4,5},{6,7},{8,9},{10,11},{12,13},{14,15},{16,17},{18,... | collective-permute-start | bytes 55304 | tf_op jit(solution)/shard_map/ppermute | solution.py:26
  926.1 42.4 %collective-permute-start.42 = (bf16[2,18,1,256]{3,2,1,0:T(2,128)(2,1)}, bf16[2,18,1,256]{3,2,1,0:T(2,128)(2,1)}, u32[]{:S(2)}, u32[]{:S(2)}) collective-permute-start(bf16[2,18,1,256]{3,2,1,0:T(2,128)(2,1)} %get-tuple-element.588), channel_id=1, source_target_pairs={{1,0},{3,2},{5,4},{7,6},{9,8},{11,10},{13,12},{15,14},{17,16},{19,... | collective-permute-start | bytes 55304 | tf_op jit(solution)/shard_map/ppermute | solution.py:29
  929.6 38.9 %collective-permute-start.43 = (bf16[2,18,1,256]{3,2,1,0:T(2,128)(2,1)}, bf16[2,18,1,256]{3,2,1,0:T(2,128)(2,1)}, u32[]{:S(2)}, u32[]{:S(2)}) collective-permute-start(bf16[2,18,1,256]{3,2,1,0:T(2,128)(2,1)} %get-tuple-element.587), channel_id=1, source_target_pairs={{0,1},{2,3},{4,5},{6,7},{8,9},{10,11},{12,13},{14,15},{16,17},{18,... | collective-permute-start | bytes 55304 | tf_op jit(solution)/shard_map/ppermute | solution.py:26
  935.3 42.2 %collective-permute-start.46 = (bf16[2,18,1,256]{3,2,1,0:T(2,128)(2,1)}, bf16[2,18,1,256]{3,2,1,0:T(2,128)(2,1)}, u32[]{:S(2)}, u32[]{:S(2)}) collective-permute-start(bf16[2,18,1,256]{3,2,1,0:T(2,128)(2,1)} %get-tuple-element.584), channel_id=1, source_target_pairs={{1,0},{3,2},{5,4},{7,6},{9,8},{11,10},{13,12},{15,14},{17,16},{19,... | collective-permute-start | bytes 55304 | tf_op jit(solution)/shard_map/ppermute | solution.py:29
  950.4 53.3 %all-to-all-start.32 = ((bf16[16,2,8192]{2,1,0:T(2,128)(2,1)}), bf16[16,2,8192]{2,1,0:T(2,128)(2,1)S(1)}, u32[]{:S(2)}, u32[]{:S(2)}) async-start(bf16[16,2,8192]{2,1,0:T(2,128)(2,1)} %reshape.2342), calls=%async_computation.32 | async-start | bytes 1048576 | tf_op jit(solution)/shard_map/all_to_all | solution.py:62
  954.0 23.5 %collective-permute-start.47 = (bf16[2,18,1,256]{3,2,1,0:T(2,128)(2,1)S(1)}, bf16[2,18,1,256]{3,2,1,0:T(2,128)(2,1)S(1)}, u32[]{:S(2)}, u32[]{:S(2)}) collective-permute-start(bf16[2,18,1,256]{3,2,1,0:T(2,128)(2,1)S(1)} %copy-done.174), channel_id=1, source_target_pairs={{0,1},{2,3},{4,5},{6,7},{8,9},{10,11},{12,13},{14,15},{16,17},{18,... | collective-permute-start | bytes 55304 | tf_op jit(solution)/shard_map/ppermute | solution.py:26
  1003.7 20.5 %all-to-all-start.36 = ((bf16[16,2,8192]{2,1,0:T(2,128)(2,1)}), bf16[16,2,8192]{2,1,0:T(2,128)(2,1)}, u32[]{:S(2)}, u32[]{:S(2)}) async-start(bf16[16,2,8192]{2,1,0:T(2,128)(2,1)} %reshape.2348), calls=%async_computation.36 | async-start | bytes 1048576 | tf_op jit(solution)/shard_map/all_to_all | solution.py:62
  1024.3 19.3 %all-to-all-start.40 = ((bf16[16,2,8192]{2,1,0:T(2,128)(2,1)}), bf16[16,2,8192]{2,1,0:T(2,128)(2,1)}, u32[]{:S(2)}, u32[]{:S(2)}) async-start(bf16[16,2,8192]{2,1,0:T(2,128)(2,1)} %reshape.2354), calls=%async_computation.40 | async-start | bytes 1048576 | tf_op jit(solution)/shard_map/all_to_all | solution.py:62
  1043.6 47.9 %all-to-all-start.44 = ((bf16[16,2,8192]{2,1,0:T(2,128)(2,1)}), bf16[16,2,8192]{2,1,0:T(2,128)(2,1)S(1)}, u32[]{:S(2)}, u32[]{:S(2)}) async-start(bf16[16,2,8192]{2,1,0:T(2,128)(2,1)} %reshape.2360), calls=%async_computation.44 | async-start | bytes 1048576 | tf_op jit(solution)/shard_map/all_to_all | solution.py:62
  1189.1 38.8 %all-to-all-start.35 = ((bf16[16,2,8192]{2,1,0:T(2,128)(2,1)}), bf16[16,2,8192]{2,1,0:T(2,128)(2,1)S(1)}, u32[]{:S(2)}, u32[]{:S(2)}) async-start(bf16[16,2,8192]{2,1,0:T(2,128)(2,1)} %reshape.2346), calls=%async_computation.35 | async-start | bytes 1048576 | tf_op jit(solution)/shard_map/all_to_all | solution.py:81
  1227.9 20.5 %all-to-all-start.39 = ((bf16[16,2,8192]{2,1,0:T(2,128)(2,1)}), bf16[16,2,8192]{2,1,0:T(2,128)(2,1)S(1)}, u32[]{:S(2)}, u32[]{:S(2)}) async-start(bf16[16,2,8192]{2,1,0:T(2,128)(2,1)} %reshape.2352), calls=%async_computation.39 | async-start | bytes 1048576 | tf_op jit(solution)/shard_map/all_to_all | solution.py:81
  1249.2 27.2 %all-to-all-start.43 = ((bf16[16,2,8192]{2,1,0:T(2,128)(2,1)}), bf16[16,2,8192]{2,1,0:T(2,128)(2,1)S(1)}, u32[]{:S(2)}, u32[]{:S(2)}) async-start(bf16[16,2,8192]{2,1,0:T(2,128)(2,1)} %reshape.2358), calls=%async_computation.43 | async-start | bytes 1048576 | tf_op jit(solution)/shard_map/all_to_all | solution.py:81
  1276.4 29.5 %all-to-all-start.47 = ((bf16[16,2,8192]{2,1,0:T(2,128)(2,1)}), bf16[16,2,8192]{2,1,0:T(2,128)(2,1)S(1)}, u32[]{:S(2)}, u32[]{:S(2)}) async-start(bf16[16,2,8192]{2,1,0:T(2,128)(2,1)} %reshape.2364), calls=%async_computation.47 | async-start | bytes 1048576 | tf_op jit(solution)/shard_map/all_to_all | solution.py:81
  1282.5 218.1 %all-reduce.4.cloned.1.call-start = ((), (), s32[]{:S(2)}) async-start(), calls=%async_computation.48 | async-start | bytes 6291456 | tf_op jit(solution)/shard_map/psum | solution.py:229
  (333 other events, 8155.2 us)
Sparse Core Ops, SparseCore 0:
  1360.3 140.2 all-reduce.3
where the time goes:
time: 1530 us; the launch traced here: 1520 us
  local copies, waits for them, and re-layouts  602 us (39%)
  starting transfers between devices  349 us (23%)
  matrix products  196 us (13%)
  waiting for transfers between devices  183 us (12%)
  other arithmetic  124 us (8%)
  blocking collectives  41.3 us (3%)
  between operations  25.5 us (2%)
    unnamed x752, local copies, waits for them, and re-layouts  240 us
    another operation x20, local copies, waits for them, and re-layouts, neighbours(): stacked = jnp.stack(parts, axis=3)  112 us
    psum x1, waiting for transfers between devices, body(): lax.psum((sums[0], sums[1], sums[2], sums[3], loss, total), ('lon', 'lat'))  93.7 us
    ppermute x24, starting transfers between devices, with_halo(): lax.ppermute(lax.slice_in_dim(block, 0, width, axis=dim), axis, backward)  69 us
    all_to_all x12, starting transfers between devices, spectral(): lax.all_to_all(grid.astype(jnp.bfloat16), 'lon', split_axis=1, concat_axi...  65.9 us
    all_to_all x12, starting transfers between devices, spectral(): lax.all_to_all(values.astype(jnp.bfloat16), 'lon', split_axis=3, concat_a...  65.4 us
    ppermute x24, starting transfers between devices, with_halo(): lax.ppermute(lax.slice_in_dim(block, block.shape[dim] - width, None, axis...  57.7 us
    all_to_all x12, starting transfers between devices, spectral(): lax.all_to_all(back.astype(jnp.bfloat16), 'lat', split_axis=2, concat_axi...  45.6 us
  transfers between devices with their start and end apart: 97, of which 28 were waited for; matrix products, arithmetic and copies ran while one was open for 53% of the time, Pallas kernels for 0%

commit v1 on v0

--- a/solution.py
+++ b/solution.py
@@ -1,8 +1,12 @@
+import functools
 import math
 
 import jax
 import jax.numpy as jnp
+import numpy as np
 from jax import lax
+from jax.experimental import pallas as pl
+from jax.experimental.pallas import tpu as pltpu
 from jax.sharding import PartitionSpec as P
 
 MW = 86
@@ -14,6 +18,660 @@
 MOMENTUM = 0.9
 AVERAGE = 0.99
 RATE_BASE = 0.0006
+
+F32 = jnp.float32
+BF16 = jnp.bfloat16
+CHUNK = 4
+VMEM = 56 * 1024 * 1024
+GELU_A = math.sqrt(2.0 / math.pi)
+GELU_B = 0.044715
+
+
+def split_table(table):
+    table = np.asarray(table, np.float32)
+    high = table.astype(BF16)
+    low = (table - high.astype(np.float32)).astype(BF16)
+    return np.concatenate([high, low], axis=0)
+
+
+def host_tables(nlon, nlat, deg):
+    kept = np.arange(2 * MW)
+    wave = np.where(kept < MW, kept, kept - MW + 1).astype(np.float64)
+    angle = 2.0 * np.pi * wave[:, None] * np.arange(nlon)[None, :] / nlon
+    fourier = np.where((kept < MW)[:, None], np.cos(angle), np.sin(angle)) * np.sqrt(2.0 / nlon)
+    zonal = (fourier * (1.0 - 0.5 * wave / MW)[:, None]).T @ fourier
+    phase = ((np.arange(nlat) + 0.5) / nlat - 0.5) * np.pi
+    sine, area = np.sin(phase), np.cos(phase)
+    polys = [np.ones_like(sine), sine]
+    for n in range(1, NDEG - 1):
+        polys.append(((2 * n + 1) * sine * polys[-1] - n * polys[-2]) / (n + 1))
+    degrees = np.arange(NDEG)
+    legendre = np.sqrt((2 * degrees + 1) / 2)[:, None] * np.sqrt(area * np.pi / nlat)[None, :]
+    legendre = legendre * np.stack(polys)
+    damping = 1.5 * (1.0 - 2.0 * degrees * (degrees + 1) / (NDEG * (NDEG + 1)))
+    forward = np.zeros((deg, nlat))
+    forward[:NDEG] = legendre
+    inverse = np.zeros((nlat, -(-deg // 32) * 32))
+    inverse[:, :NDEG] = (legendre * damping[:, None]).T
+    return split_table(zonal), split_table(forward), split_table(inverse), area
+
+
+def mm(a, b):
+    return jnp.dot(a, b, preferred_element_type=F32)
+
+
+def mm_rows(a, b):
+    return lax.dot_general(a, b, (((0,), (0,)), ((), ())), preferred_element_type=F32)
+
+
+def whole(shape):
+    return pl.BlockSpec(shape, lambda *_: (0,) * len(shape))
+
+
+def params():
+    return pltpu.CompilerParams(vmem_limit_bytes=VMEM)
+
+
+def legendre_kernel(x_ref, l_ref, o_ref, tmp):
+    lon_t = x_ref.shape[2]
+    deg = l_ref.shape[0] // 2
+    chans = x_ref.shape[-1]
+    for base in range(0, lon_t, 4):
+        cols = [
+            jnp.concatenate([x_ref[h, 0, base + i] for h in range(x_ref.shape[0])], axis=0)
+            for i in range(4)
+        ]
+        r = mm(l_ref[...], jnp.concatenate(cols, axis=1))
+        r = r[:deg] + r[deg:]
+        for i in range(4):
+            tmp[:, base + i, :] = r[:, i * chans : (i + 1) * chans]
+    o_ref[...] = tmp[...].astype(BF16).reshape(o_ref.shape)
+
+
+def legendre_call(fields, table):
+    hemis, snaps, lon_t, lat_t, chans = fields.shape
+    deg = table.shape[0] // 2
+    parts = 8
+    return pl.pallas_call(
+        legendre_kernel,
+        grid=(snaps,),
+        in_specs=[
+            pl.BlockSpec((hemis, 1, lon_t, lat_t, chans), lambda s: (0, s, 0, 0, 0)),
+            whole(table.shape),
+        ],
+        out_specs=pl.BlockSpec((parts, deg // parts, lon_t, chans), lambda s: (s, 0, 0, 0)),
+        out_shape=jax.ShapeDtypeStruct((snaps * parts, deg // parts, lon_t, chans), BF16),
+        scratch_shapes=[pltpu.VMEM((deg, lon_t, chans), F32)],
+        compiler_params=params(),
+        name="legendre",
+    )(fields, table)
+
+
+def zonal_kernel(x_ref, a_ref, o_ref):
+    groups, rows, lon_t, chans = x_ref.shape
+    nlon = groups * lon_t
+    for base in range(0, rows, 4):
+        count = min(4, rows - base)
+        cols = [x_ref[:, base + i].reshape(nlon, chans) for i in range(count)]
+        r = mm(a_ref[...], jnp.concatenate(cols, axis=1))
+        r = (r[:nlon] + r[nlon:]).astype(BF16)
+        for i in range(count):
+            o_ref[:, base + i] = r[:, i * chans : (i + 1) * chans].reshape(groups, lon_t, chans)
+
+
+def zonal_call(fields, table):
+    return pl.pallas_call(
+        zonal_kernel,
+        in_specs=[pl.BlockSpec(memory_space=pltpu.VMEM)] * 2,
+        out_specs=pl.BlockSpec(memory_space=pltpu.VMEM),
+        out_shape=jax.ShapeDtypeStruct(fields.shape, BF16),
+        compiler_params=params(),
+        name="zonal",
+    )(fields, table)
+
+
+def synthesis_kernel(halo, x_ref, l_ref, o_ref, tmp):
+    parts, rows, lon_t, chans = x_ref.shape
+    deg = parts * rows
+    nlat = l_ref.shape[0] // 2
+    half = nlat // 2
+    tmp[:deg] = x_ref[...].reshape(deg, lon_t, chans).astype(F32)
+    tmp[deg:] = jnp.zeros((tmp.shape[0] - deg, lon_t, chans), F32)
+    for base in range(0, lon_t, 4):
+        cols = jnp.concatenate([tmp[:, base + i, :] for i in range(4)], axis=1).astype(BF16)
+        r = mm(l_ref[...], cols)
+        r = r[:nlat] + r[nlat:]
+        for i in range(4):
+            one = r[:, i * chans : (i + 1) * chans]
+            o_ref[0, 0, base + i] = one[:half].astype(BF16)
+            o_ref[1, 0, base + i] = one[half:].astype(BF16)
+            if halo:
+                tmp[0, base + i : base + i + 1, :] = one[half : half + 1]
+                tmp[1, base + i : base + i + 1, :] = one[half - 1 : half]
+    if halo:
+        rest = jnp.zeros((half - lon_t, chans), BF16)
+        for h in range(2):
+            o_ref[h, 0, lon_t, :lon_t] = tmp[h].astype(BF16)
+            o_ref[h, 0, lon_t, lon_t:] = rest
+
+
+def synthesis_call(coeffs, table, snaps, halo):
+    total, rows, lon_t, chans = coeffs.shape
+    parts = total // snaps
+    nlat = table.shape[0] // 2
+    slabs = lon_t + 1 if halo else lon_t
+    return pl.pallas_call(
+        functools.partial(synthesis_kernel, halo),
+        grid=(snaps,),
+        in_specs=[
+            pl.BlockSpec((parts, rows, lon_t, chans), lambda s: (s, 0, 0, 0)),
+            whole(table.shape),
+        ],
+        out_specs=pl.BlockSpec((2, 1, slabs, nlat // 2, chans), lambda s: (0, s, 0, 0, 0)),
+        out_shape=jax.ShapeDtypeStruct((2, snaps, slabs, nlat // 2, chans), BF16),
+        scratch_shapes=[pltpu.VMEM((table.shape[1], lon_t, chans), F32)],
+        compiler_params=params(),
+        name="synthesis",
+    )(coeffs, table)
+
+
+def spectral_fast(low, tabs, halo):
+    zonal, forward, inverse = tabs
+    snaps, lon_t, lat_t, chans = low.shape
+    mine = snaps // 2
+    cols = lax.all_to_all(low, "lat", split_axis=0, concat_axis=0, tiled=True)
+    spec = legendre_call(cols.reshape(2, mine, lon_t, lat_t, chans), forward)
+    spec = lax.all_to_all(spec, "lon", split_axis=0, concat_axis=0, tiled=True)
+    spec = zonal_call(spec, zonal)
+    spec = lax.all_to_all(spec, "lon", split_axis=0, concat_axis=0, tiled=True)
+    back = synthesis_call(spec, inverse, mine, halo)
+    back = lax.all_to_all(back, "lat", split_axis=0, concat_axis=0, tiled=True)
+    return back.reshape((snaps,) + back.shape[2:])
+
+
+def gelu_of(x):
+    t = jnp.tanh(x * (GELU_A + (GELU_A * GELU_B) * (x * x)))
+    return 0.5 * x * (1.0 + t)
+
+
+def gelu_and_slope(x):
+    sq = x * x
+    t = jnp.tanh(x * (GELU_A + (GELU_A * GELU_B) * sq))
+    cdf = 0.5 + 0.5 * t
+    slope = cdf + (0.5 * x) * (1.0 - t * t) * (GELU_A + (3.0 * GELU_A * GELU_B) * sq)
+    return x * cdf, slope
+
+
+def fill_patches(patches, moved, halo_row, lon_lo, lon_hi, masks):
+    lon_t, lat_t, chans = moved.shape
+    slabs = [lon_lo[:lat_t].astype(F32)] + [moved[i] for i in range(lon_t)] + [lon_hi[:lat_t].astype(F32)]
+    ends = [lon_lo[lat_t : lat_t + 1].astype(F32)]
+    ends += [halo_row[i : i + 1] for i in range(lon_t)]
+    ends += [lon_hi[lat_t : lat_t + 1].astype(F32)]
+    place = lax.broadcasted_iota(jnp.int32, (lat_t, chans), 0)
+    for i in range(lon_t + 2):
+        low_row, high_row = ends[i] * masks[0:1], ends[i] * masks[1:2]
+        down = jnp.where(place == 0, low_row, pltpu.roll(slabs[i], 1, 0)).astype(BF16)
+        up = jnp.where(place == lat_t - 1, high_row, pltpu.roll(slabs[i], lat_t - 1, 0)).astype(BF16)
+        mid = slabs[i].astype(BF16)
+        for a in range(3):
+            x = i - a
+            if 0 <= x < lon_t:
+                for b, piece in enumerate((down, mid, up)):
+                    k = 3 * a + b
+                    patches[x * lat_t : (x + 1) * lat_t, k * chans : (k + 1) * chans] = piece
+
+
+def assemble(patches, state_ref, s_ref, row_ref, lo_ref, hi_ref, extra_ref, masks_ref, moved):
+    lon_t, lat_t, chans = moved.shape
+    moved[...] = state_ref[0].astype(F32) + s_ref[0, :lon_t].astype(F32)
+    halo_row = row_ref[0].astype(F32) + s_ref[0, lon_t, :lon_t].astype(F32)
+    fill_patches(patches, moved, halo_row, lo_ref[0], hi_ref[0], masks_ref[...])
+    patches[:, 9 * chans :] = extra_ref[0]
+
+
+def forward_kernel(
+    state_ref, s_ref, row_ref, lo_ref, hi_ref, extra_ref, masks_ref, w1_ref, mid_ref, dec_ref, bias_ref,
+    state_out, low_out, pre1_out, pre2_out, patches, moved,
+):
+    lon_t, lat_t, chans = moved.shape
+    hid = mid_ref.shape[0]
+    assemble(patches, state_ref, s_ref, row_ref, lo_ref, hi_ref, extra_ref, masks_ref, moved)
+    step = 4
+    for x in range(0, lon_t, step):
+        rows = slice(x * lat_t, (x + step) * lat_t)
+        pre1 = mm(patches[rows], w1_ref[...])
+        pre1_out[0, rows] = pre1
+        active1 = gelu_of(pre1).astype(BF16)
+        pre2 = mm(active1, mid_ref[...]) + bias_ref[0:1, :hid]
+        pre2_out[0, rows] = pre2
+        active2 = gelu_of(pre2).astype(BF16)
+        out = mm(active2, dec_ref[...]) + bias_ref[1:2, :chans]
+        fresh = moved[x : x + step] + out.reshape(step, lat_t, chans)
+        state_out[0, x : x + step] = fresh
+        low_out[0, x : x + step] = fresh.astype(BF16)
+
+
+def grad_layout(chans, hid):
+    return (9 * chans, 9 * chans + hid, 9 * chans + hid + chans, 9 * chans + hid + chans + 8)
+
+
+def add_grads(first, patches, active1, active2, g_out, g_pre2, g_pre1, acc_enc, acc_mid, acc_dec):
+    enc = mm_rows(patches[...], g_pre1[...])
+    mid = mm_rows(active1[...], g_pre2[...])
+    dec = mm_rows(g_out[...], active2[...])
+
+    @pl.when(first)
+    def _():
+        acc_enc[...] = enc
+        acc_mid[...] = mid
+        acc_dec[...] = dec
+
+    @pl.when(jnp.logical_not(first))
+    def _():
+        acc_enc[...] += enc
+        acc_mid[...] += mid
+        acc_dec[...] += dec
+
+
+def pack_grads(out, chans, hid, acc_enc, acc_mid, acc_dec, vec2, tail):
+    one, two, three, _ = grad_layout(chans, hid)
+    out[:one] = acc_enc[:one]
+    out[one:two] = acc_mid[...]
+    out[two:three] = acc_dec[...]
+    out[three : three + 1] = acc_enc[one + 3 : one + 4]
+    out[three + 1 : three + 2] = acc_enc[one : one + 1]
+    out[three + 2 : three + 3] = vec2
+    out[three + 3 : three + 4] = tail
+    out[three + 4 :] = jnp.zeros((4, hid), F32)
+
+
+def turn_kernel(
+    state_ref, s_ref, row_ref, lo_ref, hi_ref, extra_ref, masks_ref, w1_ref, mid_ref, dec_ref, bias_ref,
+    target_ref, area_ref, w1t_ref, midt_ref, dect_ref,
+    gm_out, edge_out, rows_out, grads_out,
+    patches, moved, active1, active2, slope1, slope2, g_out, g_pre2, g_pre1, spread, acc_enc, acc_mid, acc_dec, vecs,
+):
+    lon_t, lat_t, chans = moved.shape
+    hid = mid_ref.shape[0]
+    first = pl.program_id(0) == 0
+    assemble(patches, state_ref, s_ref, row_ref, lo_ref, hi_ref, extra_ref, masks_ref, moved)
+    spread[...] = jnp.zeros_like(spread)
+
+    @pl.when(first)
+    def _():
+        vecs[...] = jnp.zeros_like(vecs)
+
+    step = 4
+    for x in range(0, lon_t, step):
+        rows = slice(x * lat_t, (x + step) * lat_t)
+        pre1 = mm(patches[rows], w1_ref[...])
+        a1, d1 = gelu_and_slope(pre1)
+        active1[rows] = a1.astype(BF16)
+        slope1[rows] = d1
+        pre2 = mm(active1[rows], mid_ref[...]) + bias_ref[0:1, :hid]
+        a2, d2 = gelu_and_slope(pre2)
+        active2[rows] = a2.astype(BF16)
+        slope2[rows] = d2
+        out = mm(active2[rows], dec_ref[...]) + bias_ref[1:2, :chans]
+        fresh = moved[x : x + step] + out.reshape(step, lat_t, chans)
+        diff = fresh - target_ref[0, x : x + step].astype(F32)
+        valid = jnp.broadcast_to(extra_ref[0, rows, 6:7].astype(F32), (step * lat_t, chans))
+        weighted = valid.reshape(step, lat_t, chans) * area_ref[...][None] * diff
+        vecs[1:2, :chans] += jnp.sum((weighted * diff).reshape(step * lat_t, chans), 0, keepdims=True)
+        grad = 2.0 * weighted
+        moved[x : x + step] = grad
+        low = grad.reshape(step * lat_t, chans).astype(BF16)
+        g_out[rows] = low
+        vecs[2:3, :chans] += jnp.sum(low.astype(F32), 0, keepdims=True)
+        gp2 = (mm(low, dect_ref[...]) * slope2[rows]).astype(BF16)
+        g_pre2[rows] = gp2
+        vecs[0:1] += jnp.sum(gp2.astype(F32), 0, keepdims=True)
+        gp1 = (mm(gp2, midt_ref[...]) * slope1[rows]).astype(BF16)
+        g_pre1[rows] = gp1
+        taps = mm(gp1, w1t_ref[...])
+        for a in range(3):
+            for b in range(3):
+                k = 3 * a + b
+                spread[b, x + a : x + a + step] += taps[:, k * chans : (k + 1) * chans].reshape(
+                    step, lat_t, chans
+                )
+    place = lax.broadcasted_iota(jnp.int32, (lat_t, chans), 0)
+    masks = masks_ref[...]
+    for i in range(lon_t + 2):
+        down, here, up = spread[0, i], spread[1, i], spread[2, i]
+        got = here + jnp.where(place == lat_t - 1, 0.0, pltpu.roll(down, lat_t - 1, 0))
+        got = got + jnp.where(place == 0, 0.0, pltpu.roll(up, 1, 0))
+        rows_out[0, i : i + 1] = down[0:1] * masks[0:1] + up[lat_t - 1 : lat_t] * masks[1:2]
+        if i == 0:
+            edge_out[0, 0] = got
+        elif i == lon_t + 1:
+            edge_out[0, 1] = got
+        else:
+            gm_out[0, i - 1] = got + moved[i - 1]
+    add_grads(first, patches, active1, active2, g_out, g_pre2, g_pre1, acc_enc, acc_mid, acc_dec)
+
+    @pl.when(pl.program_id(0) == pl.num_programs(0) - 1)
+    def _():
+        tail = jnp.concatenate([vecs[2:3, :chans], vecs[1:2, :chans]], axis=1)
+        pack_grads(grads_out, chans, hid, acc_enc, acc_mid, acc_dec, vecs[0:1], tail)
+
+
+def bottom_kernel(
+    state_ref, s_ref, row_ref, lo_ref, hi_ref, extra_ref, masks_ref, pre1_ref, pre2_ref, gm_ref, gs_ref,
+    midt_ref, dect_ref, grads_out,
+    patches, moved, active1, active2, g_out, g_pre2, g_pre1, acc_enc, acc_mid, acc_dec, vecs,
+):
+    lon_t, lat_t, chans = moved.shape
+    hid = midt_ref.shape[0]
+    first = pl.program_id(0) == 0
+    assemble(patches, state_ref, s_ref, row_ref, lo_ref, hi_ref, extra_ref, masks_ref, moved)
+
+    @pl.when(first)
+    def _():
+        vecs[...] = jnp.zeros_like(vecs)
+
+    step = 4
+    for x in range(0, lon_t, step):
+        rows = slice(x * lat_t, (x + step) * lat_t)
+        a1, d1 = gelu_and_slope(pre1_ref[0, rows])
+        active1[rows] = a1.astype(BF16)
+        a2, d2 = gelu_and_slope(pre2_ref[0, rows])
+        active2[rows] = a2.astype(BF16)
+        grad = gm_ref[0, x : x + step] + gs_ref[0, x : x + step].astype(F32)
+        low = grad.reshape(step * lat_t, chans).astype(BF16)
+        g_out[rows] = low
+        vecs[2:3, :chans] += jnp.sum(low.astype(F32), 0, keepdims=True)
+        gp2 = (mm(low, dect_ref[...]) * d2).astype(BF16)
+        g_pre2[rows] = gp2
+        vecs[0:1] += jnp.sum(gp2.astype(F32), 0, keepdims=True)
+        g_pre1[rows] = (mm(gp2, midt_ref[...]) * d1).astype(BF16)
+    add_grads(first, patches, active1, active2, g_out, g_pre2, g_pre1, acc_enc, acc_mid, acc_dec)
+
+    @pl.when(pl.program_id(0) == pl.num_programs(0) - 1)
+    def _():
+        tail = jnp.concatenate([vecs[2:3, :chans], jnp.zeros((1, chans), F32)], axis=1)
+        pack_grads(grads_out, chans, hid, acc_enc, acc_mid, acc_dec, vecs[0:1], tail)
+
+
+def per_snap(shape):
+    return pl.BlockSpec((1,) + shape, lambda s: (s,) + (0,) * len(shape))
+
+
+def field_specs(lon_t, lat_t, chans, edge):
+    return [
+        per_snap((lon_t, lat_t, chans)),
+        per_snap((lon_t + 1, lat_t, chans)),
+        per_snap((lon_t, chans)),
+        per_snap((edge, chans)),
+        per_snap((edge, chans)),
+        per_snap((lon_t * lat_t, chans)),
+        whole((2, chans)),
+    ]
+
+
+def cost(flops):
+    return pl.CostEstimate(flops=int(flops), bytes_accessed=30_000_000, transcendentals=0)
+
+
+def forward_call(field, masks, weights):
+    state, s_ext, row, lo, hi, extra = field
+    snaps, lon_t, lat_t, chans = state.shape
+    hid = weights["mid"].shape[0]
+    cells = lon_t * lat_t
+    ws = [weights[k] for k in ("w1", "mid", "dec", "bias")]
+    return pl.pallas_call(
+        forward_kernel,
+        grid=(snaps,),
+        in_specs=field_specs(lon_t, lat_t, chans, lo.shape[1]) + [whole(w.shape) for w in ws],
+        out_specs=[
+            per_snap((lon_t, lat_t, chans)),
+            per_snap((lon_t, lat_t, chans)),
+            per_snap((cells, hid)),
+            per_snap((cells, hid)),
+        ],
+        out_shape=[
+            jax.ShapeDtypeStruct((snaps, lon_t, lat_t, chans), F32),
+            jax.ShapeDtypeStruct((snaps, lon_t, lat_t, chans), BF16),
+            jax.ShapeDtypeStruct((snaps, cells, hid), F32),
+            jax.ShapeDtypeStruct((snaps, cells, hid), F32),
+        ],
+        scratch_shapes=[
+            pltpu.VMEM((cells, 10 * chans), BF16),
+            pltpu.VMEM((lon_t, lat_t, chans), F32),
+        ],
+        compiler_params=params(),
+        cost_estimate=cost(snaps * cells * 2 * hid * (10 * chans + hid + chans)),
+        name="forward",
+    )(state, s_ext, row, lo, hi, extra, masks, *ws)
+
+
+def acc_scratch(chans, hid):
+    return [
+        pltpu.VMEM((10 * chans, hid), F32),
+        pltpu.VMEM((hid, hid), F32),
+        pltpu.VMEM((chans, hid), F32),
+        pltpu.VMEM((8, hid), F32),
+    ]
+
+
+def turn_call(field, masks, weights, target, area):
+    state, s_ext, row, lo, hi, extra = field
+    snaps, lon_t, lat_t, chans = state.shape
+    hid = weights["mid"].shape[0]
+    cells = lon_t * lat_t
+    ws = [weights[k] for k in ("w1", "mid", "dec", "bias")]
+    wt = [weights[k] for k in ("w1t", "midt", "dect")]
+    grad_rows = grad_layout(chans, hid)[-1]
+    return pl.pallas_call(
+        turn_kernel,
+        grid=(snaps,),
+        in_specs=field_specs(lon_t, lat_t, chans, lo.shape[1])
+        + [whole(w.shape) for w in ws]
+        + [per_snap((lon_t, lat_t, chans)), whole(area.shape)]
+        + [whole(w.shape) for w in wt],
+        out_specs=[
+            per_snap((lon_t, lat_t, chans)),
+            per_snap((2, lat_t, chans)),
+            per_snap((lon_t + 2, chans)),
+            whole((grad_rows, hid)),
+        ],
+        out_shape=[
+            jax.ShapeDtypeStruct((snaps, lon_t, lat_t, chans), F32),
+            jax.ShapeDtypeStruct((snaps, 2, lat_t, chans), F32),
+            jax.ShapeDtypeStruct((snaps, lon_t + 2, chans), F32),
+            jax.ShapeDtypeStruct((grad_rows, hid), F32),
+        ],
+        scratch_shapes=[
+            pltpu.VMEM((cells, 10 * chans), BF16),
+            pltpu.VMEM((lon_t, lat_t, chans), F32),
+            pltpu.VMEM((cells, hid), BF16),
+            pltpu.VMEM((cells, hid), BF16),
+            pltpu.VMEM((cells, hid), F32),
+            pltpu.VMEM((cells, hid), F32),
+            pltpu.VMEM((cells, chans), BF16),
+            pltpu.VMEM((cells, hid), BF16),
+            pltpu.VMEM((cells, hid), BF16),
+            pltpu.VMEM((3, lon_t + 2, lat_t, chans), F32),
+        ]
+        + acc_scratch(chans, hid),
+        compiler_params=params(),
+        cost_estimate=cost(snaps * cells * 6 * hid * (10 * chans + hid + chans)),
+        name="turn",
+    )(state, s_ext, row, lo, hi, extra, masks, *ws, target, area, *wt)
+
+
+def bottom_call(field, masks, weights, pre1, pre2, gm, gs):
+    state, s_ext, row, lo, hi, extra = field
+    snaps, lon_t, lat_t, chans = state.shape
+    hid = weights["mid"].shape[0]
+    cells = lon_t * lat_t
+    wt = [weights[k] for k in ("midt", "dect")]
+    grad_rows = grad_layout(chans, hid)[-1]
+    return pl.pallas_call(
+        bottom_kernel,
+        grid=(snaps,),
+        in_specs=field_specs(lon_t, lat_t, chans, lo.shape[1])
+        + [per_snap((cells, hid)), per_snap((cells, hid))]
+        + [per_snap((lon_t, lat_t, chans)), per_snap((lon_t, lat_t, chans))]
+        + [whole(w.shape) for w in wt],
+        out_specs=whole((grad_rows, hid)),
+        out_shape=jax.ShapeDtypeStruct((grad_rows, hid), F32),
+        scratch_shapes=[
+            pltpu.VMEM((cells, 10 * chans), BF16),
+            pltpu.VMEM((lon_t, lat_t, chans), F32),
+            pltpu.VMEM((cells, hid), BF16),
+            pltpu.VMEM((cells, hid), BF16),
+            pltpu.VMEM((cells, chans), BF16),
+            pltpu.VMEM((cells, hid), BF16),
+            pltpu.VMEM((cells, hid), BF16),
+        ]
+        + acc_scratch(chans, hid),
+        compiler_params=params(),
+        cost_estimate=cost(snaps * cells * 3 * hid * (10 * chans + hid + chans)),
+        name="bottom",
+    )(state, s_ext, row, lo, hi, extra, masks, pre1, pre2, gm, gs, *wt)
+
+
+def three_parts(vec):
+    high = lax.reduce_precision(vec, 8, 7)
+    rest = vec - high
+    mid = lax.reduce_precision(rest, 8, 7)
+    low = lax.reduce_precision(rest - mid, 8, 7)
+    return jnp.stack([high, mid, low], axis=-2)
+
+
+def layer_weights(enc, mid, dec, vec):
+    taps, chans, hid = enc.shape
+    parts = jnp.concatenate([three_parts(vec[hid : 2 * hid]), three_parts(vec[:hid])], axis=0)
+    parts = jnp.pad(parts, ((0, chans - 6), (0, 0)))
+    w1 = jnp.concatenate([enc.reshape(taps * chans, hid), parts], axis=0).astype(BF16)
+    pad = jnp.zeros((hid - chans,), F32)
+    bias = jnp.stack([vec[2 * hid : 3 * hid], jnp.concatenate([vec[3 * hid :], pad])])
+    return {
+        "w1": w1,
+        "mid": mid.astype(BF16),
+        "dec": dec.astype(BF16),
+        "bias": bias,
+        "w1t": jnp.transpose(enc, (2, 0, 1)).reshape(hid, taps * chans).astype(BF16),
+        "midt": mid.T.astype(BF16),
+        "dect": dec.T.astype(BF16),
+    }
+
+
+def reduce_all(part):
+    count = lax.axis_size("lon") * lax.axis_size("lat")
+    rows, wide = part.shape
+    each = -(-rows // (8 * count)) * 8
+    cut = jnp.pad(part, ((0, each * count - rows), (0, 0))).reshape(count, each, wide)
+    got = lax.all_to_all(cut, ("lon", "lat"), split_axis=0, concat_axis=0, tiled=True)
+    mine = jnp.sum(got, axis=0, keepdims=True)
+    spread = jnp.broadcast_to(mine, (count, each, wide))
+    full = lax.all_to_all(spread, ("lon", "lat"), split_axis=0, concat_axis=0, tiled=True)
+    return full.reshape(count * each, wide)[:rows]
+
+
+def fast_grads(states, targets, sea_temp, ocean, valid, w_enc, w_mid, w_dec, biases):
+    pool, lon_t, lat_t, chans = states.shape
+    hid = w_mid.shape[1]
+    lon_n, lat_n = lax.axis_size("lon"), lax.axis_size("lat")
+    nlon, nlat = lon_t * lon_n, lat_t * lat_n
+    zonal, forward, inverse, area_all = host_tables(nlon, nlat, 88)
+    tabs = (jnp.asarray(zonal), jnp.asarray(forward), jnp.asarray(inverse))
+    where = lax.axis_index("lat")
+    side = jnp.stack([where == 1, where == 0]).astype(F32)
+    masks = jnp.broadcast_to(side[:, None], (2, chans))
+    area = lax.dynamic_slice_in_dim(jnp.asarray(area_all, F32), where * lat_t, lat_t)
+    area_wide = jnp.broadcast_to(area[:, None], (lat_t, chans))
+    sea = ocean.astype(F32) * sea_temp.astype(F32)
+    weight_sum = jnp.sum(valid.astype(F32) * area)
+
+    cells = lon_t * lat_t
+    lane = jnp.arange(chans)
+    wide_sea = sea.reshape(pool, cells, 1).astype(BF16)
+    wide_valid = valid.reshape(pool, cells, 1).astype(BF16)
+    extra = jnp.where(lane < 3, wide_sea, jnp.where(lane < 6, jnp.ones((), BF16), wide_valid))
+    extra = jnp.where(lane < 7, extra, jnp.zeros((), BF16))
+
+    layers = [layer_weights(w_enc[i], w_mid[i], w_dec[i], biases[i]) for i in range(2)]
+    up = [(i, (i + 1) % lon_n) for i in range(lon_n)]
+    down = [(t, s) for s, t in up]
+    swap = [(0, 1), (1, 0)]
+
+    def inner_row(field):
+        return jnp.where(where == 0, field[:, :, -1], field[:, :, 0])
+
+    def lon_edges(state, s_ext, row):
+        def edge(i):
+            body = (state[:, i].astype(F32) + s_ext[:, i].astype(F32)).astype(BF16)
+            corner = (row[:, i].astype(F32) + s_ext[:, lon_t, i].astype(F32)).astype(BF16)
+            return jnp.concatenate([body, corner[:, None]], axis=1)
+
+        lo = lax.ppermute(edge(lon_t - 1), "lon", up)
+        hi = lax.ppermute(edge(0), "lon", down)
+        return lo, hi
+
+    rows0 = lax.ppermute(inner_row(states), "lat", swap)
+    totals = [[], []]
+    starts = range(0, pool, CHUNK)
+    for start in starts:
+        cut = slice(start, start + CHUNK)
+        state, row = states[cut], rows0[cut]
+        s_ext = spectral_fast(state, tabs, True)
+        lo, hi = lon_edges(state, s_ext, row)
+        field0 = (state, s_ext, row, lo, hi, extra[cut])
+        fresh, low, pre1, pre2 = forward_call(field0, masks, layers[0])
+        row1 = lax.ppermute(inner_row(fresh), "lat", swap)
+        s_ext = spectral_fast(low, tabs, True)
+        lo, hi = lon_edges(fresh, s_ext, row1)
+        field1 = (fresh, s_ext, row1, lo, hi, extra[cut])
+        gm, edges, rows, found = turn_call(field1, masks, layers[1], targets[cut], area_wide)
+        totals[1].append(found)
+        rows = lax.ppermute(rows, "lat", swap)
+        place = jnp.arange(lat_t)[:, None]
+        inner = jnp.where(where == 0, place == lat_t - 1, place == 0)
+        to_lo = edges[:, 0] + jnp.where(inner, rows[:, 0][:, None], 0.0)
+        to_hi = edges[:, 1] + jnp.where(inner, rows[:, lon_t + 1][:, None], 0.0)
+        from_hi = lax.ppermute(to_lo, "lon", down)
+        from_lo = lax.ppermute(to_hi, "lon", up)
+        lon_place = jnp.arange(lon_t)[:, None, None]
+        gm = gm + jnp.where(inner, rows[:, 1 : lon_t + 1][:, :, None], 0.0)
+        gm = gm + jnp.where(lon_place == 0, from_lo[:, None], 0.0)
+        gm = gm + jnp.where(lon_place == lon_t - 1, from_hi[:, None], 0.0)
+        gs = spectral_fast(gm.astype(BF16), tabs, False)
+        totals[0].append(bottom_call(field0, masks, layers[0], pre1, pre2, gm, gs))
+
+    one, two, three, _ = grad_layout(chans, hid)
+    sums = []
+    for layer_id in range(2):
+        part = sum(totals[layer_id][1:], totals[layer_id][0])
+        if layer_id == 0:
+            part = part.at[three + 4, 0].set(weight_sum)
+        sums.append(reduce_all(part))
+    g_enc = jnp.stack([s[:one] for s in sums])
+    g_mid = jnp.stack([s[one:two] for s in sums])
+    g_dec = jnp.stack([s[two:three].T for s in sums])
+    g_vec = jnp.stack(
+        [jnp.concatenate([s[three : three + 3].reshape(-1), s[three + 3, :chans]]) for s in sums]
+    )
+    loss = jnp.sum(sums[1][three + 3, chans : 2 * chans])
+    total = sums[0][three + 4, 0]
+    return g_enc, g_mid, g_dec, g_vec, loss, total
+
+
+def fits(states, w_mid, lon_n, lat_n):
+    pool, lon_t, lat_t, chans = states.shape
+    return (
+        lat_n == 2
+        and lon_n == 16
+        and lon_t == 16
+        and lat_t % 16 == 0
+        and lat_t >= lon_t
+        and pool % CHUNK == 0
+        and chans == 128
+        and w_mid.shape[1] == 2 * chans
+        and w_mid.shape[0] == 2
+    )
 
 
 def with_halo(block, sides, width, periodic):
@@ -152,26 +810,7 @@
     return (grad_moved + spectral(grad_moved, tabs), (g_enc, g_mid, g_dec, g_vec))
 
 
-def body(
-    states,
-    targets,
-    sea_temp,
-    ocean,
-    valid,
-    order,
-    w_enc,
-    w_mid,
-    w_dec,
-    biases,
-    mom_enc,
-    mom_mid,
-    mom_dec,
-    mom_bias,
-    avg_enc,
-    avg_mid,
-    avg_dec,
-    avg_bias,
-):
+def general_grads(states, targets, sea_temp, ocean, valid, order, w_enc, w_mid, w_dec, biases):
     pool, lon_t, lat_t, chans = states.shape
     layers, hid = (w_mid.shape[0], w_mid.shape[1])
     nlon = lon_t * lax.axis_size("lon")
@@ -229,8 +868,40 @@
     g_enc, g_mid, g_dec, g_vec, loss, total = lax.psum(
         (sums[0], sums[1], sums[2], sums[3], loss, total), ("lon", "lat")
     )
-    grads = (g_enc.reshape(w_enc.shape), g_mid, g_dec, g_vec)
-    rate = RATE_BASE * math.sqrt(pool * nlon * nlat)
+    return g_enc.reshape(w_enc.shape), g_mid, g_dec, g_vec, loss, total
+
+
+def body(
+    states,
+    targets,
+    sea_temp,
+    ocean,
+    valid,
+    order,
+    w_enc,
+    w_mid,
+    w_dec,
+    biases,
+    mom_enc,
+    mom_mid,
+    mom_dec,
+    mom_bias,
+    avg_enc,
+    avg_mid,
+    avg_dec,
+    avg_bias,
+):
+    pool, lon_t, lat_t = states.shape[:3]
+    lon_n, lat_n = lax.axis_size("lon"), lax.axis_size("lat")
+    if fits(states, w_mid, lon_n, lat_n):
+        found = fast_grads(states, targets, sea_temp, ocean, valid, w_enc, w_mid, w_dec, biases)
+    else:
+        found = general_grads(
+            states, targets, sea_temp, ocean, valid, order, w_enc, w_mid, w_dec, biases
+        )
+    loss, total = found[4:]
+    grads = (found[0].reshape(w_enc.shape),) + found[1:4]
+    rate = RATE_BASE * math.sqrt(pool * lon_t * lon_n * lat_t * lat_n)
     news, moms, avgs, copies = ([], [], [], [])
     for weight_now, grad, mom, avg in zip(
         (w_enc, w_mid, w_dec, biases),

time: 1530 us -> 852 us (0.56)
  local copies, waits for them, and re-layouts: 602 us -> 79.9 us
  starting transfers between devices: 349 us -> 145 us
  matrix products: 196 us -> 0 us
  waiting for transfers between devices: 183 us -> 373 us
  Pallas kernels: 0 us -> 168 us
  other arithmetic: 124 us -> 41.5 us
  between operations: 25.5 us -> 2.33 us
    all_to_all x48 -> x26, waiting for transfers between devices: 89.3 us -> 361 us  [the longest x12 162 us: spectral_fast(): spec = lax.all_to_all(spec, 'lon', split_axis=0, concat_axis=0, tiled=True)]
    unnamed x752 -> x167, local copies, waits for them, and re-layouts: 240 us -> 12.7 us
    dot_general x116 -> x0, matrix products: 196 us -> none  [the longest x8 23.8 us: layer_backward(): jnp.einsum('rk,rh->kh', patches, g_pre1, preferred_element_type=jnp.float32)]
    pallas_call x0 -> x24, Pallas kernels: none -> 168 us  [the longest x2 56.3 us: turn_call(): pl.pallas_call(turn_kernel, grid=(snaps,), in_specs=field_specs(lon_t, la...]
    another operation x23 -> x6, local copies, waits for them, and re-layouts: 112 us -> 3.98 us  [the longest x2 2.39 us: fast_grads(): g_mid = jnp.stack([s[one:two] for s in sums])]
    all_to_all x48 -> x26, starting transfers between devices: 222 us -> 117 us  [the longest x12 60.4 us: spectral_fast(): spec = lax.all_to_all(spec, 'lon', split_axis=0, concat_axis=0, tiled=True)]
    convert_element_type x64 -> x10, local copies, waits for them, and re-layouts: 108 us -> 5.57 us  [the longest x2 1.52 us: layer_weights(): mid.astype(BF16)]
    ppermute x48 -> x17, starting transfers between devices: 127 us -> 28.5 us  [the longest x4 12.2 us: lon_edges(): hi = lax.ppermute(edge(0), 'lon', down)]
  transfers between devices with their start and end apart: 97 -> 43, of which waited for: 28 -> 29; matrix products, arithmetic and copies ran while one was open for 53% -> 8% of each run, Pallas kernels for 0% -> 18%
where the time goes in v1:
time: 852 us; the launch traced here: 841 us
  waiting for transfers between devices  373 us (44%)
  Pallas kernels  168 us (20%)
  starting transfers between devices  145 us (17%)
  local copies, waits for them, and re-layouts  79.9 us (9%)
  other arithmetic  41.5 us (5%)
  blocking collectives  31.2 us (4%)
    all_to_all x12, waiting for transfers between devices, spectral_fast(): spec = lax.all_to_all(spec, 'lon', split_axis=0, concat_axis=0, tiled=True)  162 us
    all_to_all x2, waiting for transfers between devices, reduce_all(): lax.all_to_all(spread, ('lon', 'lat'), split_axis=0, concat_axis=0, tiled...  80.8 us
    all_to_all x12, starting transfers between devices, spectral_fast(): spec = lax.all_to_all(spec, 'lon', split_axis=0, concat_axis=0, tiled=True)  60.4 us
    pallas_call x2, Pallas kernels, turn_call(): pl.pallas_call(turn_kernel, grid=(snaps,), in_specs=field_specs(lon_t, la...  56.3 us
    all_to_all x2, waiting for transfers between devices, reduce_all(): lax.all_to_all(cut, ('lon', 'lat'), split_axis=0, concat_axis=0, tiled=True)  52.5 us
    all_to_all x6, waiting for transfers between devices, spectral_fast(): back = lax.all_to_all(back, 'lat', split_axis=0, concat_axis=0, tiled=True)  42 us
    all_to_all x2, blocking collectives, spectral_fast(): cols = lax.all_to_all(low, 'lat', split_axis=0, concat_axis=0, tiled=True)  31.2 us
    pallas_call x2, Pallas kernels, bottom_call(): pl.pallas_call(bottom_kernel, grid=(snaps,), in_specs=field_specs(lon_t,...  29.2 us
  transfers between devices with their start and end apart: 43, of which 29 were waited for; matrix products, arithmetic and copies ran while one was open for 8% of the time, Pallas kernels for 18%

profile of v1, /device:TPU:0, one launch (start us, length us, event | category | flops | bytes accessed | tf_op | source)
XLA Modules:
  0.0 840.9 jit_solution(802374251777481153)
XLA Ops:
  4.3 18.3 %all_to_all.140 = bf16[4,16,64,128]{3,2,1,0:T(8,128)(2,1)} all-to-all(bf16[4,16,64,128]{3,2,1,0:T(8,128)(2,1)S(1)} %get-tuple-element.127.state_ref), channel_id=1, replica_groups=mesh['lon'=16,'lat'=2] {'lat'}, dimensions={0} | all-to-all | bytes 2097152 | tf_op jit(solution)/shard_map/all_to_all | solution.py:182
  29.4 10.2 %all-to-all-done = bf16[4,16,64,128]{3,2,1,0:T(8,128)(2,1)S(1)} async-done(((bf16[4,16,64,128]{3,2,1,0:T(8,128)(2,1)}), bf16[4,16,64,128]{3,2,1,0:T(8,128)(2,1)S(1)}, u32[]{:S(2)}, u32[]{:S(2)}) %all-to-all-start) | async-done | bytes 1048608 | tf_op jit(solution)/shard_map/all_to_all | solution.py:182
  39.6 5.8 all-to-all-start.9
  48.5 14.5 %all-to-all-done.9.x_ref = bf16[16,11,16,128]{3,2,1,0:T(8,128)(2,1)S(1)} async-done(((bf16[16,11,16,128]{3,2,1,0:T(8,128)(2,1)}), bf16[16,11,16,128]{3,2,1,0:T(8,128)(2,1)S(1)}, u32[]{:S(2)}, u32[]{:S(2)}) %all-to-all-start.9) | async-done | bytes 720928 | tf_op jit(solution)/shard_map/all_to_all | solution.py:184
  63.0 5.1 all-to-all-start.1
  70.9 14.9 %all-to-all-done.1.x_ref = bf16[16,11,16,128]{3,2,1,0:T(8,128)(2,1)S(1)} async-done(((bf16[16,11,16,128]{3,2,1,0:T(8,128)(2,1)}), bf16[16,11,16,128]{3,2,1,0:T(8,128)(2,1)S(1)}, u32[]{:S(2)}, u32[]{:S(2)}) %all-to-all-start.1) | async-done | bytes 720928 | tf_op jit(solution)/shard_map/all_to_all | solution.py:184
  85.8 5.2 all-to-all-start.10
  99.3 9.4 %all-to-all-done.10.x_ref = bf16[16,11,16,128]{3,2,1,0:T(8,128)(2,1)} async-done(((bf16[16,11,16,128]{3,2,1,0:T(8,128)(2,1)}), bf16[16,11,16,128]{3,2,1,0:T(8,128)(2,1)}, u32[]{:S(2)}, u32[]{:S(2)}) %all-to-all-start.10) | async-done | bytes 720928 | tf_op jit(solution)/shard_map/all_to_all | solution.py:186
  108.7 5.2 all-to-all-start.2
  118.2 3.7 select_select_fusion
  125.3 6.3 all-to-all-done.2.x_ref
  131.6 4.4 all-to-all-start.11
  142.4 8.6 %all-to-all-done.11 = bf16[2,2,17,64,128]{4,3,2,1,0:T(8,128)(2,1)} async-done(((bf16[2,2,17,64,128]{4,3,2,1,0:T(8,128)(2,1)}), bf16[2,2,17,64,128]{4,3,2,1,0:T(8,128)(2,1)}, u32[]{:S(2)}, u32[]{:S(2)}) %all-to-all-start.11) | async-done | bytes 1114144 | tf_op jit(solution)/shard_map/all_to_all | solution.py:188
  151.0 4.4 all-to-all-start.3
  160.3 9.3 %all-to-all-done.3 = bf16[2,2,17,64,128]{4,3,2,1,0:T(8,128)(2,1)} async-done(((bf16[2,2,17,64,128]{4,3,2,1,0:T(8,128)(2,1)}), bf16[2,2,17,64,128]{4,3,2,1,0:T(8,128)(2,1)}, u32[]{:S(2)}, u32[]{:S(2)}) %all-to-all-start.3) | async-done | bytes 1114144 | tf_op jit(solution)/shard_map/all_to_all | solution.py:188
  173.3 4.7 collective-permute-start.7
  182.0 13.6 %forward.3 = (f32[4,16,64,128]{3,2,1,0:T(8,128)}, bf16[4,16,64,128]{3,2,1,0:T(8,128)(2,1)}, f32[4,1024,256]{2,1,0:T(8,128)}, f32[4,1024,256]{2,1,0:T(8,128)}) custom-call(bf16[4,16,64,128]{3,2,1,0:T(8,128)(2,1)} %copy-done.9, bf16[4,17,64,128]{3,2,1,0:T(8,128)(2,1)} %copy.138.s_ref, bf16[4,16,128]{2,1,0:T(8,128)(2,1)} %copy.139.row_ref, ...), custom_call_target="tpu_custom_call" | custom-call | flops 3489660928 | bytes 30000000 | tf_op jit(solution)/shard_map/forward/pallas_call | solution.py:423
  195.6 3.6 all-to-all-start.12
  199.4 4.5 collective-permute-start.2
  207.0 13.6 %forward.2 = (f32[4,16,64,128]{3,2,1,0:T(8,128)}, bf16[4,16,64,128]{3,2,1,0:T(8,128)(2,1)}, f32[4,1024,256]{2,1,0:T(8,128)}, f32[4,1024,256]{2,1,0:T(8,128)}) custom-call(bf16[4,16,64,128]{3,2,1,0:T(8,128)(2,1)} %get-tuple-element.128.state_ref, bf16[4,17,64,128]{3,2,1,0:T(8,128)(2,1)} %copy.113.s_ref, bf16[4,16,128]{2,1,0:T(8,128)(2,1)} %copy.114.row_ref, ...), custom_call_target="tpu_custom_call" | custom-call | flops 3489660928 | bytes 30000000 | tf_op jit(solution)/shard_map/forward/pallas_call | solution.py:423
  220.7 3.6 all-to-all-start.4
  227.5 7.7 all-to-all-done.4
  235.2 4.4 all-to-all-start.13
  242.7 14.5 %all-to-all-done.13.x_ref = bf16[16,11,16,128]{3,2,1,0:T(8,128)(2,1)S(1)} async-done(((bf16[16,11,16,128]{3,2,1,0:T(8,128)(2,1)}), bf16[16,11,16,128]{3,2,1,0:T(8,128)(2,1)S(1)}, u32[]{:S(2)}, u32[]{:S(2)}) %all-to-all-start.13) | async-done | bytes 720928 | tf_op jit(solution)/shard_map/all_to_all | solution.py:184
  257.2 5.1 all-to-all-start.5
  265.0 15.0 %all-to-all-done.5.x_ref = bf16[16,11,16,128]{3,2,1,0:T(8,128)(2,1)S(1)} async-done(((bf16[16,11,16,128]{3,2,1,0:T(8,128)(2,1)}), bf16[16,11,16,128]{3,2,1,0:T(8,128)(2,1)S(1)}, u32[]{:S(2)}, u32[]{:S(2)}) %all-to-all-start.5) | async-done | bytes 720928 | tf_op jit(solution)/shard_map/all_to_all | solution.py:184
  280.0 5.1 all-to-all-start.14
  287.8 15.0 %all-to-all-done.14.x_ref = bf16[16,11,16,128]{3,2,1,0:T(8,128)(2,1)S(1)} async-done(((bf16[16,11,16,128]{3,2,1,0:T(8,128)(2,1)}), bf16[16,11,16,128]{3,2,1,0:T(8,128)(2,1)S(1)}, u32[]{:S(2)}, u32[]{:S(2)}) %all-to-all-start.14) | async-done | bytes 720928 | tf_op jit(solution)/shard_map/all_to_all | solution.py:186
  302.8 5.1 all-to-all-start.6
  312.3 13.3 %all-to-all-done.6.x_ref = bf16[16,11,16,128]{3,2,1,0:T(8,128)(2,1)S(1)} async-done(((bf16[16,11,16,128]{3,2,1,0:T(8,128)(2,1)}), bf16[16,11,16,128]{3,2,1,0:T(8,128)(2,1)S(1)}, u32[]{:S(2)}, u32[]{:S(2)}) %all-to-all-start.6) | async-done | bytes 720928 | tf_op jit(solution)/shard_map/all_to_all | solution.py:186
  325.6 4.9 all-to-all-start.15
  345.8 4.4 all-to-all-start.7
  355.9 4.3 copy.122
  382.8 28.1 %turn.3 = (f32[4,16,64,128]{3,2,1,0:T(8,128)}, f32[4,2,64,128]{3,2,1,0:T(8,128)}, f32[4,18,128]{2,1,0:T(8,128)}, f32[1544,256]{1,0:T(8,128)}) custom-call(f32[4,16,64,128]{3,2,1,0:T(8,128)} %get-tuple-element.49.state_ref, bf16[4,17,64,128]{3,2,1,0:T(8,128)(2,1)} %copy.150.s_ref, f32[4,16,128]{2,1,0:T(8,128)} %copy.151.row_ref, ...), custom_call_target="tpu_custom_call" | custom-call | flops 10468982784 | bytes 30000000 | tf_op jit(solution)/shard_map/turn/pallas_call | solution.py:466
  412.6 28.2 %turn.2 = (f32[4,16,64,128]{3,2,1,0:T(8,128)}, f32[4,2,64,128]{3,2,1,0:T(8,128)}, f32[4,18,128]{2,1,0:T(8,128)}, f32[1544,256]{1,0:T(8,128)}) custom-call(f32[4,16,64,128]{3,2,1,0:T(8,128)} %get-tuple-element.46.state_ref, bf16[4,17,64,128]{3,2,1,0:T(8,128)(2,1)} %copy.126.s_ref, f32[4,16,128]{2,1,0:T(8,128)} %copy.127.row_ref, ...), custom_call_target="tpu_custom_call" | custom-call | flops 10468982784 | bytes 30000000 | tf_op jit(solution)/shard_map/turn/pallas_call | solution.py:466
  449.0 4.4 collective-permute-start.13
  456.1 4.6 collective-permute-done.12
  460.7 4.7 fusion.44
  465.4 12.9 %all_to_all.141 = bf16[4,16,64,128]{3,2,1,0:T(8,128)(2,1)} all-to-all(bf16[4,16,64,128]{3,2,1,0:T(8,128)(2,1)S(1)} %get-tuple-element.175), channel_id=1, replica_groups=mesh['lon'=16,'lat'=2] {'lat'}, dimensions={0} | all-to-all | bytes 2097152 | tf_op jit(solution)/shard_map/all_to_all | solution.py:182
  478.3 3.6 all-to-all-start.22
  485.0 6.2 all-to-all-done.22
  491.3 4.0 all-to-all-start.19
  498.4 14.5 %all-to-all-done.19.x_ref = bf16[16,11,16,128]{3,2,1,0:T(8,128)(2,1)S(1)} async-done(((bf16[16,11,16,128]{3,2,1,0:T(8,128)(2,1)}), bf16[16,11,16,128]{3,2,1,0:T(8,128)(2,1)S(1)}, u32[]{:S(2)}, u32[]{:S(2)}) %all-to-all-start.19) | async-done | bytes 720928 | tf_op jit(solution)/shard_map/all_to_all | solution.py:184
  512.9 5.1 all-to-all-start.23
  520.6 15.0 %all-to-all-done.23.x_ref = bf16[16,11,16,128]{3,2,1,0:T(8,128)(2,1)S(1)} async-done(((bf16[16,11,16,128]{3,2,1,0:T(8,128)(2,1)}), bf16[16,11,16,128]{3,2,1,0:T(8,128)(2,1)S(1)}, u32[]{:S(2)}, u32[]{:S(2)}) %all-to-all-start.23) | async-done | bytes 720928 | tf_op jit(solution)/shard_map/all_to_all | solution.py:184
  535.7 5.1 all-to-all-start.20
  543.4 15.0 %all-to-all-done.20.x_ref = bf16[16,11,16,128]{3,2,1,0:T(8,128)(2,1)S(1)} async-done(((bf16[16,11,16,128]{3,2,1,0:T(8,128)(2,1)}), bf16[16,11,16,128]{3,2,1,0:T(8,128)(2,1)S(1)}, u32[]{:S(2)}, u32[]{:S(2)}) %all-to-all-start.20) | async-done | bytes 720928 | tf_op jit(solution)/shard_map/all_to_all | solution.py:186
  558.5 5.1 all-to-all-start.24
  566.9 14.3 %all-to-all-done.24.x_ref = bf16[16,11,16,128]{3,2,1,0:T(8,128)(2,1)S(1)} async-done(((bf16[16,11,16,128]{3,2,1,0:T(8,128)(2,1)}), bf16[16,11,16,128]{3,2,1,0:T(8,128)(2,1)S(1)}, u32[]{:S(2)}, u32[]{:S(2)}) %all-to-all-start.24) | async-done | bytes 720928 | tf_op jit(solution)/shard_map/all_to_all | solution.py:186
  581.2 4.4 all-to-all-start.21
  589.1 10.9 %all-to-all-done.21 = bf16[2,2,16,64,128]{4,3,2,1,0:T(8,128)(2,1)} async-done(((bf16[2,2,16,64,128]{4,3,2,1,0:T(8,128)(2,1)}), bf16[2,2,16,64,128]{4,3,2,1,0:T(8,128)(2,1)}, u32[]{:S(2)}, u32[]{:S(2)}) %all-to-all-start.21) | async-done | bytes 1048608 | tf_op jit(solution)/shard_map/all_to_all | solution.py:188
  599.9 3.6 all-to-all-start.25
  606.5 10.4 %all-to-all-done.25 = bf16[2,2,16,64,128]{4,3,2,1,0:T(8,128)(2,1)S(1)} async-done(((bf16[2,2,16,64,128]{4,3,2,1,0:T(8,128)(2,1)}), bf16[2,2,16,64,128]{4,3,2,1,0:T(8,128)(2,1)S(1)}, u32[]{:S(2)}, u32[]{:S(2)}) %all-to-all-start.25) | async-done | bytes 1048608 | tf_op jit(solution)/shard_map/all_to_all | solution.py:188
  617.8 4.6 all-to-all-start.16
  623.1 14.5 %bottom.2 = f32[1544,256]{1,0:T(8,128)} custom-call(bf16[4,16,64,128]{3,2,1,0:T(8,128)(2,1)} %get-tuple-element.128.state_ref, bf16[4,17,64,128]{3,2,1,0:T(8,128)(2,1)} %copy.113.s_ref, bf16[4,16,128]{2,1,0:T(8,128)(2,1)} %copy.114.row_ref, bf16[4,65,128]{2,1,0:T(8,128)(2,1)} %copy.115.lo_ref, bf16[4,65,128]{2,1,0:T(8,128)(2,1)} %copy.116.hi_ref, ...), custom_call_target="tpu_custom_call" | custom-call | flops 5234491392 | bytes 30000000 | tf_op jit(solution)/shard_map/bottom/pallas_call | solution.py:511
  637.7 14.7 %bottom.3 = f32[1544,256]{1,0:T(8,128)} custom-call(bf16[4,16,64,128]{3,2,1,0:T(8,128)(2,1)} %copy-done.9, bf16[4,17,64,128]{3,2,1,0:T(8,128)(2,1)} %copy.138.s_ref, bf16[4,16,128]{2,1,0:T(8,128)(2,1)} %copy.139.row_ref, bf16[4,65,128]{2,1,0:T(8,128)(2,1)} %copy.140.lo_ref, bf16[4,65,128]{2,1,0:T(8,128)(2,1)} %copy-done.76, ...), custom_call_target="tpu_custom_call" | custom-call | flops 5234491392 | bytes 30000000 | tf_op jit(solution)/shard_map/bottom/pallas_call | solution.py:511
  656.0 9.5 %all-to-all-done.16 = f32[32,56,256]{2,1,0:T(8,128)S(1)} async-done(((f32[32,56,256]{2,1,0:T(8,128)}), f32[32,56,256]{2,1,0:T(8,128)S(1)}, u32[]{:S(2)}, u32[]{:S(2)}) %all-to-all-start.16) | async-done | bytes 1835040 | tf_op jit(solution)/shard_map/all_to_all | solution.py:567
  665.6 3.8 all-to-all-start.26
  669.5 43.0 %all-to-all-done.26 = f32[32,56,256]{2,1,0:T(8,128)} async-done(((f32[32,56,256]{2,1,0:T(8,128)}), f32[32,56,256]{2,1,0:T(8,128)}, u32[]{:S(2)}, u32[]{:S(2)}) %all-to-all-start.26) | async-done | bytes 1835040 | tf_op jit(solution)/shard_map/all_to_all | solution.py:567
  713.8 3.7 all-to-all-start.17
  719.1 41.5 %all-to-all-done.17 = f32[32,56,256]{2,1,0:T(8,128)S(1)} async-done(((f32[32,56,256]{2,1,0:T(8,128)}), f32[32,56,256]{2,1,0:T(8,128)S(1)}, u32[]{:S(2)}, u32[]{:S(2)}) %all-to-all-start.17) | async-done | bytes 1835040 | tf_op jit(solution)/shard_map/all_to_all | solution.py:570
  761.9 3.8 all-to-all-start.27
  769.5 39.3 %all-to-all-done.27 = f32[32,56,256]{2,1,0:T(8,128)} async-done(((f32[32,56,256]{2,1,0:T(8,128)}), f32[32,56,256]{2,1,0:T(8,128)}, u32[]{:S(2)}, u32[]{:S(2)}) %all-to-all-start.27) | async-done | bytes 1835040 | tf_op jit(solution)/shard_map/all_to_all | solution.py:570
  827.9 5.4 fusion.43
  (339 shorter events, 186.6 us)
Async XLA Ops:
  22.7 16.9 %all-to-all-start = ((bf16[4,16,64,128]{3,2,1,0:T(8,128)(2,1)}), bf16[4,16,64,128]{3,2,1,0:T(8,128)(2,1)S(1)}, u32[]{:S(2)}, u32[]{:S(2)}) async-start(bf16[4,16,64,128]{3,2,1,0:T(8,128)(2,1)} %get-tuple-element.128.state_ref), calls=%async_computation | async-start | bytes 2097152 | tf_op jit(solution)/shard_map/all_to_all | solution.py:182
  39.6 23.5 %all-to-all-start.9 = ((bf16[16,11,16,128]{3,2,1,0:T(8,128)(2,1)}), bf16[16,11,16,128]{3,2,1,0:T(8,128)(2,1)S(1)}, u32[]{:S(2)}, u32[]{:S(2)}) async-start(bf16[16,11,16,128]{3,2,1,0:T(8,128)(2,1)} %legendre.8), calls=%async_computation.9 | async-start | bytes 1441792 | tf_op jit(solution)/shard_map/all_to_all | solution.py:184
  63.0 22.8 %all-to-all-start.1 = ((bf16[16,11,16,128]{3,2,1,0:T(8,128)(2,1)}), bf16[16,11,16,128]{3,2,1,0:T(8,128)(2,1)S(1)}, u32[]{:S(2)}, u32[]{:S(2)}) async-start(bf16[16,11,16,128]{3,2,1,0:T(8,128)(2,1)} %legendre.6), calls=%async_computation.1 | async-start | bytes 1441792 | tf_op jit(solution)/shard_map/all_to_all | solution.py:184
  68.2 24.9 %copy-start.41 = (s32[8,16,64]{2,1,0:T(8,128)S(1)}, s32[8,16,64]{2,1,0:T(8,128)}, u32[]{:S(2)}) copy-start(s32[8,16,64]{2,1,0:T(8,128)} %param.28) | copy-start | bytes 98308
  68.2 25.0 %copy-start.51 = (s32[8,16,64]{2,1,0:T(8,128)S(1)}, s32[8,16,64]{2,1,0:T(8,128)}, u32[]{:S(2)}) copy-start(s32[8,16,64]{2,1,0:T(8,128)} %param.27) | copy-start | bytes 98308
  68.2 25.0 %copy-start.52 = (bf16[8,16,64]{2,1,0:T(8,128)(2,1)S(1)}, bf16[8,16,64]{2,1,0:T(8,128)(2,1)}, u32[]{:S(2)}) copy-start(bf16[8,16,64]{2,1,0:T(8,128)(2,1)} %param.26) | copy-start | bytes 49156
  68.2 25.7 %copy-start.38 = (f32[2,256,128]{2,1,0:T(8,128)S(1)}, f32[2,256,128]{2,1,0:T(8,128)}, u32[]{:S(2)}) copy-start(f32[2,256,128]{2,1,0:T(8,128)} %param.31) | copy-start | bytes 786436
  68.2 25.9 %copy-start.53 = (f32[2,896]{1,0:T(2,128)S(1)}, f32[2,896]{1,0:T(2,128)}, u32[]{:S(2)}) copy-start(f32[2,896]{1,0:T(2,128)} %param.32) | copy-start | bytes 21508
  85.8 22.9 %all-to-all-start.10 = ((bf16[16,11,16,128]{3,2,1,0:T(8,128)(2,1)}), bf16[16,11,16,128]{3,2,1,0:T(8,128)(2,1)}, u32[]{:S(2)}, u32[]{:S(2)}) async-start(bf16[16,11,16,128]{3,2,1,0:T(8,128)(2,1)} %zonal.8), calls=%async_computation.10 | async-start | bytes 1441792 | tf_op jit(solution)/shard_map/all_to_all | solution.py:186
  92.8 64.4 %collective-permute-start = (bf16[8,16,128]{2,0,1:T(8,128)(2,1)}, bf16[8,16,128]{2,0,1:T(8,128)(2,1)}, u32[]{:S(2)}, u32[]{:S(2)}) collective-permute-start(bf16[8,16,128]{2,0,1:T(8,128)(2,1)} %fusion.21), channel_id=1, source_target_pairs={{0,1},{1,0},{2,3},{3,2},{4,5},{5,4},{6,7},{7,6},{8,9},{9,8},{10,11... | collective-permute-start | bytes 98312 | tf_op jit(solution)/shard_map/ppermute | solution.py:614
  94.1 22.2 %copy-start.24 = (f32[2,256,128]{1,2,0:T(8,128)}, f32[2,256,128]{1,2,0:T(8,128)S(1)}, u32[]{:S(2)}) copy-start(f32[2,256,128]{1,2,0:T(8,128)S(1)} %copy.112) | copy-start | bytes 786436
  96.5 21.5 %copy-start.3 = (f32[2,9,128,256]{3,2,1,0:T(8,128)S(1)}, f32[2,9,128,256]{3,2,1,0:T(8,128)}, u32[]{:S(2)}) copy-start(f32[2,9,128,256]{3,2,1,0:T(8,128)} %param.29) | copy-start | bytes 7077892
  108.7 22.9 %all-to-all-start.2 = ((bf16[16,11,16,128]{3,2,1,0:T(8,128)(2,1)}), bf16[16,11,16,128]{3,2,1,0:T(8,128)(2,1)}, u32[]{:S(2)}, u32[]{:S(2)}) async-start(bf16[16,11,16,128]{3,2,1,0:T(8,128)(2,1)} %zonal.6), calls=%async_computation.2 | async-start | bytes 1441792 | tf_op jit(solution)/shard_map/all_to_all | solution.py:186
  131.6 19.4 %all-to-all-start.11 = ((bf16[2,2,17,64,128]{4,3,2,1,0:T(8,128)(2,1)}), bf16[2,2,17,64,128]{4,3,2,1,0:T(8,128)(2,1)}, u32[]{:S(2)}, u32[]{:S(2)}) async-start(bf16[2,2,17,64,128]{4,3,2,1,0:T(8,128)(2,1)} %synthesis.8), calls=%async_computation.11 | async-start | bytes 2228224 | tf_op jit(solution)/shard_map/all_to_all | solution.py:188
  139.1 16.4 %copy-start.35 = (bf16[1,256,256]{2,1,0:T(8,128)(2,1)S(1)}, bf16[1,256,256]{2,1,0:T(8,128)(2,1)}, u32[]{:S(2)}) copy-start(bf16[1,256,256]{2,1,0:T(8,128)(2,1)} %get-tuple-element.143) | copy-start | bytes 393220
  139.1 17.3 %copy-start.44 = (bf16[256,128]{0,1:T(8,128)(2,1)S(1)}, bf16[256,128]{0,1:T(8,128)(2,1)}, u32[]{:S(2)}) copy-start(bf16[256,128]{0,1:T(8,128)(2,1)} %get-tuple-element.149) | copy-start | bytes 196612
  151.0 18.6 %all-to-all-start.3 = ((bf16[2,2,17,64,128]{4,3,2,1,0:T(8,128)(2,1)}), bf16[2,2,17,64,128]{4,3,2,1,0:T(8,128)(2,1)}, u32[]{:S(2)}, u32[]{:S(2)}) async-start(bf16[2,2,17,64,128]{4,3,2,1,0:T(8,128)(2,1)} %synthesis.6), calls=%async_computation.3 | async-start | bytes 2228224 | tf_op jit(solution)/shard_map/all_to_all | solution.py:188
  173.2 7.6 collective-permute-start.6
  173.3 8.1 collective-permute-start.7
  195.6 25.0 %all-to-all-start.12 = ((bf16[4,16,64,128]{3,2,1,0:T(8,128)(2,1)}), bf16[4,16,64,128]{3,2,1,0:T(8,128)(2,1)S(1)}, u32[]{:S(2)}, u32[]{:S(2)}) async-start(bf16[4,16,64,128]{3,2,1,0:T(8,128)(2,1)} %get-tuple-element.50), calls=%async_computation.12 | async-start | bytes 2097152 | tf_op jit(solution)/shard_map/all_to_all | solution.py:182
  199.3 6.5 collective-permute-start.1
  199.4 7.0 collective-permute-start.2
  220.7 14.5 %all-to-all-start.4 = ((bf16[4,16,64,128]{3,2,1,0:T(8,128)(2,1)}), bf16[4,16,64,128]{3,2,1,0:T(8,128)(2,1)S(1)}, u32[]{:S(2)}, u32[]{:S(2)}) async-start(bf16[4,16,64,128]{3,2,1,0:T(8,128)(2,1)} %get-tuple-element.47), calls=%async_computation.4 | async-start | bytes 2097152 | tf_op jit(solution)/shard_map/all_to_all | solution.py:182
  235.2 22.1 %all-to-all-start.13 = ((bf16[16,11,16,128]{3,2,1,0:T(8,128)(2,1)}), bf16[16,11,16,128]{3,2,1,0:T(8,128)(2,1)S(1)}, u32[]{:S(2)}, u32[]{:S(2)}) async-start(bf16[16,11,16,128]{3,2,1,0:T(8,128)(2,1)} %legendre.9), calls=%async_computation.13 | async-start | bytes 1441792 | tf_op jit(solution)/shard_map/all_to_all | solution.py:184
  257.2 22.8 %all-to-all-start.5 = ((bf16[16,11,16,128]{3,2,1,0:T(8,128)(2,1)}), bf16[16,11,16,128]{3,2,1,0:T(8,128)(2,1)S(1)}, u32[]{:S(2)}, u32[]{:S(2)}) async-start(bf16[16,11,16,128]{3,2,1,0:T(8,128)(2,1)} %legendre.7), calls=%async_computation.5 | async-start | bytes 1441792 | tf_op jit(solution)/shard_map/all_to_all | solution.py:184
  265.0 43.0 %copy-start.73 = (f32[128]{0:T(128)S(1)}, f32[128]{0:T(128)}, u32[]{:S(2)}) copy-start(f32[128]{0:T(128)} %get-tuple-element.173) | copy-start | bytes 1540
  265.0 43.0 %copy-start.58 = (bf16[1,256]{1,0:T(2,128)(2,1)S(1)}, bf16[1,256]{1,0:T(2,128)(2,1)}, u32[]{:S(2)}) copy-start(bf16[1,256]{1,0:T(2,128)(2,1)} %get-tuple-element.160) | copy-start | bytes 1540
  265.0 43.0 %copy-start.59 = (bf16[1,256]{1,0:T(2,128)(2,1)S(1)}, bf16[1,256]{1,0:T(2,128)(2,1)}, u32[]{:S(2)}) copy-start(bf16[1,256]{1,0:T(2,128)(2,1)} %get-tuple-element.161) | copy-start | bytes 1540
  265.0 43.0 %copy-start.60 = (bf16[1,256]{1,0:T(2,128)(2,1)S(1)}, bf16[1,256]{1,0:T(2,128)(2,1)}, u32[]{:S(2)}) copy-start(bf16[1,256]{1,0:T(2,128)(2,1)} %get-tuple-element.166) | copy-start | bytes 1540
  265.0 43.0 %copy-start.61 = (bf16[1,256]{1,0:T(2,128)(2,1)S(1)}, bf16[1,256]{1,0:T(2,128)(2,1)}, u32[]{:S(2)}) copy-start(bf16[1,256]{1,0:T(2,128)(2,1)} %get-tuple-element.167) | copy-start | bytes 1540
  265.0 43.0 %copy-start.62 = (bf16[1,256]{1,0:T(2,128)(2,1)S(1)}, bf16[1,256]{1,0:T(2,128)(2,1)}, u32[]{:S(2)}) copy-start(bf16[1,256]{1,0:T(2,128)(2,1)} %get-tuple-element.168) | copy-start | bytes 1540
  265.0 43.0 %copy-start.63 = (bf16[1,256]{1,0:T(2,128)(2,1)S(1)}, bf16[1,256]{1,0:T(2,128)(2,1)}, u32[]{:S(2)}) copy-start(bf16[1,256]{1,0:T(2,128)(2,1)} %get-tuple-element.169) | copy-start | bytes 1540
  280.0 22.8 %all-to-all-start.14 = ((bf16[16,11,16,128]{3,2,1,0:T(8,128)(2,1)}), bf16[16,11,16,128]{3,2,1,0:T(8,128)(2,1)S(1)}, u32[]{:S(2)}, u32[]{:S(2)}) async-start(bf16[16,11,16,128]{3,2,1,0:T(8,128)(2,1)} %zonal.9), calls=%async_computation.14 | async-start | bytes 1441792 | tf_op jit(solution)/shard_map/all_to_all | solution.py:186
  302.8 22.8 %all-to-all-start.6 = ((bf16[16,11,16,128]{3,2,1,0:T(8,128)(2,1)}), bf16[16,11,16,128]{3,2,1,0:T(8,128)(2,1)S(1)}, u32[]{:S(2)}, u32[]{:S(2)}) async-start(bf16[16,11,16,128]{3,2,1,0:T(8,128)(2,1)} %zonal.7), calls=%async_computation.6 | async-start | bytes 1441792 | tf_op jit(solution)/shard_map/all_to_all | solution.py:186
  309.0 21.5 %copy-start.70 = (f32[1,256]{1,0:T(1,128)S(1)}, f32[1,256]{1,0:T(1,128)}, u32[]{:S(2)}) copy-start(f32[1,256]{1,0:T(1,128)} %get-tuple-element.159) | copy-start | bytes 3076
  312.3 18.8 %copy-start.21 = (bf16[8,16,64,128]{3,2,1,0:T(8,128)(2,1)S(1)}, bf16[8,16,64,128]{3,2,1,0:T(8,128)(2,1)}, u32[]{:S(2)}) copy-start(bf16[8,16,64,128]{3,2,1,0:T(8,128)(2,1)} %param.25) | copy-start | bytes 6291460
  325.6 20.2 %all-to-all-start.15 = ((bf16[2,2,17,64,128]{4,3,2,1,0:T(8,128)(2,1)}), bf16[2,2,17,64,128]{4,3,2,1,0:T(8,128)(2,1)}, u32[]{:S(2)}, u32[]{:S(2)}) async-start(bf16[2,2,17,64,128]{4,3,2,1,0:T(8,128)(2,1)} %synthesis.9), calls=%async_computation.15 | async-start | bytes 2228224 | tf_op jit(solution)/shard_map/all_to_all | solution.py:188
  334.8 28.1 %collective-permute-start.3 = (f32[4,16,128]{2,0,1:T(4,128)S(1)}, f32[4,16,128]{2,0,1:T(4,128)S(1)}, u32[]{:S(2)}, u32[]{:S(2)}) collective-permute-start(f32[4,16,128]{2,0,1:T(4,128)S(1)} %fusion.20), channel_id=1, source_target_pairs={{0,1},{1,0},{2,3},{3,2},{4,5},{5,4},{6,7},{7,6},{8,9},{9,8},{10,11... | collective-permute-start | bytes 98312 | tf_op jit(solution)/shard_map/ppermute | solution.py:624
  345.8 23.2 %all-to-all-start.7 = ((bf16[2,2,17,64,128]{4,3,2,1,0:T(8,128)(2,1)}), bf16[2,2,17,64,128]{4,3,2,1,0:T(8,128)(2,1)}, u32[]{:S(2)}, u32[]{:S(2)}) async-start(bf16[2,2,17,64,128]{4,3,2,1,0:T(8,128)(2,1)} %synthesis.7), calls=%async_computation.7 | async-start | bytes 2228224 | tf_op jit(solution)/shard_map/all_to_all | solution.py:188
  351.0 13.6 %collective-permute-start.8 = (f32[4,16,128]{2,0,1:T(4,128)S(1)}, f32[4,16,128]{2,0,1:T(4,128)S(1)}, u32[]{:S(2)}, u32[]{:S(2)}) collective-permute-start(f32[4,16,128]{2,0,1:T(4,128)S(1)} %fusion.19), channel_id=1, source_target_pairs={{0,1},{1,0},{2,3},{3,2},{4,5},{5,4},{6,7},{7,6},{8,9},{9,8},{10,11... | collective-permute-start | bytes 98312 | tf_op jit(solution)/shard_map/ppermute | solution.py:624
  373.9 37.5 %collective-permute-start.4 = (bf16[4,65,128]{2,0,1:T(4,128)(2,1)S(1)}, bf16[4,65,128]{2,0,1:T(4,128)(2,1)S(1)}, u32[]{:S(2)}, u32[]{:S(2)}) collective-permute-start(bf16[4,65,128]{2,0,1:T(4,128)(2,1)S(1)} %pad_maximum_fusion.4), channel_id=1, source_target_pairs={{0,2},{2,4},{4,6},{6,8},{8,10},{10,12},{12,14},{14,16},{16,18},{18... | collective-permute-start | bytes 199688 | tf_op jit(solution)/shard_map/ppermute | solution.py:610
  375.0 6.5 collective-permute-start.9
  377.3 4.8 collective-permute-start.10
  379.7 32.3 %collective-permute-start.5 = (bf16[4,65,128]{2,0,1:T(4,128)(2,1)S(1)}, bf16[4,65,128]{2,0,1:T(4,128)(2,1)S(1)}, u32[]{:S(2)}, u32[]{:S(2)}) collective-permute-start(bf16[4,65,128]{2,0,1:T(4,128)(2,1)S(1)} %pad_maximum_fusion.5), channel_id=1, source_target_pairs={{2,0},{4,2},{6,4},{8,6},{10,8},{12,10},{14,12},{16,14},{18,16},{20... | collective-permute-start | bytes 199688 | tf_op jit(solution)/shard_map/ppermute | solution.py:611
  411.0 31.7 %collective-permute-start.14 = (f32[4,18,128]{2,1,0:T(8,128)}, f32[4,18,128]{2,1,0:T(8,128)S(1)}, u32[]{:S(2)}, u32[]{:S(2)}) collective-permute-start(f32[4,18,128]{2,1,0:T(8,128)} %get-tuple-element.60), channel_id=1, source_target_pairs={{0,1},{1,0},{2,3},{3,2},{4,5},{5,4},{6,7},{7,6},{8,9},{9,8},{10,11... | collective-permute-start | bytes 110600 | tf_op jit(solution)/shard_map/ppermute | solution.py:630
  412.6 32.6 %copy-start.45 = (f32[4,2,64,128]{3,2,1,0:T(8,128)S(1)}, f32[4,2,64,128]{3,2,1,0:T(8,128)}, u32[]{:S(2)}) copy-start(f32[4,2,64,128]{3,2,1,0:T(8,128)} %get-tuple-element.61) | copy-start | bytes 786436
  412.6 48.1 %copy-start.23 = (f32[4,16,64,128]{3,2,1,0:T(8,128)S(1)}, f32[4,16,64,128]{3,2,1,0:T(8,128)}, u32[]{:S(2)}) copy-start(f32[4,16,64,128]{3,2,1,0:T(8,128)} %get-tuple-element.59) | copy-start | bytes 6291460
  440.8 4.4 collective-permute-start.11
  446.3 7.3 collective-permute-start.16
  449.0 7.1 collective-permute-start.15
  449.0 7.1 collective-permute-start.13
  453.4 7.3 collective-permute-start.12
  478.3 13.0 %all-to-all-start.22 = ((bf16[4,16,64,128]{3,2,1,0:T(8,128)(2,1)}), bf16[4,16,64,128]{3,2,1,0:T(8,128)(2,1)S(1)}, u32[]{:S(2)}, u32[]{:S(2)}) async-start(bf16[4,16,64,128]{3,2,1,0:T(8,128)(2,1)} %get-tuple-element.109), calls=%async_computation.22 | async-start | bytes 2097152 | tf_op jit(solution)/shard_map/all_to_all | solution.py:182
  491.3 21.6 %all-to-all-start.19 = ((bf16[16,11,16,128]{3,2,1,0:T(8,128)(2,1)}), bf16[16,11,16,128]{3,2,1,0:T(8,128)(2,1)S(1)}, u32[]{:S(2)}, u32[]{:S(2)}) async-start(bf16[16,11,16,128]{3,2,1,0:T(8,128)(2,1)} %legendre.10), calls=%async_computation.19 | async-start | bytes 1441792 | tf_op jit(solution)/shard_map/all_to_all | solution.py:184
  512.9 22.8 %all-to-all-start.23 = ((bf16[16,11,16,128]{3,2,1,0:T(8,128)(2,1)}), bf16[16,11,16,128]{3,2,1,0:T(8,128)(2,1)S(1)}, u32[]{:S(2)}, u32[]{:S(2)}) async-start(bf16[16,11,16,128]{3,2,1,0:T(8,128)(2,1)} %legendre.11), calls=%async_computation.23 | async-start | bytes 1441792 | tf_op jit(solution)/shard_map/all_to_all | solution.py:184
  535.7 22.8 %all-to-all-start.20 = ((bf16[16,11,16,128]{3,2,1,0:T(8,128)(2,1)}), bf16[16,11,16,128]{3,2,1,0:T(8,128)(2,1)S(1)}, u32[]{:S(2)}, u32[]{:S(2)}) async-start(bf16[16,11,16,128]{3,2,1,0:T(8,128)(2,1)} %zonal.10), calls=%async_computation.20 | async-start | bytes 1441792 | tf_op jit(solution)/shard_map/all_to_all | solution.py:186
  558.5 22.8 %all-to-all-start.24 = ((bf16[16,11,16,128]{3,2,1,0:T(8,128)(2,1)}), bf16[16,11,16,128]{3,2,1,0:T(8,128)(2,1)S(1)}, u32[]{:S(2)}, u32[]{:S(2)}) async-start(bf16[16,11,16,128]{3,2,1,0:T(8,128)(2,1)} %zonal.11), calls=%async_computation.24 | async-start | bytes 1441792 | tf_op jit(solution)/shard_map/all_to_all | solution.py:186
  581.2 18.7 %all-to-all-start.21 = ((bf16[2,2,16,64,128]{4,3,2,1,0:T(8,128)(2,1)}), bf16[2,2,16,64,128]{4,3,2,1,0:T(8,128)(2,1)}, u32[]{:S(2)}, u32[]{:S(2)}) async-start(bf16[2,2,16,64,128]{4,3,2,1,0:T(8,128)(2,1)} %synthesis.10), calls=%async_computation.21 | async-start | bytes 2097152 | tf_op jit(solution)/shard_map/all_to_all | solution.py:188
  585.7 17.9 %copy-start.25 = (f32[1544,256]{1,0:T(8,128)S(1)}, f32[1544,256]{1,0:T(8,128)}, u32[]{:S(2)}) copy-start(f32[1544,256]{1,0:T(8,128)} %get-tuple-element.51) | copy-start | bytes 4743172
  599.9 16.9 %all-to-all-start.25 = ((bf16[2,2,16,64,128]{4,3,2,1,0:T(8,128)(2,1)}), bf16[2,2,16,64,128]{4,3,2,1,0:T(8,128)(2,1)S(1)}, u32[]{:S(2)}, u32[]{:S(2)}) async-start(bf16[2,2,16,64,128]{4,3,2,1,0:T(8,128)(2,1)} %synthesis.11), calls=%async_computation.25 | async-start | bytes 2097152 | tf_op jit(solution)/shard_map/all_to_all | solution.py:188
  617.8 47.7 %all-to-all-start.16 = ((f32[32,56,256]{2,1,0:T(8,128)}), f32[32,56,256]{2,1,0:T(8,128)S(1)}, u32[]{:S(2)}, u32[]{:S(2)}) async-start(f32[32,56,256]{2,1,0:T(8,128)} %bitcast.149), calls=%async_computation.16 | async-start | bytes 3670016 | tf_op jit(solution)/shard_map/all_to_all | solution.py:567
  665.6 46.9 %all-to-all-start.26 = ((f32[32,56,256]{2,1,0:T(8,128)}), f32[32,56,256]{2,1,0:T(8,128)}, u32[]{:S(2)}, u32[]{:S(2)}) async-start(f32[32,56,256]{2,1,0:T(8,128)} %bitcast.150), calls=%async_computation.26 | async-start | bytes 3670016 | tf_op jit(solution)/shard_map/all_to_all | solution.py:567
  713.8 46.8 %all-to-all-start.17 = ((f32[32,56,256]{2,1,0:T(8,128)}), f32[32,56,256]{2,1,0:T(8,128)S(1)}, u32[]{:S(2)}, u32[]{:S(2)}) async-start(f32[32,56,256]{2,1,0:T(8,128)} %broadcast_in_dim.223), calls=%async_computation.17 | async-start | bytes 3670016 | tf_op jit(solution)/shard_map/all_to_all | solution.py:570
  761.9 46.9 %all-to-all-start.27 = ((f32[32,56,256]{2,1,0:T(8,128)}), f32[32,56,256]{2,1,0:T(8,128)}, u32[]{:S(2)}, u32[]{:S(2)}) async-start(f32[32,56,256]{2,1,0:T(8,128)} %broadcast_in_dim.244), calls=%async_computation.27 | async-start | bytes 3670016 | tf_op jit(solution)/shard_map/all_to_all | solution.py:570
  (58 other events, 427.1 us)

commit v2 on v0

--- a/solution.py
+++ b/solution.py
@@ -1,8 +1,12 @@
+import functools
 import math
 
 import jax
 import jax.numpy as jnp
+import numpy as np
 from jax import lax
+from jax.experimental import pallas as pl
+from jax.experimental.pallas import tpu as pltpu
 from jax.sharding import PartitionSpec as P
 
 MW = 86
@@ -14,6 +18,923 @@
 MOMENTUM = 0.9
 AVERAGE = 0.99
 RATE_BASE = 0.0006
+
+F32 = jnp.float32
+BF16 = jnp.bfloat16
+CHUNK = 4
+VMEM = 56 * 1024 * 1024
+GELU_A = math.sqrt(2.0 / math.pi)
+GELU_B = 0.044715
+
+
+def split_table(table):
+    table = np.asarray(table, np.float32)
+    high = table.astype(BF16)
+    low = (table - high.astype(np.float32)).astype(BF16)
+    return np.concatenate([high, low], axis=0)
+
+
+def host_tables(nlon, nlat, deg):
+    kept = np.arange(2 * MW)
+    wave = np.where(kept < MW, kept, kept - MW + 1).astype(np.float64)
+    angle = 2.0 * np.pi * wave[:, None] * np.arange(nlon)[None, :] / nlon
+    fourier = np.where((kept < MW)[:, None], np.cos(angle), np.sin(angle)) * np.sqrt(2.0 / nlon)
+    zonal = (fourier * (1.0 - 0.5 * wave / MW)[:, None]).T @ fourier
+    phase = ((np.arange(nlat) + 0.5) / nlat - 0.5) * np.pi
+    sine, area = np.sin(phase), np.cos(phase)
+    polys = [np.ones_like(sine), sine]
+    for n in range(1, NDEG - 1):
+        polys.append(((2 * n + 1) * sine * polys[-1] - n * polys[-2]) / (n + 1))
+    degrees = np.arange(NDEG)
+    legendre = np.sqrt((2 * degrees + 1) / 2)[:, None] * np.sqrt(area * np.pi / nlat)[None, :]
+    legendre = legendre * np.stack(polys)
+    damping = 1.5 * (1.0 - 2.0 * degrees * (degrees + 1) / (NDEG * (NDEG + 1)))
+    forward = np.zeros((deg, nlat))
+    forward[:NDEG] = legendre
+    inverse = np.zeros((nlat, -(-deg // 32) * 32))
+    inverse[:, :NDEG] = (legendre * damping[:, None]).T
+    return split_table(zonal), split_table(forward), split_table(inverse), area
+
+
+def mm(a, b):
+    return jnp.dot(a, b, preferred_element_type=F32)
+
+
+def mm_rows(a, b):
+    return lax.dot_general(a, b, (((0,), (0,)), ((), ())), preferred_element_type=F32)
+
+
+def whole(shape):
+    return pl.BlockSpec(shape, lambda *_: (0,) * len(shape))
+
+
+def params():
+    return pltpu.CompilerParams(vmem_limit_bytes=VMEM)
+
+
+HALF = CHUNK // 2
+
+
+def any_spec():
+    return pl.BlockSpec(memory_space=pl.ANY)
+
+
+def shape_of(dims, dtype):
+    return jax.ShapeDtypeStruct(dims, dtype)
+
+
+def grid_of(count, in_specs, out_specs, scratch):
+    return pltpu.PrefetchScalarGridSpec(
+        num_scalar_prefetch=1,
+        grid=(count,),
+        in_specs=in_specs,
+        out_specs=out_specs,
+        scratch_shapes=scratch,
+    )
+
+
+def first_of(chunk, half, info):
+    if chunk is None:
+        return 0
+    return chunk * CHUNK + HALF * (info[0] if half == 0 else 1 - info[0])
+
+
+def snap_spec(dims, chunk=None, half=0):
+    return pl.BlockSpec(
+        (1,) + dims, lambda g, info: (first_of(chunk, half, info) + g,) + (0,) * len(dims)
+    )
+
+
+def legendre_kernel(wide, info, own_ref, other_ref, l_ref, dep_ref, o_ref, tmp):
+    parts, rows, lon_t, chans = o_ref.shape
+    lat_t = own_ref.shape[2]
+    deg = l_ref.shape[0] // 2
+    count = lon_t + 2 if wide else lon_t
+    each = deg // parts
+    place = lax.broadcasted_iota(jnp.int32, (lat_t, chans), 0)
+    south = info[0] == 1
+    inner = place == jnp.where(south, 0, lat_t - 1)
+    other_inner = place == jnp.where(south, lat_t - 1, 0)
+
+    def column(x):
+        own, other = own_ref[0, x], other_ref[0, x]
+        if wide:
+            to_own = other_ref[0, count, x : x + 1].astype(F32)
+            to_other = own_ref[0, count, x : x + 1].astype(F32)
+            own = (own.astype(F32) + jnp.where(inner, to_own, 0.0)).astype(BF16)
+            other = (other.astype(F32) + jnp.where(other_inner, to_other, 0.0)).astype(BF16)
+        return jnp.concatenate([own, other], axis=0)
+
+    for base in range(0, count, 4):
+        span = range(base, min(base + 4, count))
+        r = mm(l_ref[...], jnp.concatenate([column(x) for x in span], axis=1))
+        r = r[:deg] + r[deg:]
+        for x in span:
+            tmp[:, x, :] = r[:, (x - base) * chans : (x - base + 1) * chans]
+    o_ref[:, :each] = tmp[:, :lon_t, :].astype(BF16).reshape(parts, each, lon_t, chans)
+    if wide:
+        rest = jnp.zeros((lon_t - each, chans), F32)
+        for p in range(parts):
+            for side in range(2):
+                edge = tmp[p * each : (p + 1) * each, lon_t + side, :]
+                o_ref[p, each + side] = jnp.concatenate([edge, rest], axis=0).astype(BF16)
+
+
+def legendre_call(info, own, chunk, half, other, table, dep, wide):
+    snaps, slabs, lat_t, chans = other.shape
+    deg = table.shape[0] // 2
+    parts = 8
+    lon_t = slabs - 3 if wide else slabs
+    rows = deg // parts + (2 if wide else 0)
+    return pl.pallas_call(
+        functools.partial(legendre_kernel, wide),
+        grid_spec=grid_of(
+            snaps,
+            [
+                snap_spec(own.shape[1:], chunk, half),
+                snap_spec(other.shape[1:]),
+                whole(table.shape),
+                any_spec(),
+            ],
+            pl.BlockSpec((parts, rows, lon_t, chans), lambda s, info: (s, 0, 0, 0)),
+            [pltpu.VMEM((deg, lon_t + 8 if wide else lon_t, chans), F32)],
+        ),
+        out_shape=shape_of((snaps * parts, rows, lon_t, chans), BF16),
+        compiler_params=params(),
+        cost_estimate=cost(3.2),
+        name="legendre",
+    )(info, own, other, table, dep)
+
+
+def zonal_kernel(wide_in, x_ref, a_ref, dep_ref, o_ref, tmp):
+    groups, _, lon_t, chans = x_ref.shape
+    nlon = groups * lon_t
+    rows = min(x_ref.shape[1], o_ref.shape[1])
+    if wide_in:
+        for side in range(2):
+            tmp[side * groups : (side + 1) * groups] = x_ref[:, rows + side].astype(F32)
+    else:
+        tmp[...] = jnp.zeros_like(tmp)
+    for base in range(0, rows, 4):
+        span = range(base, min(base + 4, rows))
+        fields = jnp.concatenate([x_ref[:, n].reshape(nlon, chans) for n in span], axis=1)
+        if wide_in:
+            edges = jnp.concatenate([tmp[:, n, :] for n in span], axis=1).astype(BF16)
+            r = mm(a_ref[:, :nlon], fields) + mm(a_ref[:, nlon:], edges)
+            r = r[:nlon] + r[nlon:]
+        else:
+            r = mm(a_ref[...], fields)
+            size = r.shape[0] // 2
+            r = r[:size] + r[size:]
+        low = r[:nlon].astype(BF16)
+        for n in span:
+            lanes = slice((n - base) * chans, (n - base + 1) * chans)
+            o_ref[:, n] = low[:, lanes].reshape(groups, lon_t, chans)
+            if not wide_in:
+                tmp[:, n, :] = r[nlon:, lanes]
+    if not wide_in:
+        for side in range(2):
+            o_ref[:, rows + side] = tmp[side * groups : (side + 1) * groups].astype(BF16)
+
+
+def zonal_call(fields, table, dep, wide_in):
+    groups, rows, lon_t, chans = fields.shape
+    out = (groups, rows - 2 if wide_in else rows + 2, lon_t, chans)
+    return pl.pallas_call(
+        functools.partial(zonal_kernel, wide_in),
+        in_specs=[pl.BlockSpec(memory_space=pltpu.VMEM)] * 2 + [any_spec()],
+        out_specs=pl.BlockSpec(memory_space=pltpu.VMEM),
+        out_shape=shape_of(out, BF16),
+        scratch_shapes=[pltpu.VMEM((2 * groups, lon_t, chans), F32)],
+        compiler_params=params(),
+        cost_estimate=cost(2.8),
+        name="zonal",
+    )(fields, table, dep)
+
+
+def synthesis_kernel(wide, info, x_ref, l_ref, dep_ref, own_ref, send_ref, tmp):
+    parts, rows, lon_t, chans = x_ref.shape
+    each = rows - 2 if wide else rows
+    deg = parts * each
+    count = lon_t + 2 if wide else lon_t
+    nlat = l_ref.shape[0] // 2
+    half = nlat // 2
+    south = info[0] == 1
+    tmp[:deg, :lon_t, :] = x_ref[:, :each].reshape(deg, lon_t, chans).astype(F32)
+    if wide:
+        for p in range(parts):
+            for side in range(2):
+                tmp[p * each : (p + 1) * each, lon_t + side, :] = x_ref[p, each + side, :each].astype(F32)
+    tmp[deg:] = jnp.zeros((tmp.shape[0] - deg,) + tmp.shape[1:], F32)
+    for base in range(0, count, 4):
+        span = range(base, min(base + 4, count))
+        cols = jnp.concatenate([tmp[:, x, :] for x in span], axis=1).astype(BF16)
+        r = mm(l_ref[...], cols)
+        r = r[:nlat] + r[nlat:]
+        for x in span:
+            one = r[:, (x - base) * chans : (x - base + 1) * chans]
+            own_ref[0, x] = one[:half].astype(BF16)
+            send_ref[0, x] = one[half:].astype(BF16)
+            if wide:
+                tmp[0, x : x + 1, :] = jnp.where(south, one[2 * half - 1 :], one[half : half + 1])
+                tmp[1, x : x + 1, :] = jnp.where(south, one[:1], one[half - 1 : half])
+    if wide:
+        size = tmp.shape[1]
+        rest = jnp.zeros((half - size, chans), F32)
+        for h, ref in enumerate((own_ref, send_ref)):
+            ref[0, count] = jnp.concatenate([tmp[h], rest], axis=0).astype(BF16)
+
+
+def synthesis_call(info, coeffs, table, snaps, wide, dep):
+    total, rows, lon_t, chans = coeffs.shape
+    parts = total // snaps
+    nlat = table.shape[0] // 2
+    slabs = lon_t + 3 if wide else lon_t
+    out = snap_spec((slabs, nlat // 2, chans))
+    return pl.pallas_call(
+        functools.partial(synthesis_kernel, wide),
+        grid_spec=grid_of(
+            snaps,
+            [
+                pl.BlockSpec((parts, rows, lon_t, chans), lambda s, info: (s, 0, 0, 0)),
+                whole(table.shape),
+                any_spec(),
+            ],
+            [out, out],
+            [pltpu.VMEM((table.shape[1], lon_t + 8 if wide else lon_t, chans), F32)],
+        ),
+        out_shape=[shape_of((snaps, slabs, nlat // 2, chans), BF16)] * 2,
+        compiler_params=params(),
+        cost_estimate=cost(3.4),
+        name="synthesis",
+    )(info, coeffs, table, dep)
+
+
+def gelu_of(x):
+    t = jnp.tanh(x * (GELU_A + (GELU_A * GELU_B) * (x * x)))
+    return 0.5 * x * (1.0 + t)
+
+
+def gelu_and_slope(x):
+    sq = x * x
+    t = jnp.tanh(x * (GELU_A + (GELU_A * GELU_B) * sq))
+    cdf = 0.5 + 0.5 * t
+    slope = cdf + (0.5 * x) * (1.0 - t * t) * (GELU_A + (3.0 * GELU_A * GELU_B) * sq)
+    return x * cdf, slope
+
+
+def fill_patches(patches, slabs, ends, masks):
+    lat_t, chans = slabs[0].shape
+    lon_t = len(slabs) - 2
+    place = lax.broadcasted_iota(jnp.int32, (lat_t, chans), 0)
+    for i in range(lon_t + 2):
+        low_row, high_row = ends[i] * masks[0:1], ends[i] * masks[1:2]
+        down = jnp.where(place == 0, low_row, pltpu.roll(slabs[i], 1, 0)).astype(BF16)
+        up = jnp.where(place == lat_t - 1, high_row, pltpu.roll(slabs[i], lat_t - 1, 0)).astype(BF16)
+        mid = slabs[i].astype(BF16)
+        for a in range(3):
+            x = i - a
+            if 0 <= x < lon_t:
+                for b, piece in enumerate((down, mid, up)):
+                    k = 3 * a + b
+                    patches[x * lat_t : (x + 1) * lat_t, k * chans : (k + 1) * chans] = piece
+
+
+def assemble(patches, field_refs, moved):
+    state_ref, s_ref, row_ref, lo_ref, hi_ref, extra_ref, masks_ref = field_refs
+    lon_t, lat_t, chans = moved.shape
+    moved[...] = state_ref[0].astype(F32) + s_ref[0, :lon_t].astype(F32)
+    rows = row_ref[0].astype(F32) + s_ref[0, lon_t + 2, : lon_t + 2].astype(F32)
+    slabs = [lo_ref[0].astype(F32) + s_ref[0, lon_t].astype(F32)]
+    slabs += [moved[i] for i in range(lon_t)]
+    slabs += [hi_ref[0].astype(F32) + s_ref[0, lon_t + 1].astype(F32)]
+    ends = [rows[i : i + 1] for i in [lon_t] + list(range(lon_t)) + [lon_t + 1]]
+    fill_patches(patches, slabs, ends, masks_ref[...])
+    patches[:, 9 * chans :] = extra_ref[0]
+
+
+def forward_kernel(info, *refs):
+    field_refs, (w1_ref, mid_ref, dec_ref, bias_ref, dep_ref) = refs[:7], refs[7:12]
+    state_out, low_out, row_out, up_out, down_out, pre1_out, pre2_out, patches, moved = refs[12:]
+    lon_t, lat_t, chans = moved.shape
+    hid = mid_ref.shape[0]
+    assemble(patches, field_refs, moved)
+    pre1 = mm(patches[...], w1_ref[...])
+    pre1_out[0] = pre1
+    active1 = gelu_of(pre1).astype(BF16)
+    pre2 = mm(active1, mid_ref[...]) + bias_ref[0:1, :hid]
+    pre2_out[0] = pre2
+    active2 = gelu_of(pre2).astype(BF16)
+    out = mm(active2, dec_ref[...]) + bias_ref[1:2, :chans]
+    state_out[0] = moved[...] + out.reshape(lon_t, lat_t, chans)
+    row_out[0] = jnp.where(info[0] == 1, state_out[0, :, 0, :], state_out[0, :, lat_t - 1, :])
+    low_out[0] = state_out[0].astype(BF16)
+    up_out[0] = state_out[0, lon_t - 1]
+    down_out[0] = state_out[0, 0]
+
+
+GRAD_PAD = 128
+
+
+def grad_layout(chans, hid):
+    one, two, three = 9 * chans, 9 * chans + hid, 9 * chans + hid + chans
+    return (one, two, three, -(-(three + 8) // GRAD_PAD) * GRAD_PAD)
+
+
+def add_grads(first, patches, active1, active2, g_out, g_pre2, g_pre1, acc_enc, acc_mid, acc_dec):
+    enc = mm_rows(patches[...], g_pre1[...])
+    mid = mm_rows(active1[...], g_pre2[...])
+    dec = mm_rows(g_out[...], active2[...])
+
+    @pl.when(first)
+    def _():
+        acc_enc[...] = enc
+        acc_mid[...] = mid
+        acc_dec[...] = dec
+
+    @pl.when(jnp.logical_not(first))
+    def _():
+        acc_enc[...] += enc
+        acc_mid[...] += mid
+        acc_dec[...] += dec
+
+
+def pack_grads(out, before, chans, hid, acc_enc, acc_mid, acc_dec, vecs):
+    one, two, three, rows = grad_layout(chans, hid)
+    tail = jnp.concatenate([vecs[2:3, :chans], vecs[1:2, :chans]], axis=1)
+    out[three:] = jnp.zeros((rows - three, hid), F32)
+    pieces = [
+        (0, one, lambda: acc_enc[:one]),
+        (one, two, lambda: acc_mid[...]),
+        (two, three, lambda: acc_dec[...]),
+        (three, three + 1, lambda: acc_enc[one + 3 : one + 4]),
+        (three + 1, three + 2, lambda: acc_enc[one : one + 1]),
+        (three + 2, three + 3, lambda: vecs[0:1]),
+        (three + 3, three + 4, lambda: tail),
+        (three + 4, three + 5, lambda: vecs[3:4]),
+    ]
+    for start, stop, piece in pieces:
+        if before is None:
+            out[start:stop] = piece()
+        else:
+            out[start:stop] = before[start:stop] + piece()
+
+
+def turn_kernel(more, info, *refs):
+    field_refs, (w1_ref, mid_ref, dec_ref, bias_ref) = refs[:7], refs[7:11]
+    extra_ref, masks_ref = field_refs[5:]
+    target_ref, area_ref, w1t_ref, midt_ref, dect_ref, dep_ref = refs[11:17]
+    before = refs[17] if more else None
+    (
+        gm_out, low_out, lo_out, hi_out, rows_out, grads_out,
+        patches, moved, active1, active2, slope1, slope2, g_out, g_pre2, g_pre1, spread,
+        acc_enc, acc_mid, acc_dec, vecs,
+    ) = refs[18 if more else 17 :]
+    lon_t, lat_t, chans = moved.shape
+    hid = mid_ref.shape[0]
+    first = pl.program_id(0) == 0
+    assemble(patches, field_refs, moved)
+    spread[...] = jnp.zeros_like(spread)
+
+    @pl.when(first)
+    def _():
+        vecs[...] = jnp.zeros_like(vecs)
+
+    step = 8
+    for x in range(0, lon_t, step):
+        rows = slice(x * lat_t, (x + step) * lat_t)
+        pre1 = mm(patches[rows], w1_ref[...])
+        a1, d1 = gelu_and_slope(pre1)
+        active1[rows] = a1.astype(BF16)
+        slope1[rows] = d1
+        pre2 = mm(active1[rows], mid_ref[...]) + bias_ref[0:1, :hid]
+        a2, d2 = gelu_and_slope(pre2)
+        active2[rows] = a2.astype(BF16)
+        slope2[rows] = d2
+        out = mm(active2[rows], dec_ref[...]) + bias_ref[1:2, :chans]
+        fresh = moved[x : x + step] + out.reshape(step, lat_t, chans)
+        diff = fresh - target_ref[0, x : x + step].astype(F32)
+        valid = jnp.broadcast_to(extra_ref[0, rows, 6:7].astype(F32), (step * lat_t, chans))
+        weight = valid.reshape(step, lat_t, chans) * area_ref[...][None]
+        vecs[3:4, :chans] += jnp.sum(weight.reshape(step * lat_t, chans), 0, keepdims=True)
+        weighted = weight * diff
+        vecs[1:2, :chans] += jnp.sum((weighted * diff).reshape(step * lat_t, chans), 0, keepdims=True)
+        grad = 2.0 * weighted
+        moved[x : x + step] = grad
+        low = grad.reshape(step * lat_t, chans).astype(BF16)
+        g_out[rows] = low
+        vecs[2:3, :chans] += jnp.sum(low.astype(F32), 0, keepdims=True)
+        gp2 = (mm(low, dect_ref[...]) * slope2[rows]).astype(BF16)
+        g_pre2[rows] = gp2
+        vecs[0:1] += jnp.sum(gp2.astype(F32), 0, keepdims=True)
+        gp1 = (mm(gp2, midt_ref[...]) * slope1[rows]).astype(BF16)
+        g_pre1[rows] = gp1
+        taps = mm(gp1, w1t_ref[...])
+        for a in range(3):
+            for b in range(3):
+                k = 3 * a + b
+                spread[b, x + a : x + a + step] += taps[:, k * chans : (k + 1) * chans].reshape(
+                    step, lat_t, chans
+                )
+    place = lax.broadcasted_iota(jnp.int32, (lat_t, chans), 0)
+    masks = masks_ref[...]
+    for i in range(lon_t + 2):
+        down, here, up = spread[0, i], spread[1, i], spread[2, i]
+        got = here + jnp.where(place == lat_t - 1, 0.0, pltpu.roll(down, lat_t - 1, 0))
+        got = got + jnp.where(place == 0, 0.0, pltpu.roll(up, 1, 0))
+        beyond = down[0:1] * masks[0:1] + up[lat_t - 1 : lat_t] * masks[1:2]
+        if i in (0, lon_t + 1):
+            at = lon_t if i == 0 else lon_t + 1
+            edge = lo_out if i == 0 else hi_out
+            edge[0, :lat_t] = got.astype(BF16)
+            edge[0, lat_t:] = jnp.broadcast_to(beyond, (edge.shape[1] - lat_t, chans)).astype(BF16)
+            low_out[0, at] = got.astype(BF16)
+        else:
+            at = i - 1
+            total = got + moved[at]
+            gm_out[0, at] = total
+            low_out[0, at] = total.astype(BF16)
+        rows_out[0, at : at + 1] = beyond
+    rest = jnp.zeros((lat_t - rows_out.shape[1], chans), F32)
+    low_out[0, lon_t + 2] = jnp.concatenate([rows_out[0], rest], axis=0).astype(BF16)
+    add_grads(first, patches, active1, active2, g_out, g_pre2, g_pre1, acc_enc, acc_mid, acc_dec)
+
+    @pl.when(pl.program_id(0) == pl.num_programs(0) - 1)
+    def _():
+        pack_grads(grads_out, before, chans, hid, acc_enc, acc_mid, acc_dec, vecs)
+
+
+def bottom_kernel(more, info, *refs):
+    field_refs = refs[:7]
+    pre1_ref, pre2_ref, gm_ref, glo_ref, ghi_ref, grow_ref, gs_ref, midt_ref, dect_ref, dep_ref = refs[7:17]
+    before = refs[17] if more else None
+    (
+        grads_out, patches, moved, active1, active2, g_out, g_pre2, g_pre1, acc_enc, acc_mid, acc_dec, vecs,
+    ) = refs[17 + more :]
+    lon_t, lat_t, chans = moved.shape
+    hid = midt_ref.shape[0]
+    first = pl.program_id(0) == 0
+    assemble(patches, field_refs, moved)
+
+    moved[...] = gm_ref[0] + gs_ref[0].astype(F32)
+    moved[0] += glo_ref[0, :lat_t].astype(F32)
+    moved[lon_t - 1] += ghi_ref[0, :lat_t].astype(F32)
+    place = lax.broadcasted_iota(jnp.int32, (lat_t, chans), 0)
+    inner = place == jnp.where(info[0] == 1, 0, lat_t - 1)
+    for x in range(lon_t):
+        moved[x] += jnp.where(inner, grow_ref[0, x : x + 1], 0.0)
+
+    @pl.when(first)
+    def _():
+        vecs[...] = jnp.zeros_like(vecs)
+
+    step = 8
+    for x in range(0, lon_t, step):
+        rows = slice(x * lat_t, (x + step) * lat_t)
+        a1, d1 = gelu_and_slope(pre1_ref[0, rows])
+        active1[rows] = a1.astype(BF16)
+        a2, d2 = gelu_and_slope(pre2_ref[0, rows])
+        active2[rows] = a2.astype(BF16)
+        low = moved[x : x + step].reshape(step * lat_t, chans).astype(BF16)
+        g_out[rows] = low
+        vecs[2:3, :chans] += jnp.sum(low.astype(F32), 0, keepdims=True)
+        gp2 = (mm(low, dect_ref[...]) * d2).astype(BF16)
+        g_pre2[rows] = gp2
+        vecs[0:1] += jnp.sum(gp2.astype(F32), 0, keepdims=True)
+        g_pre1[rows] = (mm(gp2, midt_ref[...]) * d1).astype(BF16)
+    add_grads(first, patches, active1, active2, g_out, g_pre2, g_pre1, acc_enc, acc_mid, acc_dec)
+
+    @pl.when(pl.program_id(0) == pl.num_programs(0) - 1)
+    def _():
+        pack_grads(grads_out, before, chans, hid, acc_enc, acc_mid, acc_dec, vecs)
+
+
+def field_specs(field, chunk, half, pool_state):
+    state, s_ext, row, lo, hi, extra, masks = field
+    there = chunk if pool_state else None
+    return [
+        snap_spec(state.shape[1:], there, half),
+        snap_spec(s_ext.shape[1:]),
+        snap_spec(row.shape[1:], there, half),
+        snap_spec(lo.shape[1:], there, half),
+        snap_spec(hi.shape[1:], there, half),
+        snap_spec(extra.shape[1:], chunk, half),
+        whole(masks.shape),
+    ]
+
+
+def cost(micros):
+    return pl.CostEstimate(flops=int(micros * 1e9), bytes_accessed=int(micros * 3e6), transcendentals=0)
+
+
+def forward_call(info, chunk, half, field, weights, dep):
+    dims = field[0].shape[1:]
+    lon_t, lat_t, chans = dims
+    cells = lon_t * lat_t
+    hid = weights["mid"].shape[0]
+    ws = [weights[k] for k in ("w1", "mid", "dec", "bias")]
+    edge = ((lat_t, chans), F32)
+    outs = [(dims, F32), (dims, BF16), ((lon_t, chans), F32), edge, edge, ((cells, hid), F32), ((cells, hid), F32)]
+    return pl.pallas_call(
+        forward_kernel,
+        grid_spec=grid_of(
+            HALF,
+            field_specs(field, chunk, half, True) + [whole(w.shape) for w in ws] + [any_spec()],
+            [snap_spec(d) for d, _ in outs],
+            [pltpu.VMEM((cells, 10 * chans), BF16), pltpu.VMEM(dims, F32)],
+        ),
+        out_shape=[shape_of((HALF,) + d, t) for d, t in outs],
+        compiler_params=params(),
+        cost_estimate=cost(6.5),
+        name="forward",
+    )(info, *field, *ws, dep)
+
+
+def back_scratch(dims, hid):
+    lon_t, lat_t, chans = dims
+    cells = lon_t * lat_t
+    return [
+        pltpu.VMEM((cells, chans), BF16),
+        pltpu.VMEM((cells, hid), BF16),
+        pltpu.VMEM((cells, hid), BF16),
+    ], [
+        pltpu.VMEM((10 * chans, hid), F32),
+        pltpu.VMEM((hid, hid), F32),
+        pltpu.VMEM((chans, hid), F32),
+        pltpu.VMEM((8, hid), F32),
+    ]
+
+
+def turn_call(info, chunk, half, field, weights, targets, area, dep, before):
+    dims = field[0].shape[1:]
+    lon_t, lat_t, chans = dims
+    cells = lon_t * lat_t
+    hid = weights["mid"].shape[0]
+    ws = [weights[k] for k in ("w1", "mid", "dec", "bias")]
+    wt = [weights[k] for k in ("w1t", "midt", "dect")]
+    grad_rows = grad_layout(chans, hid)[-1]
+    more = before is not None
+    last = [before] if more else []
+    edge = ((lat_t + 16, chans), BF16)
+    low = ((lon_t + 3, lat_t, chans), BF16)
+    outs = [(dims, F32), low, edge, edge, ((lon_t + 8, chans), F32)]
+    grads, sums = back_scratch(dims, hid)
+    return pl.pallas_call(
+        functools.partial(turn_kernel, more),
+        grid_spec=grid_of(
+            HALF,
+            field_specs(field, chunk, half, False)
+            + [whole(w.shape) for w in ws]
+            + [snap_spec(dims, chunk, half), whole(area.shape)]
+            + [whole(w.shape) for w in wt]
+            + [any_spec()]
+            + [whole(w.shape) for w in last],
+            [snap_spec(d) for d, _ in outs] + [whole((grad_rows, hid))],
+            [
+                pltpu.VMEM((cells, 10 * chans), BF16),
+                pltpu.VMEM(dims, F32),
+                pltpu.VMEM((cells, hid), BF16),
+                pltpu.VMEM((cells, hid), BF16),
+                pltpu.VMEM((cells, hid), F32),
+                pltpu.VMEM((cells, hid), F32),
+            ]
+            + grads
+            + [pltpu.VMEM((3, lon_t + 2, lat_t, chans), F32)]
+            + sums,
+        ),
+        out_shape=[shape_of((HALF,) + d, t) for d, t in outs] + [shape_of((grad_rows, hid), F32)],
+        compiler_params=params(),
+        cost_estimate=cost(13.0),
+        name="turn",
+    )(info, *field, *ws, targets, area, *wt, dep, *last)
+
+
+def bottom_call(info, chunk, half, field, weights, pre, gm, gs, dep, before):
+    dims = field[0].shape[1:]
+    lon_t, lat_t, chans = dims
+    cells = lon_t * lat_t
+    hid = weights["mid"].shape[0]
+    wt = [weights[k] for k in ("midt", "dect")]
+    grad_rows = grad_layout(chans, hid)[-1]
+    more = before is not None
+    last = [before] if more else []
+    grads, sums = back_scratch(dims, hid)
+    return pl.pallas_call(
+        functools.partial(bottom_kernel, more),
+        grid_spec=grid_of(
+            HALF,
+            field_specs(field, chunk, half, True)
+            + [snap_spec(v.shape[1:]) for v in (*pre, *gm, gs)]
+            + [whole(w.shape) for w in wt]
+            + [any_spec()]
+            + [whole(w.shape) for w in last],
+            whole((grad_rows, hid)),
+            [
+                pltpu.VMEM((cells, 10 * chans), BF16),
+                pltpu.VMEM(dims, F32),
+                pltpu.VMEM((cells, hid), BF16),
+                pltpu.VMEM((cells, hid), BF16),
+            ]
+            + grads
+            + sums,
+        ),
+        out_shape=shape_of((grad_rows, hid), F32),
+        compiler_params=params(),
+        cost_estimate=cost(8.0),
+        name="bottom",
+    )(info, *field, *pre, *gm, gs, *wt, dep, *last)
+
+
+def three_parts(vec):
+    high = lax.reduce_precision(vec, 8, 7)
+    rest = vec - high
+    mid = lax.reduce_precision(rest, 8, 7)
+    low = lax.reduce_precision(rest - mid, 8, 7)
+    return jnp.stack([high, mid, low], axis=-2)
+
+
+def layer_weights(enc, mid, dec, vec):
+    taps, chans, hid = enc.shape
+    parts = jnp.concatenate([three_parts(vec[hid : 2 * hid]), three_parts(vec[:hid])], axis=0)
+    parts = jnp.pad(parts, ((0, chans - 6), (0, 0)))
+    w1 = jnp.concatenate([enc.reshape(taps * chans, hid), parts], axis=0).astype(BF16)
+    pad = jnp.zeros((hid - chans,), F32)
+    bias = jnp.stack([vec[2 * hid : 3 * hid], jnp.concatenate([vec[3 * hid :], pad])])
+    return {
+        "w1": w1,
+        "mid": mid.astype(BF16),
+        "dec": dec.astype(BF16),
+        "bias": bias,
+        "w1t": jnp.transpose(enc, (2, 0, 1)).reshape(hid, taps * chans).astype(BF16),
+        "midt": mid.T.astype(BF16),
+        "dect": dec.T.astype(BF16),
+    }
+
+
+def reduce_all(part):
+    lon_n = lax.axis_size("lon")
+    me = lax.axis_index("lon")
+
+    def over(stride):
+        return "lon", (me // stride) % 2, [(i, i ^ stride) for i in range(lon_n)]
+
+    stages = [over(1), over(2), ("lat", lax.axis_index("lat"), [(0, 1), (1, 0)]), over(8)]
+    for axis, bit, perm in stages:
+        half = part.shape[0] // 2
+        give = lax.dynamic_slice_in_dim(part, (1 - bit) * half, half)
+        mine = lax.dynamic_slice_in_dim(part, bit * half, half)
+        part = mine + lax.ppermute(give, axis, perm)
+    axis, _, perm = over(4)
+    part = part + lax.ppermute(part, axis, perm)
+    for axis, bit, perm in reversed(stages):
+        got = lax.ppermute(part, axis, perm)
+        part = jnp.concatenate([jnp.where(bit == 0, part, got), jnp.where(bit == 0, got, part)])
+    return part
+
+
+def fast_grads(states, targets, sea_temp, ocean, valid, w_enc, w_mid, w_dec, biases):
+    pool, lon_t, lat_t, chans = states.shape
+    lon_n, lat_n = lax.axis_size("lon"), lax.axis_size("lat")
+    nlon, nlat = lon_t * lon_n, lat_t * lat_n
+    zonal, forward, inverse, area_all = host_tables(nlon, nlat, 88)
+    hemi = lax.axis_index("lat")
+    info = hemi[None].astype(jnp.int32)
+    flip = np.concatenate([np.arange(lat_t, nlat), np.arange(lat_t)])
+    flip2 = np.concatenate([flip, nlat + flip])
+    ends = (np.arange(0, nlon, lon_t)[None, :] + np.array([[-1], [lon_t]])).reshape(-1) % nlon
+    zonal_in = jnp.asarray(np.concatenate([zonal, zonal[:, ends]], axis=1))
+    zonal_out = jnp.asarray(
+        np.concatenate([zonal[:nlon], zonal[:nlon][ends], zonal[nlon:], zonal[nlon:][ends]], axis=0)
+    )
+    forward = jnp.where(hemi == 0, jnp.asarray(forward), jnp.asarray(forward[:, flip]))
+    inverse = jnp.where(hemi == 0, jnp.asarray(inverse), jnp.asarray(inverse[flip2]))
+    side = jnp.stack([hemi == 1, hemi == 0]).astype(F32)
+    masks = jnp.broadcast_to(side[:, None], (2, chans))
+    area = lax.dynamic_slice_in_dim(jnp.asarray(area_all, F32), hemi * lat_t, lat_t)
+    area_wide = jnp.broadcast_to(area[:, None], (lat_t, chans))
+    up = [(i, (i + 1) % lon_n) for i in range(lon_n)]
+    down = [(t, s) for s, t in up]
+    swap = [(0, 1), (1, 0)]
+    chunks = range(pool // CHUNK)
+
+    traded = [
+        lax.ppermute(lax.dynamic_slice_in_dim(states, first_of(c, 1, info), HALF), "lat", swap)
+        for c in chunks
+    ]
+    def inner_row(column):
+        return jnp.where(hemi == 0, column[..., -1:, :], column[..., 0:1, :])
+
+    def edge_rows(row, lo, hi):
+        return lax.ppermute(jnp.concatenate([row, inner_row(lo), inner_row(hi)], axis=1), "lat", swap)
+
+    lo0, hi0 = lax.ppermute(states[:, -1], "lon", up), lax.ppermute(states[:, 0], "lon", down)
+    rows0 = edge_rows(inner_row(states)[:, :, 0], lo0, hi0)
+    sea = ocean.astype(F32) * sea_temp.astype(F32)
+    cells = lon_t * lat_t
+    lane = jnp.arange(chans)
+    wide_sea = sea.reshape(pool, cells, 1).astype(BF16)
+    wide_valid = valid.reshape(pool, cells, 1).astype(BF16)
+    extra = jnp.where(lane < 3, wide_sea, jnp.where(lane < 6, jnp.ones((), BF16), wide_valid))
+    extra = jnp.where(lane < 7, extra, jnp.zeros((), BF16))
+    layers = [layer_weights(w_enc[i], w_mid[i], w_dec[i], biases[i]) for i in range(2)]
+
+    last = [forward]
+
+    def then(result, pick=None):
+        last[0] = result if pick is None else result[pick]
+        return result
+
+    def over_lon(spec):
+        return lax.all_to_all(spec, "lon", split_axis=0, concat_axis=0, tiled=True)
+
+    class Chunk:
+        def __init__(self, c):
+            self.c = c
+            self.early = 0
+            self.round = 0
+            self.other = traded[c]
+            self.field0, self.pres = [None, None], [None, None]
+            self.low, self.s_ext, self.gm = [None, None], [None, None], [None, None]
+            self.fresh, self.edge, self.row = [None, None], [None, None], [None, None]
+            self.back, self.beyond = [None, None], [None, None]
+
+        def legendre(self):
+            half = self.early
+            own = states if self.round == 0 else self.low[half]
+            there = self.c if self.round == 0 else None
+            got = legendre_call(
+                info, own, there, half, self.other, forward, last[0], self.round == 2
+            )
+            self.spec = over_lon(then(got))
+
+        def zonal(self):
+            table = zonal_in if self.round == 2 else zonal_out
+            self.spec = over_lon(then(zonal_call(self.spec, table, last[0], self.round == 2)))
+
+        def synthesis(self):
+            got = synthesis_call(info, self.spec, inverse, HALF, self.round < 2, last[0])
+            own, send = then(got, 0)
+            self.s_ext[self.early] = own
+            self.s_ext[1 - self.early] = lax.ppermute(send, "lat", swap)
+
+        def forward(self, late):
+            half = self.early ^ late
+            field = (states, self.s_ext[half], rows0, lo0, hi0, extra, masks)
+            self.field0[half] = field
+            got = forward_call(info, self.c, half, field, layers[0], last[0])
+            fresh, low, row, to_up, to_down, *pre = then(got, 1)
+            self.fresh[half], self.low[half], self.pres[half] = fresh, low, pre
+            self.send(half, late)
+            lo, hi = lax.ppermute(to_up, "lon", up), lax.ppermute(to_down, "lon", down)
+            self.edge[half] = (lo, hi)
+            self.row[1 - half] = edge_rows(row, lo, hi)
+
+        def turn(self, late, before):
+            half = self.early ^ late
+            field = (self.fresh[half], self.s_ext[half], self.row[half], *self.edge[half], extra, masks)
+            got = turn_call(info, self.c, half, field, layers[1], targets, area_wide, last[0], before)
+            gm, low, to_lo, to_hi, rows, before = then(got, 1)
+            self.low[half] = low
+            self.send(half, late)
+            from_lo, from_hi = lax.ppermute(to_hi, "lon", up), lax.ppermute(to_lo, "lon", down)
+            self.back[half] = (gm, from_lo, from_hi)
+            rows = rows[:, :lon_t]
+            place = jnp.arange(lon_t)[:, None]
+            rows = rows + jnp.where(place == 0, from_lo[:, lat_t : lat_t + 1].astype(F32), 0.0)
+            rows = rows + jnp.where(place == lon_t - 1, from_hi[:, lat_t : lat_t + 1].astype(F32), 0.0)
+            self.beyond[1 - half] = lax.ppermute(rows, "lat", swap)
+            return before
+
+        def send(self, half, late):
+            if not late:
+                self.other = lax.ppermute(self.low[half], "lat", swap)
+
+        def flip(self):
+            self.early = 1 - self.early
+            self.round += 1
+
+        def bottom(self, late, before):
+            half = self.early ^ late
+            gm = (*self.back[half], self.beyond[half])
+            got = bottom_call(
+                info, self.c, half, self.field0[half], layers[0], self.pres[half], gm,
+                self.s_ext[half], last[0], before,
+            )
+            return then(got)
+
+    a, b = (Chunk(c) for c in chunks)
+    top, low = None, None
+    a.legendre()
+    a.zonal()
+    b.legendre()
+    for one, two in ((a, b), (b, a)):
+        one.synthesis()
+        one.forward(0)
+        two.zonal()
+        one.forward(1)
+        one.flip()
+        one.legendre()
+    for one, two in ((a, b), (b, a)):
+        one.synthesis()
+        top = one.turn(0, top)
+        two.zonal()
+        top = one.turn(1, top)
+        one.flip()
+        one.legendre()
+    upper = reduce_all(top)
+    a.synthesis()
+    low = a.bottom(0, low)
+    b.zonal()
+    low = a.bottom(1, low)
+    b.synthesis()
+    low = b.bottom(0, low)
+    low = b.bottom(1, low)
+    return reduce_all(low), upper
+
+
+def update_kernel(
+    rate, pick_ref, g0_ref, g1_ref, v_ref, *refs,
+):
+    ins, outs = refs[:12], refs[12:]
+    layer, part = pl.program_id(0), pl.program_id(1)
+    chans = ins[0].shape[2]
+    hid = ins[0].shape[3]
+    scale = 1.0 / v_ref[1, 4:5, 0:1]
+    one, two, three, _ = grad_layout(chans, hid)
+
+    def apply(group, at, grad):
+        w_ref, m_ref, a_ref = (ins[4 * i + group] for i in range(3))
+        new_ref, mom_ref, avg_ref, copy_ref = (outs[4 * i + group] for i in range(4))
+        scaled = grad * scale
+        mom = MOMENTUM * m_ref[at] + scaled
+        fresh = w_ref[at] - rate * (scaled + MOMENTUM * mom)
+        new_ref[at] = fresh
+        mom_ref[at] = mom
+        avg_ref[at] = AVERAGE * a_ref[at] + (1.0 - AVERAGE) * fresh
+        copy_ref[at] = fresh.astype(BF16)
+
+    def layer_step(g_ref):
+        for tap in range(3):
+            rows = pl.ds(pl.multiple_of((part * 3 + tap) * chans, chans), chans)
+            apply(0, (0, tap), g_ref[rows].astype(F32))
+
+        @pl.when(part == 0)
+        def _():
+            apply(1, (0,), g_ref[one:two].astype(F32))
+            apply(2, (0,), g_ref[two:three].astype(F32).T)
+
+    pl.when(layer == 0)(lambda: layer_step(g0_ref))
+    pl.when(layer == 1)(lambda: layer_step(g1_ref))
+
+    @pl.when((layer == 0) & (part == 0))
+    def _():
+        for i in range(2):
+            for r in range(4):
+                wide = hid if r < 3 else chans
+                at = (slice(i, i + 1), slice(r * hid, r * hid + wide))
+                apply(3, at, v_ref[i, r : r + 1, :wide])
+
+
+def update_call(rate, sums, arrays):
+    w_enc, w_mid, w_dec, biases = arrays[:4]
+    layers, taps, chans, hid = w_enc.shape
+    three = grad_layout(chans, hid)[2]
+    vecs = jnp.stack([s[three : three + 8].astype(F32) for s in sums])
+    enc = pl.BlockSpec((1, taps // 3, chans, hid), lambda i, p, pick: (i, p, 0, 0))
+    mid = pl.BlockSpec((1, hid, hid), lambda i, p, pick: (i, 0, 0))
+    dec = pl.BlockSpec((1, hid, chans), lambda i, p, pick: (i, 0, 0))
+    bias = whole(biases.shape)
+    specs = [enc, mid, dec, bias]
+    shapes = [w_enc.shape, w_mid.shape, w_dec.shape, biases.shape]
+    got = pl.pallas_call(
+        functools.partial(update_kernel, rate),
+        grid_spec=pltpu.PrefetchScalarGridSpec(
+            num_scalar_prefetch=1,
+            grid=(layers, 3),
+            in_specs=[whole(sums[0].shape), whole(sums[1].shape), whole(vecs.shape)]
+            + specs * 3,
+            out_specs=specs * 4,
+        ),
+        out_shape=[shape_of(s, F32) for s in shapes * 3] + [shape_of(s, BF16) for s in shapes],
+        compiler_params=params(),
+        cost_estimate=cost(8.0),
+        name="update",
+    )(jnp.zeros((1,), jnp.int32), sums[0], sums[1], vecs, *arrays)
+    return (jnp.sum(vecs[1, 3, chans:]), vecs[1, 4, 0], *got)
+
+
+def fits(states, w_mid, lon_n, lat_n):
+    pool, lon_t, lat_t, chans = states.shape
+    return (
+        lat_n == 2
+        and lon_n == 16
+        and lon_t == 16
+        and lat_t == 64
+        and pool == 2 * CHUNK
+        and chans == 128
+        and w_mid.shape[1] == 2 * chans
+        and w_mid.shape[0] == 2
+    )
 
 
 def with_halo(block, sides, width, periodic):
@@ -152,26 +1073,7 @@
     return (grad_moved + spectral(grad_moved, tabs), (g_enc, g_mid, g_dec, g_vec))
 
 
-def body(
-    states,
-    targets,
-    sea_temp,
-    ocean,
-    valid,
-    order,
-    w_enc,
-    w_mid,
-    w_dec,
-    biases,
-    mom_enc,
-    mom_mid,
-    mom_dec,
-    mom_bias,
-    avg_enc,
-    avg_mid,
-    avg_dec,
-    avg_bias,
-):
+def general_grads(states, targets, sea_temp, ocean, valid, order, w_enc, w_mid, w_dec, biases):
     pool, lon_t, lat_t, chans = states.shape
     layers, hid = (w_mid.shape[0], w_mid.shape[1])
     nlon = lon_t * lax.axis_size("lon")
@@ -229,8 +1131,42 @@
     g_enc, g_mid, g_dec, g_vec, loss, total = lax.psum(
         (sums[0], sums[1], sums[2], sums[3], loss, total), ("lon", "lat")
     )
-    grads = (g_enc.reshape(w_enc.shape), g_mid, g_dec, g_vec)
-    rate = RATE_BASE * math.sqrt(pool * nlon * nlat)
+    return g_enc.reshape(w_enc.shape), g_mid, g_dec, g_vec, loss, total
+
+
+def body(
+    states,
+    targets,
+    sea_temp,
+    ocean,
+    valid,
+    order,
+    w_enc,
+    w_mid,
+    w_dec,
+    biases,
+    mom_enc,
+    mom_mid,
+    mom_dec,
+    mom_bias,
+    avg_enc,
+    avg_mid,
+    avg_dec,
+    avg_bias,
+):
+    pool, lon_t, lat_t = states.shape[:3]
+    lon_n, lat_n = lax.axis_size("lon"), lax.axis_size("lat")
+    rate = RATE_BASE * math.sqrt(pool * lon_t * lon_n * lat_t * lat_n)
+    if fits(states, w_mid, lon_n, lat_n):
+        sums = fast_grads(states, targets, sea_temp, ocean, valid, w_enc, w_mid, w_dec, biases)
+        arrays = (w_enc, w_mid, w_dec, biases, mom_enc, mom_mid, mom_dec, mom_bias)
+        arrays += (avg_enc, avg_mid, avg_dec, avg_bias)
+        return update_call(rate, sums, arrays)
+    found = general_grads(
+        states, targets, sea_temp, ocean, valid, order, w_enc, w_mid, w_dec, biases
+    )
+    loss, total = found[4:]
+    grads = (found[0].reshape(w_enc.shape),) + found[1:4]
     news, moms, avgs, copies = ([], [], [], [])
     for weight_now, grad, mom, avg in zip(
         (w_enc, w_mid, w_dec, biases),

time: 1530 us -> 520 us (0.34)
  local copies, waits for them, and re-layouts: 602 us -> 28.7 us
  starting transfers between devices: 349 us -> 143 us
  matrix products: 196 us -> 0 us
  Pallas kernels: 0 us -> 192 us
  other arithmetic: 124 us -> 17.3 us
  waiting for transfers between devices: 183 us -> 127 us
  blocking collectives: 41.3 us -> 0 us
  between operations: 25.5 us -> 2.43 us
    unnamed x752 -> x148, local copies, waits for them, and re-layouts: 240 us -> 14.6 us
    dot_general x116 -> x0, matrix products: 196 us -> none  [the longest x8 23.8 us: layer_backward(): jnp.einsum('rk,rh->kh', patches, g_pre1, preferred_element_type=jnp.float32)]
    pallas_call x0 -> x31, Pallas kernels: none -> 192 us  [the longest x4 57.4 us: turn_call(): pl.pallas_call(functools.partial(turn_kernel, more), grid_spec=grid_of(HA...]
    all_to_all x48 -> x12, starting transfers between devices: 222 us -> 68.8 us  [over_lon(): return lax.all_to_all(spec, 'lon', split_axis=0, concat_axis=0, tiled=True)]
    another operation x23 -> x2, local copies, waits for them, and re-layouts: 112 us -> 0.01 us  [update_call(): vecs = jnp.stack([s[three:three + 8].astype(F32) for s in sums])]
    convert_element_type x64 -> x7, local copies, waits for them, and re-layouts: 108 us -> 4.24 us  [the longest x2 1.52 us: layer_weights(): mid.astype(BF16)]
    ppermute x48 -> x57, waiting for transfers between devices: 0.13 us -> 103 us  [the longest x8 20.9 us: reduce_all(): got = lax.ppermute(part, axis, perm)]
    psum x1 -> x0, waiting for transfers between devices: 93.7 us -> none  [body(): lax.psum((sums[0], sums[1], sums[2], sums[3], loss, total), ('lon', 'lat'))]
  transfers between devices with their start and end apart: 97 -> 69, of which waited for: 28 -> 26; matrix products, arithmetic and copies ran while one was open for 53% -> 6% of each run, Pallas kernels for 0% -> 35%
where the time goes in v2:
time: 520 us; the launch traced here: 510 us
  Pallas kernels  192 us (37%)
  starting transfers between devices  143 us (28%)
  waiting for transfers between devices  127 us (24%)
  local copies, waits for them, and re-layouts  28.7 us (6%)
  other arithmetic  17.3 us (3%)
    all_to_all x12, starting transfers between devices, over_lon(): return lax.all_to_all(spec, 'lon', split_axis=0, concat_axis=0, tiled=True)  68.8 us
    pallas_call x4, Pallas kernels, turn_call(): pl.pallas_call(functools.partial(turn_kernel, more), grid_spec=grid_of(HA...  57.4 us
    pallas_call x4, Pallas kernels, bottom_call(): pl.pallas_call(functools.partial(bottom_kernel, more), grid_spec=grid_of(...  39.7 us
    pallas_call x4, Pallas kernels, forward_call(): pl.pallas_call(forward_kernel, grid_spec=grid_of(HALF, field_specs(field,...  25.5 us
    all_to_all x12, waiting for transfers between devices, over_lon(): return lax.all_to_all(spec, 'lon', split_axis=0, concat_axis=0, tiled=True)  23.7 us
    pallas_call x6, Pallas kernels, synthesis_call(): pl.pallas_call(functools.partial(synthesis_kernel, wide), grid_spec=grid_...  21.2 us
    ppermute x8, waiting for transfers between devices, reduce_all(): got = lax.ppermute(part, axis, perm)  20.9 us
    ppermute x4, waiting for transfers between devices, forward(): lax.ppermute(to_up, 'lon', up)  20.7 us
  transfers between devices with their start and end apart: 69, of which 26 were waited for; matrix products, arithmetic and copies ran while one was open for 6% of the time, Pallas kernels for 35%

profile of v2, /device:TPU:0, one launch (start us, length us, event | category | flops | bytes accessed | tf_op | source)
XLA Modules:
  0.0 510.0 jit_solution(4454104991809142397)
XLA Ops:
  2.0 3.0 collective-permute-start.1
  6.1 3.9 collective-permute-start.3
  11.3 6.5 %collective-permute-done.1.other_ref = bf16[2,16,64,128]{3,2,1,0:T(8,128)(2,1)S(1)} collective-permute-done((bf16[2,16,64,128]{3,2,1,0:T(8,128)(2,1)S(1)}, bf16[2,16,64,128]{3,2,1,0:T(8,128)(2,1)S(1)}, u32[]{:S(2)}, u32[]{:S(2)}) %collective-permute-start.1) | collective-permute-done | bytes 524320 | tf_op jit(solution)/shard_map/ppermute | solution.py:721
  18.6 3.2 legendre.6.dep_ref
  21.8 6.6 %all-to-all-start = ((bf16[16,11,16,128]{3,2,1,0:T(8,128)(2,1)}), bf16[16,11,16,128]{3,2,1,0:T(8,128)(2,1)S(1)}, u32[]{:S(2)}, u32[]{:S(2)}) async-start(bf16[16,11,16,128]{3,2,1,0:T(8,128)(2,1)} %legendre.6.dep_ref), calls=%async_computation | async-start | bytes 1441792 | tf_op jit(solution)/shard_map/all_to_all | solution.py:748
  31.5 14.5 %all-to-all-done.x_ref = bf16[16,11,16,128]{3,2,1,0:T(8,128)(2,1)S(1)} async-done(((bf16[16,11,16,128]{3,2,1,0:T(8,128)(2,1)}), bf16[16,11,16,128]{3,2,1,0:T(8,128)(2,1)S(1)}, u32[]{:S(2)}, u32[]{:S(2)}) %all-to-all-start) | async-done | bytes 720928 | tf_op jit(solution)/shard_map/all_to_all | solution.py:748
  49.6 5.3 %all-to-all-start.2 = ((bf16[16,13,16,128]{3,2,1,0:T(8,128)(2,1)}), bf16[16,13,16,128]{3,2,1,0:T(8,128)(2,1)S(1)}, u32[]{:S(2)}, u32[]{:S(2)}) async-start(bf16[16,13,16,128]{3,2,1,0:T(8,128)(2,1)} %zonal.6.dep_ref), calls=%async_computation.2 | async-start | bytes 1703936 | tf_op jit(solution)/shard_map/all_to_all | solution.py:748
  62.8 4.4 select_select_fusion.refs_5_
  67.2 3.1 legendre.7.dep_ref
  70.4 4.3 all-to-all-done.2.x_ref
  74.7 5.8 %all-to-all-start.1 = ((bf16[16,11,16,128]{3,2,1,0:T(8,128)(2,1)}), bf16[16,11,16,128]{3,2,1,0:T(8,128)(2,1)S(1)}, u32[]{:S(2)}, u32[]{:S(2)}) async-start(bf16[16,11,16,128]{3,2,1,0:T(8,128)(2,1)} %legendre.7.dep_ref), calls=%async_computation.1 | async-start | bytes 1441792 | tf_op jit(solution)/shard_map/all_to_all | solution.py:748
  83.6 3.6 synthesis.6
  88.4 6.3 %forward.4 = (f32[2,16,64,128]{3,2,1,0:T(8,128)}, bf16[2,16,64,128]{3,2,1,0:T(8,128)(2,1)}, f32[2,16,128]{2,1,0:T(8,128)}, f32[2,64,128]{2,1,0:T(8,128)}, f32[2,...) custom-call(s32[1]{0:T(128)} %bitcast.info, bf16[8,16,64,128]{3,2,1,0:T(8,128)(2,1)} %refs_0_.16, ...), custom_call_target="tpu_custom_call" | custom-call | flops 6499999744 | bytes 19500000 | tf_op jit(solution)/shard_map/forward/pallas_call | solution.py:538
  96.4 3.5 collective-permute-start.10
  103.6 3.8 all-to-all-start.3
  107.7 20.1 %collective-permute-done.9.refs_3_ = f32[2,64,128]{2,1,0:T(8,128)S(1)} collective-permute-done((f32[2,64,128]{2,1,0:T(8,128)S(1)}, f32[2,64,128]{2,1,0:T(8,128)S(1)}, u32[]{:S(2)}, u32[]{:S(2)}) %collective-permute-start.9) | collective-permute-done | bytes 65568 | tf_op jit(solution)/shard_map/ppermute | solution.py:788
  130.0 6.4 %forward.5 = (f32[2,16,64,128]{3,2,1,0:T(8,128)}, bf16[2,16,64,128]{3,2,1,0:T(8,128)(2,1)}, f32[2,16,128]{2,1,0:T(8,128)}, f32[2,64,128]{2,1,0:T(8,128)}, f32[2,...) custom-call(s32[1]{0:T(128)} %bitcast.info, bf16[8,16,64,128]{3,2,1,0:T(8,128)(2,1)} %refs_0_.16, ...), custom_call_target="tpu_custom_call" | custom-call | flops 6499999744 | bytes 19500000 | tf_op jit(solution)/shard_map/forward/pallas_call | solution.py:538
  138.0 3.1 legendre.8.dep_ref
  141.2 6.2 %all-to-all-start.4 = ((bf16[16,11,16,128]{3,2,1,0:T(8,128)(2,1)}), bf16[16,11,16,128]{3,2,1,0:T(8,128)(2,1)S(1)}, u32[]{:S(2)}, u32[]{:S(2)}) async-start(bf16[16,11,16,128]{3,2,1,0:T(8,128)(2,1)} %legendre.8.dep_ref), calls=%async_computation.4 | async-start | bytes 1441792 | tf_op jit(solution)/shard_map/all_to_all | solution.py:748
  147.4 3.7 synthesis.7
  151.2 6.4 %forward.6 = (f32[2,16,64,128]{3,2,1,0:T(8,128)}, bf16[2,16,64,128]{3,2,1,0:T(8,128)(2,1)}, f32[2,16,128]{2,1,0:T(8,128)}, f32[2,64,128]{2,1,0:T(8,128)}, f32[2,...) custom-call(s32[1]{0:T(128)} %bitcast.info, bf16[8,16,64,128]{3,2,1,0:T(8,128)(2,1)} %refs_0_.16, ...), custom_call_target="tpu_custom_call" | custom-call | flops 6499999744 | bytes 19500000 | tf_op jit(solution)/shard_map/forward/pallas_call | solution.py:538
  157.6 4.4 collective-permute-start.22
  168.8 6.0 %all-to-all-start.6 = ((bf16[16,13,16,128]{3,2,1,0:T(8,128)(2,1)}), bf16[16,13,16,128]{3,2,1,0:T(8,128)(2,1)S(1)}, u32[]{:S(2)}, u32[]{:S(2)}) async-start(bf16[16,13,16,128]{3,2,1,0:T(8,128)(2,1)} %zonal.8.refs_11_), calls=%async_computation.6 | async-start | bytes 1703936 | tf_op jit(solution)/shard_map/all_to_all | solution.py:748
  175.8 3.9 collective-permute-done.7.refs_1_
  180.6 6.4 %forward.7 = (f32[2,16,64,128]{3,2,1,0:T(8,128)}, bf16[2,16,64,128]{3,2,1,0:T(8,128)(2,1)}, f32[2,16,128]{2,1,0:T(8,128)}, f32[2,64,128]{2,1,0:T(8,128)}, f32[2,...) custom-call(s32[1]{0:T(128)} %bitcast.info, bf16[8,16,64,128]{3,2,1,0:T(8,128)(2,1)} %refs_0_.16, ...), custom_call_target="tpu_custom_call" | custom-call | flops 6499999744 | bytes 19500000 | tf_op jit(solution)/shard_map/forward/pallas_call | solution.py:538
  188.4 3.1 collective-permute-start.19
  191.4 3.1 legendre.9.dep_ref
  196.3 5.7 %all-to-all-start.5 = ((bf16[16,11,16,128]{3,2,1,0:T(8,128)(2,1)}), bf16[16,11,16,128]{3,2,1,0:T(8,128)(2,1)S(1)}, u32[]{:S(2)}, u32[]{:S(2)}) async-start(bf16[16,11,16,128]{3,2,1,0:T(8,128)(2,1)} %legendre.9.dep_ref), calls=%async_computation.5 | async-start | bytes 1441792 | tf_op jit(solution)/shard_map/all_to_all | solution.py:748
  202.0 3.7 synthesis.8
  207.5 13.8 %turn.4 = (f32[2,16,64,128]{3,2,1,0:T(8,128)}, bf16[2,19,64,128]{3,2,1,0:T(8,128)(2,1)}, bf16[2,80,128]{2,1,0:T(8,128)(2,1)}, bf16[2,80,128]{2,1,0:T(8,128)(2,1)...) custom-call(s32[1]{0:T(128)} %bitcast.info, f32[2,16,64,128]{3,2,1,0:T(8,128)} %get-tuple-element.107.refs_0_, ...), custom_call_target="tpu_custom_call" | custom-call | flops 12999999488 | bytes 39000000 | tf_op jit(solution)/shard_map/turn/pallas_call | solution.py:582
  225.3 6.3 %all-to-all-start.7 = ((bf16[16,13,16,128]{3,2,1,0:T(8,128)(2,1)}), bf16[16,13,16,128]{3,2,1,0:T(8,128)(2,1)S(1)}, u32[]{:S(2)}, u32[]{:S(2)}) async-start(bf16[16,13,16,128]{3,2,1,0:T(8,128)(2,1)} %zonal.9.refs_16_), calls=%async_computation.7 | async-start | bytes 1703936 | tf_op jit(solution)/shard_map/all_to_all | solution.py:748
  231.6 4.9 collective-permute-start.42
  236.5 10.3 %collective-permute-done.42.refs_11_ = bf16[2,80,128]{2,1,0:T(8,128)(2,1)S(1)} collective-permute-done((bf16[2,80,128]{2,1,0:T(8,128)(2,1)S(1)}, bf16[2,80,128]{2,1,0:T(8,128)(2,1)S(1)}, u32[]{:S(2)}, u32[]{:S(2)}) %collective-permute-start.42) | collective-permute-done | bytes 40992 | tf_op jit(solution)/shard_map/ppermute | solution.py:799
  248.7 14.6 %turn.5 = (f32[2,16,64,128]{3,2,1,0:T(8,128)}, bf16[2,19,64,128]{3,2,1,0:T(8,128)(2,1)}, bf16[2,80,128]{2,1,0:T(8,128)(2,1)}, bf16[2,80,128]{2,1,0:T(8,128)(2,1)...) custom-call(s32[1]{0:T(128)} %bitcast.info, f32[2,16,64,128]{3,2,1,0:T(8,128)} %get-tuple-element.115.refs_0_, ...), custom_call_target="tpu_custom_call" | custom-call | flops 12999999488 | bytes 39000000 | tf_op jit(solution)/shard_map/turn/pallas_call | solution.py:582
  263.4 4.4 collective-permute-start.40
  268.7 3.5 legendre.10.dep_ref
  272.2 6.8 %all-to-all-start.8 = ((bf16[16,13,16,128]{3,2,1,0:T(8,128)(2,1)}), bf16[16,13,16,128]{3,2,1,0:T(8,128)(2,1)S(1)}, u32[]{:S(2)}, u32[]{:S(2)}) async-start(bf16[16,13,16,128]{3,2,1,0:T(8,128)(2,1)} %legendre.10.dep_ref), calls=%async_computation.8 | async-start | bytes 1703936 | tf_op jit(solution)/shard_map/all_to_all | solution.py:748
  279.0 3.7 synthesis.9
  283.3 14.5 %turn.6 = (f32[2,16,64,128]{3,2,1,0:T(8,128)}, bf16[2,19,64,128]{3,2,1,0:T(8,128)(2,1)}, bf16[2,80,128]{2,1,0:T(8,128)(2,1)}, bf16[2,80,128]{2,1,0:T(8,128)(2,1)...) custom-call(s32[1]{0:T(128)} %bitcast.info, f32[2,16,64,128]{3,2,1,0:T(8,128)} %get-tuple-element.126.refs_0_, ...), custom_call_target="tpu_custom_call" | custom-call | flops 12999999488 | bytes 39000000 | tf_op jit(solution)/shard_map/turn/pallas_call | solution.py:582
  300.5 3.5 collective-permute-start.34
  306.9 3.1 zonal.10.refs_16_
  310.0 5.9 %all-to-all-start.10 = ((bf16[16,11,16,128]{3,2,1,0:T(8,128)(2,1)}), bf16[16,11,16,128]{3,2,1,0:T(8,128)(2,1)S(1)}, u32[]{:S(2)}, u32[]{:S(2)}) async-start(bf16[16,11,16,128]{3,2,1,0:T(8,128)(2,1)} %zonal.10.refs_16_), calls=%async_computation.10 | async-start | bytes 1441792 | tf_op jit(solution)/shard_map/all_to_all | solution.py:748
  316.8 14.5 %turn.7 = (f32[2,16,64,128]{3,2,1,0:T(8,128)}, bf16[2,19,64,128]{3,2,1,0:T(8,128)(2,1)}, bf16[2,80,128]{2,1,0:T(8,128)(2,1)}, bf16[2,80,128]{2,1,0:T(8,128)(2,1)...) custom-call(s32[1]{0:T(128)} %bitcast.info, f32[2,16,64,128]{3,2,1,0:T(8,128)} %get-tuple-element.103.refs_0_, ...), custom_call_target="tpu_custom_call" | custom-call | flops 12999999488 | bytes 39000000 | tf_op jit(solution)/shard_map/turn/pallas_call | solution.py:582
  331.9 4.0 collective-permute-start.36
  337.2 3.4 legendre.11.dep_ref
  340.7 4.4 all-to-all-start.9
  347.0 3.2 synthesis.10
  350.8 9.3 %bottom.4.dep_ref.refs_17_ = f32[1664,256]{1,0:T(8,128)} custom-call(s32[1]{0:T(128)} %bitcast.info, bf16[8,16,64,128]{3,2,1,0:T(8,128)(2,1)} %refs_0_.16, bf16[2,19,64,128]{3,2,1,0:T(8,128)(2,1)} %get-tuple-element.98.refs_1_.refs_11_, bf16[8,18,128]{2,1,0:T(8,128)(2,1)} %copy-done.61, bf16[8,64,128]{2,1,0:T(8,128)(2,1)} %collective-permute-done.2.refs_3_, ...), custom_call_target="tpu_custom_call" | custom-call | flops 8000000000 | bytes 24000000 | tf_op jit(solution)/shard_map/bottom/pallas_call | solution.py:622
  360.1 4.8 all-to-all-done.9.x_ref
  364.9 3.2 zonal.11.refs_16_
  368.1 6.1 %all-to-all-start.11 = ((bf16[16,11,16,128]{3,2,1,0:T(8,128)(2,1)}), bf16[16,11,16,128]{3,2,1,0:T(8,128)(2,1)}, u32[]{:S(2)}, u32[]{:S(2)}) async-start(bf16[16,11,16,128]{3,2,1,0:T(8,128)(2,1)} %zonal.11.refs_16_), calls=%async_computation.11 | async-start | bytes 1441792 | tf_op jit(solution)/shard_map/all_to_all | solution.py:748
  380.5 8.9 %collective-permute-done.44.refs_12_ = f32[2,16,128]{2,1,0:T(8,128)S(1)} collective-permute-done((f32[2,16,128]{2,1,0:T(8,128)S(1)}, f32[2,16,128]{2,1,0:T(8,128)S(1)}, u32[]{:S(2)}, u32[]{:S(2)}) %collective-permute-start.44) | collective-permute-done | bytes 16416 | tf_op jit(solution)/shard_map/ppermute | solution.py:805
  390.1 10.0 %bottom.5.dep_ref.refs_17_ = f32[1664,256]{1,0:T(8,128)} custom-call(s32[1]{0:T(128)} %bitcast.info, bf16[8,16,64,128]{3,2,1,0:T(8,128)(2,1)} %refs_0_.16, bf16[2,19,64,128]{3,2,1,0:T(8,128)(2,1)} %copy-done.49, bf16[8,18,128]{2,1,0:T(8,128)(2,1)} %copy-done.61, bf16[8,64,128]{2,1,0:T(8,128)(2,1)} %collective-permute-done.2.refs_3_, ...), custom_call_target="tpu_custom_call" | custom-call | flops 8000000000 | bytes 24000000 | tf_op jit(solution)/shard_map/bottom/pallas_call | solution.py:622
  400.1 3.2 synthesis.11
  405.0 10.0 %bottom.6.refs_16_.refs_17_ = f32[1664,256]{1,0:T(8,128)} custom-call(s32[1]{0:T(128)} %bitcast.info, bf16[8,16,64,128]{3,2,1,0:T(8,128)(2,1)} %refs_0_.16, bf16[2,19,64,128]{3,2,1,0:T(8,128)(2,1)} %get-tuple-element.102.refs_1_.refs_11_, bf16[8,18,128]{2,1,0:T(8,128)(2,1)} %copy-done.61, bf16[8,64,128]{2,1,0:T(8,128)(2,1)} %collective-permute-done.2.refs_3_, ...), custom_call_target="tpu_custom_call" | custom-call | flops 8000000000 | bytes 24000000 | tf_op jit(solution)/shard_map/bottom/pallas_call | solution.py:622
  417.7 10.3 %bottom.7 = f32[1664,256]{1,0:T(8,128)} custom-call(s32[1]{0:T(128)} %bitcast.info, bf16[8,16,64,128]{3,2,1,0:T(8,128)(2,1)} %refs_0_.16, bf16[2,19,64,128]{3,2,1,0:T(8,128)(2,1)} %copy-done.50, bf16[8,18,128]{2,1,0:T(8,128)(2,1)} %copy-done.61, bf16[8,64,128]{2,1,0:T(8,128)(2,1)} %collective-permute-done.2.refs_3_, ...), custom_call_target="tpu_custom_call" | custom-call | flops 8000000000 | bytes 24000000 | tf_op jit(solution)/shard_map/bottom/pallas_call | solution.py:622
  430.4 6.7 %collective-permute-done.26 = f32[208,256]{1,0:T(8,128)S(1)} collective-permute-done((f32[208,256]{1,0:T(8,128)S(1)}, f32[208,256]{1,0:T(8,128)S(1)}, u32[]{:S(2)}, u32[]{:S(2)}) %collective-permute-start.26) | collective-permute-done | bytes 213024 | tf_op jit(solution)/shard_map/ppermute | solution.py:686
  445.3 4.5 collective-permute-done.28
  453.0 3.7 collective-permute-done.29
  459.9 5.4 %collective-permute-done.51 = f32[104,256]{1,0:T(8,128)S(1)} collective-permute-done((f32[104,256]{1,0:T(8,128)S(1)}, f32[104,256]{1,0:T(8,128)S(1)}, u32[]{:S(2)}, u32[]{:S(2)}) %collective-permute-start.51) | collective-permute-done | bytes 106528 | tf_op jit(solution)/shard_map/ppermute | solution.py:686
  465.7 5.5 %collective-permute-done.52 = f32[104,256]{1,0:T(8,128)S(1)} collective-permute-done((f32[104,256]{1,0:T(8,128)S(1)}, f32[104,256]{1,0:T(8,128)S(1)}, u32[]{:S(2)}, u32[]{:S(2)}) %collective-permute-start.52) | collective-permute-done | bytes 106528 | tf_op jit(solution)/shard_map/ppermute | solution.py:688
  472.9 4.1 collective-permute-done.53
  485.3 8.4 %collective-permute-done.55 = f32[416,256]{1,0:T(8,128)S(1)} collective-permute-done((f32[416,256]{1,0:T(8,128)}, f32[416,256]{1,0:T(8,128)S(1)}, u32[]{:S(2)}, u32[]{:S(2)}) %collective-permute-start.55) | collective-permute-done | bytes 426016 | tf_op jit(solution)/shard_map/ppermute | solution.py:690
  498.6 10.9 %update.1 = (f32[2,9,128,256]{3,2,1,0:T(8,128)}, f32[2,256,256]{2,1,0:T(8,128)}, f32[2,256,128]{2,1,0:T(8,128)}, f32[2,896]{1,0:T(2,128)}, f32[2,9,128,256]{3,2,...) custom-call(s32[1]{0:T(128)} %constant.122.clone.1.pick_ref, ...), custom_call_target="tpu_custom_call" | custom-call | flops 8000000000 | bytes 24000000 | tf_op jit(solution)/shard_map/update/pallas_call | solution.py:909
  (352 shorter events, 107.6 us)
Async XLA Ops:
  2.0 15.8 %collective-permute-start.1 = (bf16[2,16,64,128]{3,2,1,0:T(8,128)(2,1)S(1)}, bf16[2,16,64,128]{3,2,1,0:T(8,128)(2,1)S(1)}, u32[]{:S(2)}, u32[]{:S(2)}) collective-permute-start(bf16[2,16,64,128]{3,2,1,0:T(8,128)(2,1)S(1)} %get-tuple-element.184), channel_id=1, source_target_pairs={{0,1},{1,0},{2,3},{3,2},{4,5},{5,4},{6,7},{7,6},{8,9},{9,8},{10,11... | collective-permute-start | bytes 1572872 | tf_op jit(solution)/shard_map/ppermute | solution.py:721
  5.0 62.2 %collective-permute-start = (bf16[2,16,64,128]{3,2,1,0:T(8,128)(2,1)S(1)}, bf16[2,16,64,128]{3,2,1,0:T(8,128)(2,1)}, u32[]{:S(2)}, u32[]{:S(2)}) collective-permute-start(bf16[2,16,64,128]{3,2,1,0:T(8,128)(2,1)S(1)} %get-tuple-element.185), channel_id=1, source_target_pairs={{0,1},{1,0},{2,3},{3,2},{4,5},{5,4},{6,7},{7,6},{8,9},{9,8},{10,11... | collective-permute-start | bytes 1572872 | tf_op jit(solution)/shard_map/ppermute | solution.py:721
  6.1 74.4 %collective-permute-start.3 = (bf16[8,64,128]{2,1,0:T(8,128)(2,1)S(1)}, bf16[8,64,128]{2,1,0:T(8,128)(2,1)}, u32[]{:S(2)}, u32[]{:S(2)}) collective-permute-start(bf16[8,64,128]{2,1,0:T(8,128)(2,1)S(1)} %get-tuple-element.183), channel_id=1, source_target_pairs={{2,0},{4,2},{6,4},{8,6},{10,8},{12,10},{14,12},{16,14},{18,16},{20... | collective-permute-start | bytes 393224 | tf_op jit(solution)/shard_map/ppermute | solution.py:730
  10.0 71.3 %collective-permute-start.2 = (bf16[8,64,128]{2,1,0:T(8,128)(2,1)S(1)}, bf16[8,64,128]{2,1,0:T(8,128)(2,1)}, u32[]{:S(2)}, u32[]{:S(2)}) collective-permute-start(bf16[8,64,128]{2,1,0:T(8,128)(2,1)S(1)} %get-tuple-element.182), channel_id=1, source_target_pairs={{0,2},{2,4},{4,6},{6,8},{8,10},{10,12},{12,14},{14,16},{16,18},{18... | collective-permute-start | bytes 393224 | tf_op jit(solution)/shard_map/ppermute | solution.py:730
  21.8 24.2 %all-to-all-start = ((bf16[16,11,16,128]{3,2,1,0:T(8,128)(2,1)}), bf16[16,11,16,128]{3,2,1,0:T(8,128)(2,1)S(1)}, u32[]{:S(2)}, u32[]{:S(2)}) async-start(bf16[16,11,16,128]{3,2,1,0:T(8,128)(2,1)} %legendre.6.dep_ref), calls=%async_computation | async-start | bytes 1441792 | tf_op jit(solution)/shard_map/all_to_all | solution.py:748
  49.6 25.0 %all-to-all-start.2 = ((bf16[16,13,16,128]{3,2,1,0:T(8,128)(2,1)}), bf16[16,13,16,128]{3,2,1,0:T(8,128)(2,1)S(1)}, u32[]{:S(2)}, u32[]{:S(2)}) async-start(bf16[16,13,16,128]{3,2,1,0:T(8,128)(2,1)} %zonal.6.dep_ref), calls=%async_computation.2 | async-start | bytes 1703936 | tf_op jit(solution)/shard_map/all_to_all | solution.py:748
  74.7 25.2 %all-to-all-start.1 = ((bf16[16,11,16,128]{3,2,1,0:T(8,128)(2,1)}), bf16[16,11,16,128]{3,2,1,0:T(8,128)(2,1)S(1)}, u32[]{:S(2)}, u32[]{:S(2)}) async-start(bf16[16,11,16,128]{3,2,1,0:T(8,128)(2,1)} %legendre.7.dep_ref), calls=%async_computation.1 | async-start | bytes 1441792 | tf_op jit(solution)/shard_map/all_to_all | solution.py:748
  82.0 5.7 %collective-permute-start.4 = (bf16[8,18,128]{2,1,0:T(8,128)(2,1)S(1)}, bf16[8,18,128]{2,1,0:T(8,128)(2,1)S(1)}, u32[]{:S(2)}, u32[]{:S(2)}) collective-permute-start(bf16[8,18,128]{2,1,0:T(8,128)(2,1)S(1)} %pad_maximum_fusion.8), channel_id=1, source_target_pairs={{0,1},{1,0},{2,3},{3,2},{4,5},{5,4},{6,7},{7,6},{8,9},{9,8},{10,11... | collective-permute-start | bytes 110600 | tf_op jit(solution)/shard_map/ppermute | solution.py:728
  87.3 41.9 %collective-permute-start.5 = (bf16[2,19,64,128]{3,2,1,0:T(8,128)(2,1)}, bf16[2,19,64,128]{3,2,1,0:T(8,128)(2,1)S(1)}, u32[]{:S(2)}, u32[]{:S(2)}) collective-permute-start(bf16[2,19,64,128]{3,2,1,0:T(8,128)(2,1)} %get-tuple-element.100), channel_id=1, source_target_pairs={{0,1},{1,0},{2,3},{3,2},{4,5},{5,4},{6,7},{7,6},{8,9},{9,8},{10,11... | collective-permute-start | bytes 1867784 | tf_op jit(solution)/shard_map/ppermute | solution.py:778
  94.8 42.4 %collective-permute-start.6 = (bf16[2,16,64,128]{3,2,1,0:T(8,128)(2,1)}, bf16[2,16,64,128]{3,2,1,0:T(8,128)(2,1)S(1)}, u32[]{:S(2)}, u32[]{:S(2)}) collective-permute-start(bf16[2,16,64,128]{3,2,1,0:T(8,128)(2,1)} %get-tuple-element.99.dep_ref), channel_id=1, source_target_pairs={{0,1},{1,0},{2,3},{3,2},{4,5},{5,4},{6,7},{7,6},{8,9},{9,8},{10,11... | collective-permute-start | bytes 1572872 | tf_op jit(solution)/shard_map/ppermute | solution.py:810
  96.4 11.4 %collective-permute-start.10 = (f32[2,64,128]{2,1,0:T(8,128)}, f32[2,64,128]{2,1,0:T(8,128)S(1)}, u32[]{:S(2)}, u32[]{:S(2)}) collective-permute-start(f32[2,64,128]{2,1,0:T(8,128)} %get-tuple-element.111), channel_id=1, source_target_pairs={{2,0},{4,2},{6,4},{8,6},{10,8},{12,10},{14,12},{16,14},{18,16},{20... | collective-permute-start | bytes 196616 | tf_op jit(solution)/shard_map/ppermute | solution.py:788
  103.6 37.6 %all-to-all-start.3 = ((bf16[16,13,16,128]{3,2,1,0:T(8,128)(2,1)}), bf16[16,13,16,128]{3,2,1,0:T(8,128)(2,1)S(1)}, u32[]{:S(2)}, u32[]{:S(2)}) async-start(bf16[16,13,16,128]{3,2,1,0:T(8,128)(2,1)} %zonal.7.refs_11_), calls=%async_computation.3 | async-start | bytes 1703936 | tf_op jit(solution)/shard_map/all_to_all | solution.py:748
  107.4 20.5 %collective-permute-start.9 = (f32[2,64,128]{2,1,0:T(8,128)S(1)}, f32[2,64,128]{2,1,0:T(8,128)S(1)}, u32[]{:S(2)}, u32[]{:S(2)}) collective-permute-start(f32[2,64,128]{2,1,0:T(8,128)S(1)} %copy-done.60), channel_id=1, source_target_pairs={{0,2},{2,4},{4,6},{6,8},{8,10},{10,12},{12,14},{14,16},{16,18},{18... | collective-permute-start | bytes 196616 | tf_op jit(solution)/shard_map/ppermute | solution.py:788
  127.9 78.9 %collective-permute-start.11 = (f32[2,18,128]{2,1,0:T(8,128)S(1)}, f32[2,18,128]{2,1,0:T(8,128)S(1)}, u32[]{:S(2)}, u32[]{:S(2)}) collective-permute-start(f32[2,18,128]{2,1,0:T(8,128)S(1)} %pad_maximum_fusion.9), channel_id=1, source_target_pairs={{0,1},{1,0},{2,3},{3,2},{4,5},{5,4},{6,7},{7,6},{8,9},{9,8},{10,11... | collective-permute-start | bytes 55304 | tf_op jit(solution)/shard_map/ppermute | solution.py:728
  136.5 10.9 %collective-permute-start.12 = (f32[2,64,128]{2,1,0:T(8,128)}, f32[2,64,128]{2,1,0:T(8,128)S(1)}, u32[]{:S(2)}, u32[]{:S(2)}) collective-permute-start(f32[2,64,128]{2,1,0:T(8,128)} %get-tuple-element.112), channel_id=1, source_target_pairs={{0,2},{2,4},{4,6},{6,8},{8,10},{10,12},{12,14},{14,16},{16,18},{18... | collective-permute-start | bytes 196616 | tf_op jit(solution)/shard_map/ppermute | solution.py:788
  141.2 23.8 %all-to-all-start.4 = ((bf16[16,11,16,128]{3,2,1,0:T(8,128)(2,1)}), bf16[16,11,16,128]{3,2,1,0:T(8,128)(2,1)S(1)}, u32[]{:S(2)}, u32[]{:S(2)}) async-start(bf16[16,11,16,128]{3,2,1,0:T(8,128)(2,1)} %legendre.8.dep_ref), calls=%async_computation.4 | async-start | bytes 1441792 | tf_op jit(solution)/shard_map/all_to_all | solution.py:748
  157.6 6.6 %collective-permute-start.22 = (f32[2,64,128]{2,1,0:T(8,128)}, f32[2,64,128]{2,1,0:T(8,128)S(1)}, u32[]{:S(2)}, u32[]{:S(2)}) collective-permute-start(f32[2,64,128]{2,1,0:T(8,128)} %get-tuple-element.125), channel_id=1, source_target_pairs={{2,0},{4,2},{6,4},{8,6},{10,8},{12,10},{14,12},{16,14},{18,16},{20... | collective-permute-start | bytes 196616 | tf_op jit(solution)/shard_map/ppermute | solution.py:788
  162.0 85.9 %collective-permute-start.15 = (f32[2,18,128]{2,1,0:T(8,128)S(1)}, f32[2,18,128]{2,1,0:T(8,128)S(1)}, u32[]{:S(2)}, u32[]{:S(2)}) collective-permute-start(f32[2,18,128]{2,1,0:T(8,128)S(1)} %pad_maximum_fusion.10), channel_id=1, source_target_pairs={{0,1},{1,0},{2,3},{3,2},{4,5},{5,4},{6,7},{7,6},{8,9},{9,8},{10,11... | collective-permute-start | bytes 55304 | tf_op jit(solution)/shard_map/ppermute | solution.py:728
  162.8 12.0 %collective-permute-start.21 = (f32[2,64,128]{2,1,0:T(8,128)}, f32[2,64,128]{2,1,0:T(8,128)S(1)}, u32[]{:S(2)}, u32[]{:S(2)}) collective-permute-start(f32[2,64,128]{2,1,0:T(8,128)} %get-tuple-element.124), channel_id=1, source_target_pairs={{0,2},{2,4},{4,6},{6,8},{8,10},{10,12},{12,14},{14,16},{16,18},{18... | collective-permute-start | bytes 196616 | tf_op jit(solution)/shard_map/ppermute | solution.py:788
  162.8 17.0 %collective-permute-start.7 = (bf16[2,19,64,128]{3,2,1,0:T(8,128)(2,1)S(1)}, bf16[2,19,64,128]{3,2,1,0:T(8,128)(2,1)S(1)}, u32[]{:S(2)}, u32[]{:S(2)}) collective-permute-start(bf16[2,19,64,128]{3,2,1,0:T(8,128)(2,1)S(1)} %copy-done.54), channel_id=1, source_target_pairs={{0,1},{1,0},{2,3},{3,2},{4,5},{5,4},{6,7},{7,6},{8,9},{9,8},{10,11... | collective-permute-start | bytes 1867784 | tf_op jit(solution)/shard_map/ppermute | solution.py:778
  164.2 24.1 %collective-permute-start.8 = (bf16[2,16,64,128]{3,2,1,0:T(8,128)(2,1)}, bf16[2,16,64,128]{3,2,1,0:T(8,128)(2,1)}, u32[]{:S(2)}, u32[]{:S(2)}) collective-permute-start(bf16[2,16,64,128]{3,2,1,0:T(8,128)(2,1)} %get-tuple-element.105.dep_ref), channel_id=1, source_target_pairs={{0,1},{1,0},{2,3},{3,2},{4,5},{5,4},{6,7},{7,6},{8,9},{9,8},{10,11... | collective-permute-start | bytes 1572872 | tf_op jit(solution)/shard_map/ppermute | solution.py:810
  168.8 27.5 %all-to-all-start.6 = ((bf16[16,13,16,128]{3,2,1,0:T(8,128)(2,1)}), bf16[16,13,16,128]{3,2,1,0:T(8,128)(2,1)S(1)}, u32[]{:S(2)}, u32[]{:S(2)}) async-start(bf16[16,13,16,128]{3,2,1,0:T(8,128)(2,1)} %zonal.8.refs_11_), calls=%async_computation.6 | async-start | bytes 1703936 | tf_op jit(solution)/shard_map/all_to_all | solution.py:748
  174.8 107.9 %collective-permute-start.23 = (f32[2,18,128]{2,1,0:T(8,128)S(1)}, f32[2,18,128]{2,1,0:T(8,128)S(1)}, u32[]{:S(2)}, u32[]{:S(2)}) collective-permute-start(f32[2,18,128]{2,1,0:T(8,128)S(1)} %pad_maximum_fusion.12), channel_id=1, source_target_pairs={{0,1},{1,0},{2,3},{3,2},{4,5},{5,4},{6,7},{7,6},{8,9},{9,8},{10,11... | collective-permute-start | bytes 55304 | tf_op jit(solution)/shard_map/ppermute | solution.py:728
  186.9 8.2 %collective-permute-start.18 = (f32[2,64,128]{2,1,0:T(8,128)}, f32[2,64,128]{2,1,0:T(8,128)S(1)}, u32[]{:S(2)}, u32[]{:S(2)}) collective-permute-start(f32[2,64,128]{2,1,0:T(8,128)} %get-tuple-element.122), channel_id=1, source_target_pairs={{0,2},{2,4},{4,6},{6,8},{8,10},{10,12},{12,14},{14,16},{16,18},{18... | collective-permute-start | bytes 196616 | tf_op jit(solution)/shard_map/ppermute | solution.py:788
  188.4 6.2 %collective-permute-start.19 = (f32[2,64,128]{2,1,0:T(8,128)}, f32[2,64,128]{2,1,0:T(8,128)S(1)}, u32[]{:S(2)}, u32[]{:S(2)}) collective-permute-start(f32[2,64,128]{2,1,0:T(8,128)} %get-tuple-element.123), channel_id=1, source_target_pairs={{2,0},{4,2},{6,4},{8,6},{10,8},{12,10},{14,12},{16,14},{18,16},{20... | collective-permute-start | bytes 196616 | tf_op jit(solution)/shard_map/ppermute | solution.py:788
  195.2 120.7 %collective-permute-start.20 = (f32[2,18,128]{2,1,0:T(8,128)S(1)}, f32[2,18,128]{2,1,0:T(8,128)S(1)}, u32[]{:S(2)}, u32[]{:S(2)}) collective-permute-start(f32[2,18,128]{2,1,0:T(8,128)S(1)} %pad_maximum_fusion.11), channel_id=1, source_target_pairs={{0,1},{1,0},{2,3},{3,2},{4,5},{5,4},{6,7},{7,6},{8,9},{9,8},{10,11... | collective-permute-start | bytes 55304 | tf_op jit(solution)/shard_map/ppermute | solution.py:728
  196.3 25.4 %all-to-all-start.5 = ((bf16[16,11,16,128]{3,2,1,0:T(8,128)(2,1)}), bf16[16,11,16,128]{3,2,1,0:T(8,128)(2,1)S(1)}, u32[]{:S(2)}, u32[]{:S(2)}) async-start(bf16[16,11,16,128]{3,2,1,0:T(8,128)(2,1)} %legendre.9.dep_ref), calls=%async_computation.5 | async-start | bytes 1441792 | tf_op jit(solution)/shard_map/all_to_all | solution.py:748
  205.7 42.2 %collective-permute-start.14 = (bf16[2,19,64,128]{3,2,1,0:T(8,128)(2,1)}, bf16[2,19,64,128]{3,2,1,0:T(8,128)(2,1)S(1)}, u32[]{:S(2)}, u32[]{:S(2)}) collective-permute-start(bf16[2,19,64,128]{3,2,1,0:T(8,128)(2,1)} %get-tuple-element.116), channel_id=1, source_target_pairs={{0,1},{1,0},{2,3},{3,2},{4,5},{5,4},{6,7},{7,6},{8,9},{9,8},{10,11... | collective-permute-start | bytes 1867784 | tf_op jit(solution)/shard_map/ppermute | solution.py:778
  221.4 10.2 %collective-permute-start.41 = (bf16[2,80,128]{2,1,0:T(8,128)(2,1)}, bf16[2,80,128]{2,1,0:T(8,128)(2,1)S(1)}, u32[]{:S(2)}, u32[]{:S(2)}) collective-permute-start(bf16[2,80,128]{2,1,0:T(8,128)(2,1)} %get-tuple-element.148), channel_id=1, source_target_pairs={{0,2},{2,4},{4,6},{6,8},{8,10},{10,12},{12,14},{14,16},{16,18},{18... | collective-permute-start | bytes 122888 | tf_op jit(solution)/shard_map/ppermute | solution.py:799
  225.3 46.8 %all-to-all-start.7 = ((bf16[16,13,16,128]{3,2,1,0:T(8,128)(2,1)}), bf16[16,13,16,128]{3,2,1,0:T(8,128)(2,1)S(1)}, u32[]{:S(2)}, u32[]{:S(2)}) async-start(bf16[16,13,16,128]{3,2,1,0:T(8,128)(2,1)} %zonal.9.refs_16_), calls=%async_computation.7 | async-start | bytes 1703936 | tf_op jit(solution)/shard_map/all_to_all | solution.py:748
  231.6 15.2 %collective-permute-start.42 = (bf16[2,80,128]{2,1,0:T(8,128)(2,1)S(1)}, bf16[2,80,128]{2,1,0:T(8,128)(2,1)S(1)}, u32[]{:S(2)}, u32[]{:S(2)}) collective-permute-start(bf16[2,80,128]{2,1,0:T(8,128)(2,1)S(1)} %copy-done.62), channel_id=1, source_target_pairs={{2,0},{4,2},{6,4},{8,6},{10,8},{12,10},{14,12},{16,14},{18,16},{20... | collective-permute-start | bytes 122888 | tf_op jit(solution)/shard_map/ppermute | solution.py:799
  246.9 21.0 %collective-permute-start.16 = (bf16[2,19,64,128]{3,2,1,0:T(8,128)(2,1)S(1)}, bf16[2,19,64,128]{3,2,1,0:T(8,128)(2,1)S(1)}, u32[]{:S(2)}, u32[]{:S(2)}) collective-permute-start(bf16[2,19,64,128]{3,2,1,0:T(8,128)(2,1)S(1)} %copy-done.52), channel_id=1, source_target_pairs={{0,1},{1,0},{2,3},{3,2},{4,5},{5,4},{6,7},{7,6},{8,9},{9,8},{10,11... | collective-permute-start | bytes 1867784 | tf_op jit(solution)/shard_map/ppermute | solution.py:810
  263.3 8.8 %collective-permute-start.39 = (bf16[2,80,128]{2,1,0:T(8,128)(2,1)}, bf16[2,80,128]{2,1,0:T(8,128)(2,1)S(1)}, u32[]{:S(2)}, u32[]{:S(2)}) collective-permute-start(bf16[2,80,128]{2,1,0:T(8,128)(2,1)} %get-tuple-element.145), channel_id=1, source_target_pairs={{0,2},{2,4},{4,6},{6,8},{8,10},{10,12},{12,14},{14,16},{16,18},{18... | collective-permute-start | bytes 122888 | tf_op jit(solution)/shard_map/ppermute | solution.py:799
  263.4 35.0 %collective-permute-start.40 = (bf16[2,80,128]{2,1,0:T(8,128)(2,1)}, bf16[2,80,128]{2,1,0:T(8,128)(2,1)S(1)}, u32[]{:S(2)}, u32[]{:S(2)}) collective-permute-start(bf16[2,80,128]{2,1,0:T(8,128)(2,1)} %get-tuple-element.146), channel_id=1, source_target_pairs={{2,0},{4,2},{6,4},{8,6},{10,8},{12,10},{14,12},{16,14},{18,16},{20... | collective-permute-start | bytes 122888 | tf_op jit(solution)/shard_map/ppermute | solution.py:799
  272.2 33.8 %all-to-all-start.8 = ((bf16[16,13,16,128]{3,2,1,0:T(8,128)(2,1)}), bf16[16,13,16,128]{3,2,1,0:T(8,128)(2,1)S(1)}, u32[]{:S(2)}, u32[]{:S(2)}) async-start(bf16[16,13,16,128]{3,2,1,0:T(8,128)(2,1)} %legendre.10.dep_ref), calls=%async_computation.8 | async-start | bytes 1703936 | tf_op jit(solution)/shard_map/all_to_all | solution.py:748
  297.8 6.4 %collective-permute-start.33 = (bf16[2,80,128]{2,1,0:T(8,128)(2,1)}, bf16[2,80,128]{2,1,0:T(8,128)(2,1)S(1)}, u32[]{:S(2)}, u32[]{:S(2)}) collective-permute-start(bf16[2,80,128]{2,1,0:T(8,128)(2,1)} %get-tuple-element.136), channel_id=1, source_target_pairs={{0,2},{2,4},{4,6},{6,8},{8,10},{10,12},{12,14},{14,16},{16,18},{18... | collective-permute-start | bytes 122888 | tf_op jit(solution)/shard_map/ppermute | solution.py:799
  298.4 17.5 %collective-permute-start.17 = (bf16[2,19,64,128]{3,2,1,0:T(8,128)(2,1)S(1)}, bf16[2,19,64,128]{3,2,1,0:T(8,128)(2,1)S(1)}, u32[]{:S(2)}, u32[]{:S(2)}) collective-permute-start(bf16[2,19,64,128]{3,2,1,0:T(8,128)(2,1)S(1)} %copy-done.53), channel_id=1, source_target_pairs={{0,1},{1,0},{2,3},{3,2},{4,5},{5,4},{6,7},{7,6},{8,9},{9,8},{10,11... | collective-permute-start | bytes 1867784 | tf_op jit(solution)/shard_map/ppermute | solution.py:778
  299.4 37.7 %collective-permute-start.38 = (bf16[2,19,64,128]{3,2,1,0:T(8,128)(2,1)}, bf16[2,19,64,128]{3,2,1,0:T(8,128)(2,1)}, u32[]{:S(2)}, u32[]{:S(2)}) collective-permute-start(bf16[2,19,64,128]{3,2,1,0:T(8,128)(2,1)} %get-tuple-element.130.dep_ref), channel_id=1, source_target_pairs={{0,1},{1,0},{2,3},{3,2},{4,5},{5,4},{6,7},{7,6},{8,9},{9,8},{10,11... | collective-permute-start | bytes 1867784 | tf_op jit(solution)/shard_map/ppermute | solution.py:810
  310.0 30.7 %all-to-all-start.10 = ((bf16[16,11,16,128]{3,2,1,0:T(8,128)(2,1)}), bf16[16,11,16,128]{3,2,1,0:T(8,128)(2,1)S(1)}, u32[]{:S(2)}, u32[]{:S(2)}) async-start(bf16[16,11,16,128]{3,2,1,0:T(8,128)(2,1)} %zonal.10.refs_16_), calls=%async_computation.10 | async-start | bytes 1441792 | tf_op jit(solution)/shard_map/all_to_all | solution.py:748
  331.3 13.8 %collective-permute-start.35 = (bf16[2,80,128]{2,1,0:T(8,128)(2,1)}, bf16[2,80,128]{2,1,0:T(8,128)(2,1)S(1)}, u32[]{:S(2)}, u32[]{:S(2)}) collective-permute-start(bf16[2,80,128]{2,1,0:T(8,128)(2,1)} %get-tuple-element.139), channel_id=1, source_target_pairs={{0,2},{2,4},{4,6},{6,8},{8,10},{10,12},{12,14},{14,16},{16,18},{18... | collective-permute-start | bytes 122888 | tf_op jit(solution)/shard_map/ppermute | solution.py:799
  331.9 13.3 %collective-permute-start.36 = (bf16[2,80,128]{2,1,0:T(8,128)(2,1)}, bf16[2,80,128]{2,1,0:T(8,128)(2,1)S(1)}, u32[]{:S(2)}, u32[]{:S(2)}) collective-permute-start(bf16[2,80,128]{2,1,0:T(8,128)(2,1)} %get-tuple-element.140), channel_id=1, source_target_pairs={{2,0},{4,2},{6,4},{8,6},{10,8},{12,10},{14,12},{16,14},{18,16},{20... | collective-permute-start | bytes 122888 | tf_op jit(solution)/shard_map/ppermute | solution.py:799
  337.1 41.2 %collective-permute-start.24 = (f32[832,256]{1,0:T(8,128)S(1)}, f32[832,256]{1,0:T(8,128)S(1)}, u32[]{:S(2)}, u32[]{:S(2)}) collective-permute-start(f32[832,256]{1,0:T(8,128)S(1)} %constant_dynamic-slice_fusion.7), channel_id=1, source_target_pairs={{0,2},{2,0},{4,6},{6,4},{8,10},{10,8},{12,14},{14,12},{16,18},{18,... | collective-permute-start | bytes 2555912 | tf_op jit(solution)/shard_map/ppermute | solution.py:686
  340.7 24.2 %all-to-all-start.9 = ((bf16[16,13,16,128]{3,2,1,0:T(8,128)(2,1)}), bf16[16,13,16,128]{3,2,1,0:T(8,128)(2,1)}, u32[]{:S(2)}, u32[]{:S(2)}) async-start(bf16[16,13,16,128]{3,2,1,0:T(8,128)(2,1)} %legendre.11.dep_ref), calls=%async_computation.9 | async-start | bytes 1703936 | tf_op jit(solution)/shard_map/all_to_all | solution.py:748
  368.1 32.0 %all-to-all-start.11 = ((bf16[16,11,16,128]{3,2,1,0:T(8,128)(2,1)}), bf16[16,11,16,128]{3,2,1,0:T(8,128)(2,1)}, u32[]{:S(2)}, u32[]{:S(2)}) async-start(bf16[16,11,16,128]{3,2,1,0:T(8,128)(2,1)} %zonal.11.refs_16_), calls=%async_computation.11 | async-start | bytes 1441792 | tf_op jit(solution)/shard_map/all_to_all | solution.py:748
  374.2 15.3 %collective-permute-start.45 = (bf16[2,16,64,128]{3,2,1,0:T(8,128)(2,1)}, bf16[2,16,64,128]{3,2,1,0:T(8,128)(2,1)}, u32[]{:S(2)}, u32[]{:S(2)}) collective-permute-start(bf16[2,16,64,128]{3,2,1,0:T(8,128)(2,1)} %get-tuple-element.155), channel_id=1, source_target_pairs={{0,1},{1,0},{2,3},{3,2},{4,5},{5,4},{6,7},{7,6},{8,9},{9,8},{10,11... | collective-permute-start | bytes 1572872 | tf_op jit(solution)/shard_map/ppermute | solution.py:778
  375.2 14.3 %collective-permute-start.44 = (f32[2,16,128]{2,1,0:T(8,128)S(1)}, f32[2,16,128]{2,1,0:T(8,128)S(1)}, u32[]{:S(2)}, u32[]{:S(2)}) collective-permute-start(f32[2,16,128]{2,1,0:T(8,128)S(1)} %get-tuple-element.224), channel_id=1, source_target_pairs={{0,1},{1,0},{2,3},{3,2},{4,5},{5,4},{6,7},{7,6},{8,9},{9,8},{10,11... | collective-permute-start | bytes 49160 | tf_op jit(solution)/shard_map/ppermute | solution.py:805
  376.3 28.1 %collective-permute-start.47 = (f32[2,16,128]{2,1,0:T(8,128)S(1)}, f32[2,16,128]{2,1,0:T(8,128)S(1)}, u32[]{:S(2)}, u32[]{:S(2)}) collective-permute-start(f32[2,16,128]{2,1,0:T(8,128)S(1)} %get-tuple-element.222), channel_id=1, source_target_pairs={{0,1},{1,0},{2,3},{3,2},{4,5},{5,4},{6,7},{7,6},{8,9},{9,8},{10,11... | collective-permute-start | bytes 49160 | tf_op jit(solution)/shard_map/ppermute | solution.py:805
  377.3 37.7 %collective-permute-start.37 = (f32[2,16,128]{2,1,0:T(8,128)S(1)}, f32[2,16,128]{2,1,0:T(8,128)S(1)}, u32[]{:S(2)}, u32[]{:S(2)}) collective-permute-start(f32[2,16,128]{2,1,0:T(8,128)S(1)} %get-tuple-element.225), channel_id=1, source_target_pairs={{0,1},{1,0},{2,3},{3,2},{4,5},{5,4},{6,7},{7,6},{8,9},{9,8},{10,11... | collective-permute-start | bytes 49160 | tf_op jit(solution)/shard_map/ppermute | solution.py:805
  378.5 50.8 %collective-permute-start.25 = (f32[416,256]{1,0:T(8,128)S(1)}, f32[416,256]{1,0:T(8,128)S(1)}, u32[]{:S(2)}, u32[]{:S(2)}) collective-permute-start(f32[416,256]{1,0:T(8,128)S(1)} %constant_dynamic-slice_fusion.6), channel_id=1, source_target_pairs={{0,4},{2,6},{4,0},{6,2},{8,12},{10,14},{12,8},{14,10},{16,20},{18,... | collective-permute-start | bytes 1277960 | tf_op jit(solution)/shard_map/ppermute | solution.py:686
  403.4 13.5 %collective-permute-start.46 = (bf16[2,16,64,128]{3,2,1,0:T(8,128)(2,1)}, bf16[2,16,64,128]{3,2,1,0:T(8,128)(2,1)S(1)}, u32[]{:S(2)}, u32[]{:S(2)}) collective-permute-start(bf16[2,16,64,128]{3,2,1,0:T(8,128)(2,1)} %get-tuple-element.156), channel_id=1, source_target_pairs={{0,1},{1,0},{2,3},{3,2},{4,5},{5,4},{6,7},{7,6},{8,9},{9,8},{10,11... | collective-permute-start | bytes 1572872 | tf_op jit(solution)/shard_map/ppermute | solution.py:778
  429.2 10.2 %collective-permute-start.48 = (f32[832,256]{1,0:T(8,128)S(1)}, f32[832,256]{1,0:T(8,128)S(1)}, u32[]{:S(2)}, u32[]{:S(2)}) collective-permute-start(f32[832,256]{1,0:T(8,128)S(1)} %constant_dynamic-slice_fusion.3), channel_id=1, source_target_pairs={{0,2},{2,0},{4,6},{6,4},{8,10},{10,8},{12,14},{14,12},{16,18},{18,... | collective-permute-start | bytes 2555912 | tf_op jit(solution)/shard_map/ppermute | solution.py:686
  429.4 7.7 %collective-permute-start.26 = (f32[208,256]{1,0:T(8,128)S(1)}, f32[208,256]{1,0:T(8,128)S(1)}, u32[]{:S(2)}, u32[]{:S(2)}) collective-permute-start(f32[208,256]{1,0:T(8,128)S(1)} %constant_dynamic-slice_fusion.5), channel_id=1, source_target_pairs={{0,1},{1,0},{2,3},{3,2},{4,5},{5,4},{6,7},{7,6},{8,9},{9,8},{10,11... | collective-permute-start | bytes 638984 | tf_op jit(solution)/shard_map/ppermute | solution.py:686
  437.1 7.8 %collective-permute-start.27 = (f32[104,256]{1,0:T(8,128)S(1)}, f32[104,256]{1,0:T(8,128)S(1)}, u32[]{:S(2)}, u32[]{:S(2)}) collective-permute-start(f32[104,256]{1,0:T(8,128)S(1)} %constant_dynamic-slice_fusion.4), channel_id=1, source_target_pairs={{0,16},{2,18},{4,20},{6,22},{8,24},{10,26},{12,28},{14,30},{16,0},... | collective-permute-start | bytes 319496 | tf_op jit(solution)/shard_map/ppermute | solution.py:686
  440.7 11.2 %collective-permute-start.49 = (f32[416,256]{1,0:T(8,128)S(1)}, f32[416,256]{1,0:T(8,128)S(1)}, u32[]{:S(2)}, u32[]{:S(2)}) collective-permute-start(f32[416,256]{1,0:T(8,128)S(1)} %constant_dynamic-slice_fusion.2), channel_id=1, source_target_pairs={{0,4},{2,6},{4,0},{6,2},{8,12},{10,14},{12,8},{14,10},{16,20},{18,... | collective-permute-start | bytes 1277960 | tf_op jit(solution)/shard_map/ppermute | solution.py:686
  449.8 7.0 %collective-permute-start.29 = (f32[104,256]{1,0:T(8,128)S(1)}, f32[104,256]{1,0:T(8,128)S(1)}, u32[]{:S(2)}, u32[]{:S(2)}) collective-permute-start(f32[104,256]{1,0:T(8,128)S(1)} %add.139), channel_id=1, source_target_pairs={{0,16},{2,18},{4,20},{6,22},{8,24},{10,26},{12,28},{14,30},{16,0},... | collective-permute-start | bytes 319496 | tf_op jit(solution)/shard_map/ppermute | solution.py:690
  452.0 6.4 %collective-permute-start.50 = (f32[208,256]{1,0:T(8,128)S(1)}, f32[208,256]{1,0:T(8,128)S(1)}, u32[]{:S(2)}, u32[]{:S(2)}) collective-permute-start(f32[208,256]{1,0:T(8,128)S(1)} %constant_dynamic-slice_fusion.1), channel_id=1, source_target_pairs={{0,1},{1,0},{2,3},{3,2},{4,5},{5,4},{6,7},{7,6},{8,9},{9,8},{10,11... | collective-permute-start | bytes 638984 | tf_op jit(solution)/shard_map/ppermute | solution.py:686
  458.4 6.9 %collective-permute-start.51 = (f32[104,256]{1,0:T(8,128)S(1)}, f32[104,256]{1,0:T(8,128)S(1)}, u32[]{:S(2)}, u32[]{:S(2)}) collective-permute-start(f32[104,256]{1,0:T(8,128)S(1)} %constant_dynamic-slice_fusion), channel_id=1, source_target_pairs={{0,16},{2,18},{4,20},{6,22},{8,24},{10,26},{12,28},{14,30},{16,0},... | collective-permute-start | bytes 319496 | tf_op jit(solution)/shard_map/ppermute | solution.py:686
  458.9 6.8 %collective-permute-start.30 = (f32[208,256]{1,0:T(8,128)S(1)}, f32[208,256]{1,0:T(8,128)S(1)}, u32[]{:S(2)}, u32[]{:S(2)}) collective-permute-start(f32[208,256]{1,0:T(8,128)S(1)} %pad_maximum_fusion.6), channel_id=1, source_target_pairs={{0,1},{1,0},{2,3},{3,2},{4,5},{5,4},{6,7},{7,6},{8,9},{9,8},{10,11... | collective-permute-start | bytes 638984 | tf_op jit(solution)/shard_map/ppermute | solution.py:690
  465.3 5.9 %collective-permute-start.52 = (f32[104,256]{1,0:T(8,128)S(1)}, f32[104,256]{1,0:T(8,128)S(1)}, u32[]{:S(2)}, u32[]{:S(2)}) collective-permute-start(f32[104,256]{1,0:T(8,128)S(1)} %dynamic-slice_add_fusion.6), channel_id=1, source_target_pairs={{0,8},{2,10},{4,12},{6,14},{8,0},{10,2},{12,4},{14,6},{16,24},{18,... | collective-permute-start | bytes 319496 | tf_op jit(solution)/shard_map/ppermute | solution.py:688
  471.2 5.8 %collective-permute-start.53 = (f32[104,256]{1,0:T(8,128)S(1)}, f32[104,256]{1,0:T(8,128)S(1)}, u32[]{:S(2)}, u32[]{:S(2)}) collective-permute-start(f32[104,256]{1,0:T(8,128)S(1)} %add.152), channel_id=1, source_target_pairs={{0,16},{2,18},{4,20},{6,22},{8,24},{10,26},{12,28},{14,30},{16,0},... | collective-permute-start | bytes 319496 | tf_op jit(solution)/shard_map/ppermute | solution.py:690
  471.4 8.9 %collective-permute-start.31 = (f32[416,256]{1,0:T(8,128)S(1)}, f32[416,256]{1,0:T(8,128)S(1)}, u32[]{:S(2)}, u32[]{:S(2)}) collective-permute-start(f32[416,256]{1,0:T(8,128)S(1)} %pad_maximum_fusion.4), channel_id=1, source_target_pairs={{0,4},{2,6},{4,0},{6,2},{8,12},{10,14},{12,8},{14,10},{16,20},{18,... | collective-permute-start | bytes 1277960 | tf_op jit(solution)/shard_map/ppermute | solution.py:690
  477.1 5.9 %collective-permute-start.54 = (f32[208,256]{1,0:T(8,128)S(1)}, f32[208,256]{1,0:T(8,128)S(1)}, u32[]{:S(2)}, u32[]{:S(2)}) collective-permute-start(f32[208,256]{1,0:T(8,128)S(1)} %pad_maximum_fusion.7), channel_id=1, source_target_pairs={{0,1},{1,0},{2,3},{3,2},{4,5},{5,4},{6,7},{7,6},{8,9},{9,8},{10,11... | collective-permute-start | bytes 638984 | tf_op jit(solution)/shard_map/ppermute | solution.py:690
  480.4 13.6 %collective-permute-start.32 = (f32[832,256]{1,0:T(8,128)S(1)}, f32[832,256]{1,0:T(8,128)S(1)}, u32[]{:S(2)}, u32[]{:S(2)}) collective-permute-start(f32[832,256]{1,0:T(8,128)S(1)} %pad_maximum_fusion.2), channel_id=1, source_target_pairs={{0,2},{2,0},{4,6},{6,4},{8,10},{10,8},{12,14},{14,12},{16,18},{18,... | collective-permute-start | bytes 2555912 | tf_op jit(solution)/shard_map/ppermute | solution.py:690
  483.8 9.9 %collective-permute-start.55 = (f32[416,256]{1,0:T(8,128)}, f32[416,256]{1,0:T(8,128)S(1)}, u32[]{:S(2)}, u32[]{:S(2)}) collective-permute-start(f32[416,256]{1,0:T(8,128)} %pad_maximum_fusion.5), channel_id=1, source_target_pairs={{0,4},{2,6},{4,0},{6,2},{8,12},{10,14},{12,8},{14,10},{16,20},{18,... | collective-permute-start | bytes 1277960 | tf_op jit(solution)/shard_map/ppermute | solution.py:690
  (77 other events, 495.0 us)
